TPU v7x, 128 devices: a whole 4x4x4 slice. The times are simulated.
128 devices in a mesh: dom: 32 (over x, z, core), feat: 4 (over y).
Axes of the slice: x: 4, y: 4, z: 4, core: 2. Of those that a mesh axis runs over, the one named last changes fastest.
Arguments:
- embeddings: bfloat16 [131072, 512], P('dom', 'feat'), may hold values from -6 to 6
- self_weight: bfloat16 [512, 512], P(None, 'feat'), may hold values from -0.25 to 0.25
- bases: bfloat16 [64, 512, 512], P(None, None, 'feat'), may hold values from -0.25 to 0.25
- basis_coef: bfloat16 [822, 64], replicated, may hold values from -0.75 to 0.75
- out_gain: float32 [512], P('feat'), may hold values from 0.1 to 1.9
- edge_src: int32 [16384, 128], P('dom'), may hold values from 0 to 4095, as said below
- edge_dst: int32 [16384, 128], P('dom'), may hold values from 0 to 8192, as said below
- block_rel: int32 [16384], P('dom'), may hold values from 0 to 821
- mirror_master_rows: int32 [131072], P('dom'), may hold values from 128 to 3071
- block_count: int32 [32], P('dom'), may hold values from 128 to 512, as said below
Outputs:
- updated: bfloat16 [131072, 512], P('dom', 'feat')
Inputs may be any that keep to these rules, and one draw needn't show every extreme that they name: `edge_src`: all rows of a block name sources in one aligned run of 128 rows of the slab. `edge_dst`: every block has at least one padding row and at least 64 used rows, row 0 among them; the used rows of a block name slots of one aligned run of 128 slots. `block_count`: some index of dom has all 512 blocks live. `mirror_master_rows`: hub entities are the first 128 rows of each slab; the last 1024 rows of a slab are never destinations.
All inputs are finite; a program needn't handle non-finite values.
Results may differ from a plain program's by a relative error of at most 0.007.
Values may be sent and summed in bfloat16 or wider, within the bound.
No kernel may reach another device: no remote copies, remote signals or barrier semaphores. Data moves between devices by JAX's collectives and lax.ppermute only.
A program may use at most 128 MiB of HBM per device.

v0:
```python
import jax
import jax.numpy as jnp
from jax import lax
from jax.sharding import PartitionSpec as P

TILE = 128
HUB_MIRRORS = 128
CAP = 128


def on_device(
    embeddings,
    self_weight,
    bases,
    basis_coef,
    out_gain,
    edge_src,
    edge_dst,
    block_rel,
    mirror_master_rows,
    block_count,
):
    dom_size = lax.axis_size("dom")
    blocks = edge_src.shape[0]
    n_local, part_cols = embeddings.shape
    gathered = lax.all_gather(embeddings, "feat", axis=1, tiled=True)
    model_dim = gathered.shape[1]
    n_bases = bases.shape[0]
    relations = basis_coef.shape[0]
    flat_bases = bases.reshape(n_bases, model_dim * part_cols)
    hub_count = HUB_MIRRORS * dom_size
    slot_tally_count = hub_count + CAP * dom_size
    per_group = min(32, blocks)
    live_blocks = block_count[0]
    src_tiles = n_local // TILE
    dst_tiles = slot_tally_count // TILE
    tile_table = gathered.reshape(src_tiles, TILE * model_dim)
    tile_range = jnp.arange(TILE, dtype=jnp.int32)

    def add_group(index, carry):
        partial_value, counts = carry
        row_offset = index * per_group
        sources = lax.dynamic_slice_in_dim(edge_src, row_offset, per_group, 0)
        targets = lax.dynamic_slice_in_dim(edge_dst, row_offset, per_group, 0)
        relation = lax.dynamic_slice_in_dim(block_rel, row_offset, per_group, 0)
        one_hot = (relation[:, None] == jnp.arange(relations)[None, :]).astype(jnp.bfloat16)
        mixing = jnp.dot(one_hot, basis_coef, preferred_element_type=jnp.float32).astype(
            jnp.bfloat16
        )
        combined = jnp.dot(mixing, flat_bases, preferred_element_type=jnp.float32).astype(
            jnp.bfloat16
        )
        combined = combined.reshape(per_group, model_dim, part_cols)
        src_tile = sources[:, 0] // TILE
        src_select = (src_tile[:, None] == jnp.arange(src_tiles)[None, :]).astype(jnp.bfloat16)
        tile_rows = jnp.dot(src_select, tile_table, preferred_element_type=jnp.float32).astype(
            jnp.bfloat16
        )
        tile_rows = tile_rows.reshape(per_group, TILE, model_dim)
        projected = jnp.einsum(
            "gtd,gdk->gtk", tile_rows, combined, preferred_element_type=jnp.float32
        )
        src_local = sources - src_tile[:, None] * TILE
        src_hot = (src_local[:, :, None] == tile_range[None, None, :]).astype(jnp.bfloat16)
        active = row_offset + jnp.arange(per_group) < live_blocks
        dst_tile = targets[:, 0] // TILE
        dst_local = targets - dst_tile[:, None] * TILE
        dst_hot = (
            (dst_local[:, :, None] == tile_range[None, None, :]) & active[:, None, None]
        ).astype(jnp.bfloat16)
        adjacency = jnp.einsum("gjs,gjt->gst", dst_hot, src_hot, preferred_element_type=jnp.float32)
        block_sums = jnp.einsum(
            "gst,gtk->gsk", adjacency, projected, precision=lax.Precision.HIGHEST
        )
        block_degree = jnp.sum(adjacency, axis=2)
        dst_select = (jnp.arange(dst_tiles)[:, None] == dst_tile[None, :]).astype(jnp.float32)
        partial_value = partial_value + jnp.einsum(
            "tg,gsk->tsk", dst_select, block_sums, precision=lax.Precision.HIGHEST
        )
        counts = counts + jnp.dot(dst_select, block_degree, precision=lax.Precision.HIGHEST)
        return (partial_value, counts)

    partial_start = jnp.zeros((dst_tiles, TILE, part_cols), jnp.float32)
    initial_counts = jnp.zeros((dst_tiles, TILE), jnp.float32)
    n_turns = blocks // per_group
    partial_value, counts = lax.fori_loop(0, n_turns, add_group, (partial_start, initial_counts))
    partial_value = partial_value.reshape(slot_tally_count, part_cols)
    counts = counts.reshape(slot_tally_count)
    hub_part = partial_value[:hub_count]
    hub_deg = counts[:hub_count]
    mirror_part = partial_value[hub_count:slot_tally_count]
    mirror_deg = counts[hub_count:slot_tally_count]
    hub_sum, hub_cnt = (
        lax.psum_scatter(
            hub_part.astype(jnp.bfloat16), "dom", scatter_dimension=0, tiled=True
        ).astype(jnp.float32),
        lax.psum_scatter(
            hub_deg.astype(jnp.bfloat16), "dom", scatter_dimension=0, tiled=True
        ).astype(jnp.float32),
    )
    mirror_sums, mirror_cnt = (
        lax.all_to_all(
            mirror_part.astype(jnp.bfloat16), "dom", split_axis=0, concat_axis=0, tiled=True
        ).astype(mirror_part.dtype),
        lax.all_to_all(
            mirror_deg.astype(jnp.bfloat16), "dom", split_axis=0, concat_axis=0, tiled=True
        ).astype(mirror_deg.dtype),
    )
    totals = jnp.zeros((n_local, part_cols), jnp.float32).at[mirror_master_rows].add(mirror_sums)
    totals = totals.at[:HUB_MIRRORS].add(hub_sum)
    degree = jnp.zeros((n_local,), jnp.float32).at[mirror_master_rows].add(mirror_cnt)
    degree = degree.at[:HUB_MIRRORS].add(hub_cnt)
    scale = lax.rsqrt(jnp.maximum(degree, 1.0))
    mixed = (
        jnp.dot(gathered, self_weight, preferred_element_type=jnp.float32) + totals * scale[:, None]
    )
    squares = lax.psum(jnp.sum(mixed * mixed, axis=1), "feat")
    norm = lax.rsqrt(squares / model_dim + 1e-05)
    return (mixed * norm[:, None] * out_gain).astype(jnp.bfloat16)


def solution(mesh):
    in_specs = (
        P("dom", "feat"),
        P(None, "feat"),
        P(None, None, "feat"),
        P(),
        P("feat"),
        P("dom", None),
        P("dom", None),
        P("dom"),
        P("dom"),
        P("dom"),
    )
    out_specs = P("dom", "feat")
    return jax.shard_map(
        on_device, mesh=mesh, in_specs=in_specs, out_specs=out_specs, check_vma=False
    )
```

profile of v0, /device:TPU:0, one launch (start us, length us, event | category | flops | bytes accessed | tf_op | source)
XLA Modules:
  0.0 846.7 jit_solution(15061902145734762572)
XLA Ops:
  7.3 12.0 %copy.95 = bf16[8,8,512,128]{3,1,2,0:T(8,128)(2,1)} copy(bf16[8,8,512,128]{3,2,1,0:T(8,128)(2,1)} %bitcast.63) | data formatting | bytes 16777216
  19.3 44.2 %all-gather.2.cloned.1.call-done = bf16[4096,512]{1,0:T(8,128)(2,1)} async-done(((bf16[4096,128]{1,0:T(8,128)(2,1)}), bf16[4096,512]{1,0:T(8,128)(2,1)}) %all-gather.2.cloned.1.call-update) | async-done | bytes 4194320 | tf_op jit(solution)/shard_map/all_gather | solution.py:26
  63.5 5.7 reshape.146
  69.2 600.5 %while.22 = (s32[]{:T(128)}, f32[64,128,128]{2,0,1:T(8,128)}, f32[64,128]{1,0:T(8,128)S(1)}, s32[512,128]{1,0:T(8,128)}, s32[]{:T(128)}, /*index=5*/s32[512,128]...) while((s32[]{:T(128)}, f32[64,128,128]{2,0,1:T(8,128)}, ...), condition=%wide.region_2.3_spmd.clone.clone, body=%wide.region_0.2_spmd.clone.clone.sunk | while | flops 2296658176 | bytes 92578896 | solution.py:86
  83.6 6.8 fusion.72
  99.0 5.3 select_add_fusion.2
  107.8 3.5 fusion.71
  119.1 6.8 fusion.72
  134.5 7.5 select_add_fusion.2
  156.7 6.8 fusion.72
  172.1 7.5 select_add_fusion.2
  183.1 3.5 fusion.71
  194.4 6.8 fusion.72
  209.8 7.5 select_add_fusion.2
  220.8 3.5 fusion.71
  232.0 6.8 fusion.72
  247.4 7.5 select_add_fusion.2
  269.7 6.8 fusion.72
  285.1 7.5 select_add_fusion.2
  296.1 3.5 fusion.71
  307.3 6.8 fusion.72
  322.7 7.5 select_add_fusion.2
  345.0 6.8 fusion.72
  360.4 7.5 select_add_fusion.2
  382.6 6.8 fusion.72
  398.0 7.5 select_add_fusion.2
  420.3 6.8 fusion.72
  435.7 7.5 select_add_fusion.2
  457.9 6.8 fusion.72
  473.3 7.5 select_add_fusion.2
  495.6 6.8 fusion.72
  511.0 7.5 select_add_fusion.2
  533.2 6.8 fusion.72
  548.7 7.5 select_add_fusion.2
  570.9 6.8 fusion.72
  586.3 7.5 select_add_fusion.2
  608.6 6.8 fusion.72
  624.0 7.5 select_add_fusion.2
  646.2 6.8 fusion.72
  661.6 7.5 select_add_fusion.2
  669.7 4.6 copy.94
  675.8 14.4 %all_to_all.12 = bf16[32,128,1]{1,2,0:T(2,128)(2,1)S(1)} all-to-all(bf16[32,128,1]{1,2,0:T(2,128)(2,1)S(1)} %copy.81), channel_id=1, replica_groups=mesh['dom'=32,'feat'=4] {'dom'}, dimensions={0} | all-to-all | bytes 16384 | tf_op jit(solution)/shard_map/all_to_all | solution.py:105
  690.2 3.9 all-to-all-start
  695.6 71.1 %all-reduce = bf16[4096]{0:T(1024)(128)(2,1)S(1)} all-reduce(bf16[4096]{0:T(1024)(128)(2,1)S(1)} %get-tuple-element.471), channel_id=3, replica_groups=mesh['dom'=32,'feat'=4] {'dom'}, use_global_device_ids=true, to_apply=%region_6.7.clone | all-reduce | flops 4096 | bytes 16384
  766.7 21.9 %scatter_custom_fusion.1 = f32[4096]{0:T(1024)S(1)} fusion(s32[4096]{0:T(1024)S(1)} %compare_select_fusion.3, f32[4096]{0:T(1024)S(1)} %bitcast.66, f32[]{:T(128)} %constant.179.clone.1), kind=kCustom, calls=%fused_computation.66 | custom fusion | flops 4096 | bytes 16388 | tf_op jit(solution)/shard_map/scatter-add | solution.py:111
  788.7 23.8 %scatter_custom_fusion = f32[4096,128]{1,0:T(8,128)} fusion(s32[4096]{0:T(1024)S(1)} %compare_select_fusion.3, bf16[4096,128]{1,0:T(8,128)(2,1)S(1)} %bitcast.64, f32[]{:T(128)} %constant.179.clone.1), kind=kCustom, calls=%fused_computation.54 | custom fusion | flops 1048576 | bytes 3145732 | tf_op jit(solution)/shard_map/scatter-add | solution.py:109
  815.4 5.0 multiply_reduce_fusion.1
  820.5 16.2 %psum.7 = f32[4096]{0:T(1024)S(1)} all-reduce(f32[4096]{0:T(1024)S(1)} %get-tuple-element.473), channel_id=1, replica_groups=mesh['dom'=32,'feat'=4] {'feat'}, use_global_device_ids=true, to_apply=%region_8.9 | all-reduce | flops 4096 | bytes 32768 | tf_op jit(solution)/shard_map/psum | solution.py:117
  (301 shorter events, 366.5 us)
Async XLA Ops:
  6.5 808.9 %copy-start = (bf16[512,128]{1,0:T(8,128)(2,1)S(1)}, bf16[512,128]{1,0:T(8,128)(2,1)}, u32[]{:S(2)}) copy-start(bf16[512,128]{1,0:T(8,128)(2,1)} %param.17) | copy-start | bytes 393220
  6.5 57.0 %all-gather.2.cloned.1.call-start = ((), (), s32[]{:S(2)}) async-start(), calls=%async_computation.3 | async-start | bytes 5242880 | tf_op jit(solution)/shard_map/all_gather | solution.py:26
  7.3 807.3 %reduce-scatter.4.cloned.1.call-start = ((), (), s32[]{:S(2)}) async-start(), calls=%async_computation.4 | async-start | bytes 1081344
  19.3 49.8 %copy-start.3 = (bf16[822,64]{0,1:T(8,128)(2,1)S(1)}, bf16[822,64]{0,1:T(8,128)(2,1)}, u32[]{:S(2)}) copy-start(bf16[822,64]{0,1:T(8,128)(2,1)} %param.19) | copy-start | bytes 315652
  90.4 3.4 copy-start.1
  93.9 1.6 copy-start.2
  125.9 3.4 copy-start.1
  129.3 1.6 copy-start.2
  163.6 3.4 copy-start.1
  167.0 1.6 copy-start.2
  201.2 3.4 copy-start.1
  204.7 1.6 copy-start.2
  238.9 3.4 copy-start.1
  242.3 1.6 copy-start.2
  276.5 3.4 copy-start.1
  280.0 1.6 copy-start.2
  314.2 3.4 copy-start.1
  317.6 1.6 copy-start.2
  351.8 3.4 copy-start.1
  355.3 1.6 copy-start.2
  389.5 3.4 copy-start.1
  392.9 1.6 copy-start.2
  427.1 3.4 copy-start.1
  430.6 1.6 copy-start.2
  464.8 3.4 copy-start.1
  468.2 1.6 copy-start.2
  502.4 3.4 copy-start.1
  505.9 1.6 copy-start.2
  540.1 3.4 copy-start.1
  543.5 1.6 copy-start.2
  577.7 3.4 copy-start.1
  581.2 1.6 copy-start.2
  615.4 3.4 copy-start.1
  618.8 1.6 copy-start.2
  653.0 3.4 copy-start.1
  656.5 1.6 copy-start.2
  675.8 18.4 %copy-start.6 = (u32[128]{0:T(128)S(1)}, u32[128]{0:T(128)}, u32[]{:S(2)}) copy-start(u32[128]{0:T(128)} %constant.188) | copy-start | bytes 1540
  675.8 19.8 %copy-start.4 = (s32[4096]{0:T(1024)S(1)}, s32[4096]{0:T(1024)}, u32[]{:S(2)}) copy-start(s32[4096]{0:T(1024)} %param.24) | copy-start | bytes 49156
  690.2 98.5 %all-to-all-start = ((bf16[32,128,128]{2,1,0:T(8,128)(2,1)}), bf16[32,128,128]{2,1,0:T(8,128)(2,1)S(1)}, u32[]{:S(2)}, u32[]{:S(2)}) async-start(bf16[32,128,128]{2,1,0:T(8,128)(2,1)} %get-tuple-element.470), calls=%async_computation | async-start | bytes 2097152 | tf_op jit(solution)/shard_map/all_to_all | solution.py:102
  815.4 21.2 %copy-start.5 = (f32[128]{0:T(128)S(1)}, f32[128]{0:T(128)}, u32[]{:S(2)}) copy-start(f32[128]{0:T(128)} %param.20) | copy-start | bytes 1540
Sparse Core Ops, SparseCore 0:
  9.0 54.4 all-gather.1
  675.9 78.5 reduce-scatter.3
where the time goes:
time: 853 us; the launch traced here: 847 us
  matrix products  425 us (50%)
  local copies, waits for them, and re-layouts  157 us (18%)
  blocking collectives  102 us (12%)
  other arithmetic  98.4 us (12%)
  waiting for transfers between devices  44.9 us (5%)
  between operations  14.3 us (2%)
    dot_general x16, matrix products, add_group(): jnp.einsum('tg,gsk->tsk', dst_select, block_sums, precision=lax.Precision...  118 us
    while x96, local copies, waits for them, and re-layouts  116 us
    dot_general x16, matrix products, add_group(): jnp.dot(mixing, flat_bases, preferred_element_type=jnp.float32)  109 us
    unnamed x1, blocking collectives  71.1 us
    dot_general x16, matrix products, add_group(): jnp.einsum('gjs,gjt->gst', dst_hot, src_hot, preferred_element_type=jnp.f...  56.6 us
    dot_general x16, matrix products, add_group(): jnp.einsum('gst,gtk->gsk', adjacency, projected, precision=lax.Precision....  56.1 us
    dot_general x16, matrix products, add_group(): jnp.dot(src_select, tile_table, preferred_element_type=jnp.float32)  55.6 us
    all_gather x1, waiting for transfers between devices, on_device(): gathered = lax.all_gather(embeddings, 'feat', axis=1, tiled=True)  44.2 us
  transfers between devices with their start and end apart: 3, of which 1 were waited for; matrix products, arithmetic and copies ran while one was open for 7% of the time, Pallas kernels for 0%

commit v1 on v0

v1 whole, which is shorter than its diff:
```python
import functools

import jax
import jax.numpy as jnp
from jax import lax
from jax.experimental import pallas as pl
from jax.experimental.pallas import tpu as pltpu
from jax.sharding import PartitionSpec as P

TILE = 128
HUB_MIRRORS = 128
CAP = 128
DEG_ROWS = 16
VMEM_LIMIT = 56 * 1024 * 1024
BF = jnp.bfloat16
F32 = jnp.float32


def mix_kernel(feat_ref, lhs_ref, bases_ref, w_ref, spread, *, chunk):
    n_bases, depth, cols = bases_ref.shape
    spread[...] = bases_ref[...].astype(F32).reshape(n_bases * depth, cols)

    def rows_of(d):
        return spread[pl.ds(d, n_bases, stride=depth), :].astype(BF)

    rights = []
    for octet in range(depth // 8):
        halves = []
        for half in range(2):
            first = octet * 8 + half * 4
            halves.append(jnp.concatenate([rows_of(first + i) for i in range(4)], axis=0))
        rights.append(jnp.concatenate(halves, axis=1))
    pairs = chunk // 8
    low = lax.broadcasted_iota(jnp.int32, (pairs, 8, cols), 1) < 4

    def body(step, carry):
        row = pl.multiple_of(step * chunk, chunk)
        left = lhs_ref[pl.ds(row, chunk), :]
        evens, odds = [], []
        for right in rights:
            out = jnp.dot(left, right, preferred_element_type=F32)
            first = out[:, :cols].reshape(pairs, 8, cols)
            second = out[:, cols:].reshape(pairs, 8, cols)
            evens.append(jnp.where(low, first, pltpu.roll(second, 4, 1)))
            odds.append(jnp.where(low, pltpu.roll(first, 4, 1), second))
        pair = step * pairs
        w_ref[pl.ds(pair, pairs), 0] = jnp.concatenate(evens, axis=1).astype(BF)
        w_ref[pl.ds(pair, pairs), 1] = jnp.concatenate(odds, axis=1).astype(BF)
        return carry

    lax.fori_loop(0, lhs_ref.shape[0] // chunk, body, 0)


def mix(feat, lhs, bases, blocks):
    n_bases, model_dim, cols = bases.shape
    depth = 16
    steps = model_dim // depth
    per_part = cols // depth
    return pl.pallas_call(
        functools.partial(mix_kernel, chunk=256),
        out_shape=jax.ShapeDtypeStruct((blocks // 2, 2, model_dim, cols), BF),
        grid_spec=pltpu.PrefetchScalarGridSpec(
            num_scalar_prefetch=1,
            grid=(steps,),
            in_specs=[
                pl.BlockSpec(lhs.shape, lambda i, f: (0, 0)),
                pl.BlockSpec(
                    (n_bases, depth, cols),
                    lambda i, f: (0, lax.rem(i + f[0] * per_part, steps), 0),
                ),
            ],
            out_specs=pl.BlockSpec((blocks // 2, 2, depth, cols), lambda i, f: (0, 0, i, 0)),
            scratch_shapes=[pltpu.VMEM((n_bases * depth, cols), F32)],
        ),
        compiler_params=pltpu.CompilerParams(vmem_limit_bytes=VMEM_LIMIT),
        name="mix",
    )(feat, lhs, bases)


def adjacency_kernel(
    src_tile_ref, dst_tile_ref, live_ref, src_ref, dst_ref, adj_ref, deg_ref, *, group
):
    step = pl.program_id(0)

    @pl.when(step == 0)
    def _():
        deg_ref[...] = jnp.zeros_like(deg_ref)

    slot = lax.broadcasted_iota(jnp.int32, (TILE, TILE), 0)
    total = deg_ref[...]
    for i in range(group):
        block = step * group + i
        dst_tile = dst_tile_ref[block]
        base = jnp.where(block < live_ref[0], dst_tile * TILE, 1 << 20)
        dst = dst_ref[i : i + 1, :] - base
        src = src_ref[i : i + 1, :] - src_tile_ref[block] * TILE
        dst_hot = jnp.where(slot == dst, 1.0, 0.0).astype(BF)
        src_hot = jnp.where(slot == src, 1.0, 0.0).astype(BF)
        mark = jnp.where(slot == dst_tile, 1.0, 0.0).astype(BF)
        right = jnp.concatenate([src_hot, mark], axis=0)
        out = lax.dot_general(
            dst_hot, right, (((1,), (1,)), ((), ())), preferred_element_type=F32
        )
        adj_ref[i] = out[:, :TILE].astype(BF)
        total = total + out[:, TILE:]
    deg_ref[...] = total


def adjacency(src_tile, dst_tile, live, edge_src, edge_dst):
    blocks = edge_src.shape[0]
    group = 8
    return pl.pallas_call(
        functools.partial(adjacency_kernel, group=group),
        out_shape=(
            jax.ShapeDtypeStruct((blocks, TILE, TILE), BF),
            jax.ShapeDtypeStruct((TILE, TILE), F32),
        ),
        grid_spec=pltpu.PrefetchScalarGridSpec(
            num_scalar_prefetch=3,
            grid=(blocks // group,),
            in_specs=[
                pl.BlockSpec((group, TILE), lambda i, *_: (i, 0)),
                pl.BlockSpec((group, TILE), lambda i, *_: (i, 0)),
            ],
            out_specs=(
                pl.BlockSpec((group, TILE, TILE), lambda i, *_: (i, 0, 0)),
                pl.BlockSpec((TILE, TILE), lambda i, *_: (0, 0)),
            ),
        ),
        compiler_params=pltpu.CompilerParams(vmem_limit_bytes=VMEM_LIMIT),
        name="adjacency",
    )(src_tile, dst_tile, live, edge_src, edge_dst)


def blocks_kernel(
    src_tile_ref,
    dst_tile_ref,
    live_ref,
    w_ref,
    adj_ref,
    deg_ref,
    x0_ref,
    x1_ref,
    x2_ref,
    x3_ref,
    out_ref,
    acc,
    *,
    group,
):
    step = pl.program_id(0)

    @pl.when(step == 0)
    def _():
        acc[...] = jnp.zeros_like(acc)

    @pl.when(step * group < live_ref[0])
    def _():
        for i in range(group):
            block = step * group + i
            row = pl.multiple_of(src_tile_ref[block] * TILE, TILE)
            rows = pl.ds(row, TILE)
            tile = jnp.concatenate(
                [x0_ref[rows, :], x1_ref[rows, :], x2_ref[rows, :], x3_ref[rows, :]], axis=1
            )
            message = jnp.dot(tile, w_ref[i // 2, i % 2], preferred_element_type=F32).astype(BF)
            dst = dst_tile_ref[block]
            acc[dst] = acc[dst] + jnp.dot(adj_ref[i], message, preferred_element_type=F32)

    @pl.when(step == pl.num_programs(0) - 1)
    def _():
        owners = out_ref.shape[1]
        degree = deg_ref[...].T
        high = jnp.floor(degree * (1.0 / 256.0)) * 256.0
        low = degree - high
        line = lax.broadcasted_iota(jnp.int32, (owners, DEG_ROWS, TILE), 1)
        for part in range(2):
            here = slice(part * owners, (part + 1) * owners)
            out_ref[part, :, :TILE, :] = acc[here].astype(BF)
            rows = jnp.where(
                line == 0, high[here][:, None, :], jnp.where(line == 1, low[here][:, None, :], 0.0)
            )
            out_ref[part, :, TILE:, :] = rows.astype(BF)


def blocks_call(src_tile, dst_tile, live, weights, adj, deg, pieces, owners):
    pairs, _, model_dim, cols = weights.shape
    group = 8
    whole = lambda shape: pl.BlockSpec(shape, lambda i, *_: (0,) * len(shape))
    out = (2, owners, TILE + DEG_ROWS, cols)
    return pl.pallas_call(
        functools.partial(blocks_kernel, group=group),
        out_shape=jax.ShapeDtypeStruct(out, BF),
        grid_spec=pltpu.PrefetchScalarGridSpec(
            num_scalar_prefetch=3,
            grid=(pairs * 2 // group,),
            in_specs=[
                pl.BlockSpec((group // 2, 2, model_dim, cols), lambda i, *_: (i, 0, 0, 0)),
                pl.BlockSpec((group, TILE, TILE), lambda i, *_: (i, 0, 0)),
                whole(deg.shape),
            ]
            + [whole(p.shape) for p in pieces],
            out_specs=whole(out),
            scratch_shapes=[pltpu.VMEM((2 * owners, TILE, cols), F32)],
        ),
        compiler_params=pltpu.CompilerParams(vmem_limit_bytes=VMEM_LIMIT),
        name="blocks",
    )(src_tile, dst_tile, live, weights, adj, deg, *pieces)


def final_kernel(
    hub_ref,
    mirror_ref,
    master_ref,
    self_ref,
    x0_ref,
    x1_ref,
    x2_ref,
    x3_ref,
    mixed_ref,
    squares_ref,
    right,
    *,
    chunk,
):
    step = pl.program_id(0)
    owners = mirror_ref.shape[0]
    cols = mirror_ref.shape[2]
    slots = owners * TILE
    last_chunks = pl.num_programs(0)

    @pl.when(step == 0)
    def _():
        high = mirror_ref[:, TILE, :].astype(F32)
        low = mirror_ref[:, TILE + 1, :].astype(F32)
        pad = jnp.zeros((TILE - 2 * owners, TILE), F32)
        table = jnp.concatenate([high, low, pad], axis=0).T
        lane = lax.broadcasted_iota(jnp.int32, (TILE, TILE), 1)
        for p in range(owners):
            rows = slice(p * TILE, (p + 1) * TILE)
            right[rows, :cols] = mirror_ref[p, :TILE, :]
            keep = (lane == p) | (lane == p + owners)
            right[rows, cols:] = jnp.where(keep, table, 0.0).astype(BF)

    rows = pl.ds(pl.multiple_of(step * chunk, chunk), chunk)
    tile = jnp.concatenate(
        [x0_ref[rows, :], x1_ref[rows, :], x2_ref[rows, :], x3_ref[rows, :]], axis=1
    )
    own = jnp.dot(tile, self_ref[...], preferred_element_type=F32)
    entity = lax.broadcasted_iota(jnp.int32, (chunk, TILE), 0) + step * chunk
    hot = jnp.concatenate(
        [
            jnp.where(entity == master_ref[p : p + 1, :], 1.0, 0.0).astype(BF)
            for p in range(owners)
        ],
        axis=1,
    )
    sums = jnp.dot(hot, right[...], preferred_element_type=F32)
    degree = jnp.sum(sums[:, cols:], axis=1, keepdims=True)
    total = sums[:, :cols]
    scale = lax.rsqrt(jnp.maximum(degree, 1.0))
    mixed = own + total * scale
    mixed_ref[...] = mixed

    @pl.when(step == 0)
    def _():
        hub = jnp.sum(hub_ref[:, :TILE, :].astype(F32), axis=0)
        line = jnp.sum(
            hub_ref[:, TILE, :].astype(F32) + hub_ref[:, TILE + 1, :].astype(F32),
            axis=0,
            keepdims=True,
        )
        column = jnp.broadcast_to(line, (TILE, TILE)).T[:, :1]
        hub_scale = lax.rsqrt(jnp.maximum(column + degree[:TILE], 1.0))
        mixed_ref[:TILE, :] = own[:TILE] + (total[:TILE] + hub) * hub_scale

    value = mixed_ref[...]
    squares = jnp.sum(value * value, axis=1, keepdims=True)
    squares_ref[...] = jnp.broadcast_to(squares, (chunk, TILE)).T[:8, :]


def final(hub, mirror, master, self_weight, pieces):
    n_local, cols = pieces[0].shape
    owners = mirror.shape[0]
    chunk = 256
    whole = lambda shape: pl.BlockSpec(shape, lambda i: (0,) * len(shape))
    return pl.pallas_call(
        functools.partial(final_kernel, chunk=chunk),
        out_shape=(
            jax.ShapeDtypeStruct((n_local, cols), F32),
            jax.ShapeDtypeStruct((8, n_local), F32),
        ),
        grid=(n_local // chunk,),
        in_specs=[whole(hub.shape), whole(mirror.shape), whole(master.shape), whole(self_weight.shape)]
        + [whole(p.shape) for p in pieces],
        out_specs=(
            pl.BlockSpec((chunk, cols), lambda i: (i, 0)),
            pl.BlockSpec((8, chunk), lambda i: (0, i)),
        ),
        scratch_shapes=[pltpu.VMEM((owners * TILE, 2 * cols), BF)],
        compiler_params=pltpu.CompilerParams(vmem_limit_bytes=VMEM_LIMIT),
        name="final",
    )(hub, mirror, master, self_weight, *pieces)


def from_others(x, size):
    return [
        lax.ppermute(x, "feat", [((i + shift) % size, i) for i in range(size)])
        for shift in range(1, size)
    ]


def on_device(
    embeddings,
    self_weight,
    bases,
    basis_coef,
    out_gain,
    edge_src,
    edge_dst,
    block_rel,
    mirror_master_rows,
    block_count,
):
    owners = lax.axis_size("dom")
    feat_size = lax.axis_size("feat")
    feat = lax.axis_index("feat").astype(jnp.int32)
    blocks = edge_src.shape[0]
    n_local, cols = embeddings.shape
    n_bases, model_dim, _ = bases.shape
    relations = basis_coef.shape[0]

    pieces = [embeddings] + from_others(embeddings, feat_size)

    src_tile = edge_src[:, 0] // TILE
    dst_tile = edge_dst[:, 0] // TILE

    spread = 4
    relation = jnp.repeat(block_rel, spread)
    one_hot = (relation[:, None] == jnp.arange(relations)[None, :]).astype(BF)
    wide = jnp.concatenate([basis_coef] * spread, axis=1)
    lhs = jnp.dot(one_hot, wide, preferred_element_type=F32)
    line = lax.broadcasted_iota(jnp.int32, lhs.shape, 0) % spread
    group = lax.broadcasted_iota(jnp.int32, lhs.shape, 1) // n_bases
    lhs = jnp.where(line == group, lhs, 0.0).astype(BF)

    adj, deg = adjacency(src_tile, dst_tile, block_count, edge_src, edge_dst)
    weights = mix(feat.reshape(1), lhs, bases, blocks)
    partial = blocks_call(src_tile, dst_tile, block_count, weights, adj, deg, pieces, owners)

    hub = lax.all_to_all(partial[0], "dom", split_axis=0, concat_axis=0, tiled=True)
    mirror = lax.all_to_all(partial[1], "dom", split_axis=0, concat_axis=0, tiled=True)

    turned = jnp.roll(self_weight, -feat * cols, axis=0)
    mixed, squares = final(hub, mirror, mirror_master_rows.reshape(owners, TILE), turned, pieces)
    line = squares[0].reshape(n_local // TILE, TILE)
    everyone = line
    for other in from_others(line, feat_size):
        everyone = everyone + other
    norm = lax.rsqrt(everyone.reshape(n_local) / model_dim + 1e-05)
    return (mixed * norm[:, None] * out_gain).astype(BF)


def solution(mesh):
    in_specs = (
        P("dom", "feat"),
        P(None, "feat"),
        P(None, None, "feat"),
        P(),
        P("feat"),
        P("dom", None),
        P("dom", None),
        P("dom"),
        P("dom"),
        P("dom"),
    )
    out_specs = P("dom", "feat")
    return jax.shard_map(
        on_device, mesh=mesh, in_specs=in_specs, out_specs=out_specs, check_vma=False
    )
```

time: 853 us -> 311 us (0.36)
  matrix products: 425 us -> 3.84 us
  Pallas kernels: 0 us -> 202 us
  local copies, waits for them, and re-layouts: 157 us -> 7.63 us
  other arithmetic: 98.4 us -> 4.49 us
  blocking collectives: 102 us -> 56 us
  waiting for transfers between devices: 44.9 us -> 19.8 us
  between operations: 14.3 us -> 0.8 us
  starting transfers between devices: 3.97 us -> 13.6 us
    dot_general x113 -> x1, matrix products: 425 us -> 3.84 us  [on_device(): lhs = jnp.dot(one_hot, wide, preferred_element_type=F32)]
    pallas_call x0 -> x4, Pallas kernels: none -> 202 us  [the longest x1 71.9 us: blocks_call(): pl.pallas_call(functools.partial(blocks_kernel, group=group), out_shape=j...]
    while x97 -> x0, local copies, waits for them, and re-layouts: 121 us -> none
    unnamed x1 -> x0, blocking collectives: 71.1 us -> none
    scatter-add x4 -> x0, other arithmetic: 45.8 us -> none  [the longest x1 23.8 us: on_device(): jnp.zeros((n_local, part_cols), jnp.float32).at[mirror_master_rows]]
    all_gather x1 -> x0, waiting for transfers between devices: 44.2 us -> none  [on_device(): gathered = lax.all_gather(embeddings, 'feat', axis=1, tiled=True)]
    all_to_all x1, blocking collectives: 14.4 us -> 56 us  [on_device(): lax.all_to_all(partial[0], 'dom', split_axis=0, concat_axis=0, tiled=True)]
    all_to_all x1, waiting for transfers between devices: 0.01 us -> 17.2 us  [on_device(): lax.all_to_all(partial[1], 'dom', split_axis=0, concat_axis=0, tiled=True)]
  transfers between devices with their start and end apart: 3 -> 7, of which waited for: 1 -> 4; matrix products, arithmetic and copies ran while one was open for 7% -> 2% of each run, Pallas kernels for 0% -> 36%
where the time goes in v1:
time: 311 us; the launch traced here: 308 us
  Pallas kernels  202 us (65%)
  blocking collectives  56 us (18%)
  waiting for transfers between devices  19.8 us (6%)
  starting transfers between devices  13.6 us (4%)
  local copies, waits for them, and re-layouts  7.63 us (2%)
  other arithmetic  4.49 us (1%)
  matrix products  3.84 us (1%)
    pallas_call x1, Pallas kernels, blocks_call(): pl.pallas_call(functools.partial(blocks_kernel, group=group), out_shape=j...  71.9 us
    pallas_call x1, Pallas kernels, mix(): pl.pallas_call(functools.partial(mix_kernel, chunk=256), out_shape=jax.Sh...  70.9 us
    all_to_all x1, blocking collectives, on_device(): lax.all_to_all(partial[0], 'dom', split_axis=0, concat_axis=0, tiled=True)  56 us
    pallas_call x1, Pallas kernels, adjacency(): pl.pallas_call(functools.partial(adjacency_kernel, group=group), out_shap...  38.9 us
    pallas_call x1, Pallas kernels, final(): pl.pallas_call(functools.partial(final_kernel, chunk=chunk), out_shape=(j...  20.1 us
    all_to_all x1, waiting for transfers between devices, on_device(): lax.all_to_all(partial[1], 'dom', split_axis=0, concat_axis=0, tiled=True)  17.2 us
    ppermute x6, starting transfers between devices, from_others(): lax.ppermute(x, 'feat', [((i + shift) % size, i) for i in range(size)])  9.62 us
  transfers between devices with their start and end apart: 7, of which 4 were waited for; matrix products, arithmetic and copies ran while one was open for 2% of the time, Pallas kernels for 36%

profile of v1, /device:TPU:0, one launch (start us, length us, event | category | flops | bytes accessed | tf_op | source)
XLA Modules:
  0.0 307.9 jit_solution(4436946351631886664)
XLA Ops:
  0.0 3.1 %collective-permute-start = (bf16[4096,128]{1,0:T(8,128)(2,1)}, bf16[4096,128]{1,0:T(8,128)(2,1)S(1)}, u32[]{:S(2)}, u32[]{:S(2)}) collective-permute-start(bf16[4096,128]{1,0:T(8,128)(2,1)} %x0_ref.3), channel_id=1, source_target_pairs={{1,0},{2,1},{3,2},{0,3},{5,4},{6,5},{7,6},{4,7},{9,8},{10,9},{11,1... | collective-permute-start | bytes 3145736 | tf_op jit(solution)/shard_map/ppermute | solution.py:308
  3.1 0.6 collective-permute-start.1
  3.7 1.0 collective-permute-start.2
  5.4 0.8 broadcast_in_dim.10
  6.2 0.2 eq.24
  6.4 3.8 %fusion.3.lhs_ref = bf16[2048,256]{1,0:T(8,128)(2,1)} fusion(s32[2048]{0:T(1024)S(1)} %eq.24, s32[256]{0:T(256)S(1)} %get-tuple-element.17, s32[256]{0:T(256)S(1)} %get-tuple-element.18, s32[2048]{0:T(1024)S(1)} %get-tuple-element.15, s32[2048]{0:T(1024)S(1)} %get-tuple-element.16, pred[2048]{0:T(1024)(128)(4,1)S(1)} %fusion.15, ...), kind=kOutput, calls=%fused_computation.4 | convolution fusion | flops 867917824 | bytes 1182720 | tf_op jit(solution)/shard_map/dot_general | solution.py:342
  10.2 0.0 copy-start.4
  10.2 0.0 copy-start.5
  10.2 70.9 %mix.1.w_ref = bf16[256,2,512,128]{3,2,1,0:T(8,128)(2,1)} custom-call(s32[1]{0:T(128)} %bitcast.feat_ref, bf16[2048,256]{1,0:T(8,128)(2,1)} %fusion.3.lhs_ref, bf16[64,512,128]{2,1,0:T(8,128)(2,1)} %bases_ref.1), custom_call_target="tpu_custom_call" | custom-call | tf_op jit(solution)/shard_map/mix/pallas_call | solution.py:59
  81.1 0.0 copy-done.4
  81.1 0.1 slice_reduce_fusion
  81.2 0.0 copy-done.5
  81.3 0.1 slice_reduce_fusion.1
  81.4 0.6 add_select_fusion
  82.0 38.9 %adjacency.1 = (bf16[512,128,128]{2,1,0:T(8,128)(2,1)}, f32[128,128]{1,0:T(8,128)}) custom-call(s32[512]{0:T(512)} %get-tuple-element.20.src_tile_ref, s32[512]{0:T(512)} %get-tuple-element.19.dst_tile_ref, s32[1]{0:T(128)S(6)} %copy.11.live_ref, s32[512,128]{1,0:T(8,128)} %src_ref.1, s32[512,128]{1,0:T(8,128)} %dst_ref.1), custom_call_target="tpu_custom_call" | custom-call | tf_op jit(solution)/shard_map/adjacency/pallas_call | solution.py:112
  120.9 0.0 collective-permute-done.x1_ref
  120.9 0.0 copy-start.1
  120.9 0.0 collective-permute-done.1.x2_ref
  120.9 0.0 copy-start.2
  120.9 0.0 collective-permute-done.2.x3_ref
  120.9 0.0 copy-start.3
  120.9 0.9 copy-done.1
  121.8 0.3 copy-done.2
  122.2 0.4 copy-done.3
  122.5 71.9 %blocks.1 = bf16[2,32,144,128]{3,2,1,0:T(8,128)(2,1)} custom-call(s32[512]{0:T(512)} %get-tuple-element.20.src_tile_ref, s32[512]{0:T(512)} %get-tuple-element.19.dst_tile_ref, s32[1]{0:T(128)S(6)} %copy.11.live_ref, bf16[256,2,512,128]{3,2,1,0:T(8,128)(2,1)} %mix.1.w_ref, bf16[512,128,128]{2,1,0:T(8,128)(2,1)} %get-tuple-element.9.adj_ref, ...), custom_call_target="tpu_custom_call" | custom-call | tf_op jit(solution)/shard_map/blocks/pallas_call | solution.py:191
  194.4 2.8 slice_bitcast_fusion
  197.2 0.0 copy-start.6
  197.2 56.0 %all_to_all.10.hub_ref = bf16[32,144,128]{2,1,0:T(8,128)(2,1)} all-to-all(bf16[32,144,128]{2,1,0:T(8,128)(2,1)S(1)} %get-tuple-element.14), channel_id=1, replica_groups=mesh['dom'=32,'feat'=4] {'dom'}, dimensions={0} | all-to-all | bytes 2359296 | tf_op jit(solution)/shard_map/all_to_all | solution.py:351
  253.3 3.9 %all-to-all-start.1 = ((bf16[32,144,128]{2,1,0:T(8,128)(2,1)}), bf16[32,144,128]{2,1,0:T(8,128)(2,1)S(1)}, u32[]{:S(2)}, u32[]{:S(2)}) async-start(bf16[32,144,128]{2,1,0:T(8,128)(2,1)} %get-tuple-element.13), calls=%async_computation.1 | async-start | bytes 2359296 | tf_op jit(solution)/shard_map/all_to_all | solution.py:352
  257.2 0.0 copy-done.6
  257.3 1.1 fusion.11.self_ref
  258.4 17.2 %all-to-all-done.1.mirror_ref = bf16[32,144,128]{2,1,0:T(8,128)(2,1)S(1)} async-done(((bf16[32,144,128]{2,1,0:T(8,128)(2,1)}), bf16[32,144,128]{2,1,0:T(8,128)(2,1)S(1)}, u32[]{:S(2)}, u32[]{:S(2)}) %all-to-all-start.1) | async-done | bytes 1179680 | tf_op jit(solution)/shard_map/all_to_all | solution.py:352
  275.6 0.0 copy-start
  275.6 1.0 copy-done
  276.6 0.0 copy-start.7
  276.6 20.1 %final.1 = (f32[4096,128]{1,0:T(8,128)}, f32[8,4096]{1,0:T(8,128)}) custom-call(bf16[32,144,128]{2,1,0:T(8,128)(2,1)} %all_to_all.10.hub_ref, bf16[32,144,128]{2,1,0:T(8,128)(2,1)} %copy-done, s32[32,128]{1,0:T(8,128)} %bitcast.13, bf16[512,128]{1,0:T(8,128)(2,1)} %fusion.11.self_ref, bf16[4096,128]{1,0:T(8,128)(2,1)} %x0_ref.3, ...), custom_call_target="tpu_custom_call" | custom-call | tf_op jit(solution)/shard_map/final/pallas_call | solution.py:287
  296.7 0.9 slice.19
  297.6 1.9 collective-permute-start.5
  299.6 1.9 collective-permute-start.4
  301.4 1.1 collective-permute-start.3
  302.6 0.1 collective-permute-done.5
  302.7 2.2 collective-permute-done.4
  304.8 0.4 collective-permute-done.3
  305.2 0.0 copy-done.7
  305.2 2.7 multiply_convert_fusion
  (5 shorter events, 0.0 us)
Async XLA Ops:
  0.0 120.9 %collective-permute-start = (bf16[4096,128]{1,0:T(8,128)(2,1)}, bf16[4096,128]{1,0:T(8,128)(2,1)S(1)}, u32[]{:S(2)}, u32[]{:S(2)}) collective-permute-start(bf16[4096,128]{1,0:T(8,128)(2,1)} %x0_ref.3), channel_id=1, source_target_pairs={{1,0},{2,1},{3,2},{0,3},{5,4},{6,5},{7,6},{4,7},{9,8},{10,9},{11,1... | collective-permute-start | bytes 3145736 | tf_op jit(solution)/shard_map/ppermute | solution.py:308
  3.1 117.8 %collective-permute-start.1 = (bf16[4096,128]{1,0:T(8,128)(2,1)}, bf16[4096,128]{1,0:T(8,128)(2,1)S(1)}, u32[]{:S(2)}, u32[]{:S(2)}) collective-permute-start(bf16[4096,128]{1,0:T(8,128)(2,1)} %x0_ref.3), channel_id=1, source_target_pairs={{2,0},{3,1},{0,2},{1,3},{6,4},{7,5},{4,6},{5,7},{10,8},{11,9},{8,1... | collective-permute-start | bytes 3145736 | tf_op jit(solution)/shard_map/ppermute | solution.py:308
  3.7 117.2 %collective-permute-start.2 = (bf16[4096,128]{1,0:T(8,128)(2,1)}, bf16[4096,128]{1,0:T(8,128)(2,1)S(1)}, u32[]{:S(2)}, u32[]{:S(2)}) collective-permute-start(bf16[4096,128]{1,0:T(8,128)(2,1)} %x0_ref.3), channel_id=1, source_target_pairs={{3,0},{0,1},{1,2},{2,3},{7,4},{4,5},{5,6},{6,7},{11,8},{8,9},{9,10... | collective-permute-start | bytes 3145736 | tf_op jit(solution)/shard_map/ppermute | solution.py:308
  10.2 70.9 %copy-start.4 = (s32[512,128]{1,0:T(8,128)S(1)}, s32[512,128]{1,0:T(8,128)}, u32[]{:S(2)}) copy-start(s32[512,128]{1,0:T(8,128)} %dst_ref.1) | copy-start | bytes 786436
  10.2 71.0 %copy-start.5 = (s32[512,128]{1,0:T(8,128)S(1)}, s32[512,128]{1,0:T(8,128)}, u32[]{:S(2)}) copy-start(s32[512,128]{1,0:T(8,128)} %src_ref.1) | copy-start | bytes 786436
  120.9 1.0 copy-start.1
  120.9 1.3 copy-start.2
  120.9 1.6 copy-start.3
  197.2 60.0 %copy-start.6 = (bf16[512,128]{1,0:T(8,128)(2,1)S(1)}, bf16[512,128]{1,0:T(8,128)(2,1)}, u32[]{:S(2)}) copy-start(bf16[512,128]{1,0:T(8,128)(2,1)} %param.11) | copy-start | bytes 393220
  253.3 22.3 %all-to-all-start.1 = ((bf16[32,144,128]{2,1,0:T(8,128)(2,1)}), bf16[32,144,128]{2,1,0:T(8,128)(2,1)S(1)}, u32[]{:S(2)}, u32[]{:S(2)}) async-start(bf16[32,144,128]{2,1,0:T(8,128)(2,1)} %get-tuple-element.13), calls=%async_computation.1 | async-start | bytes 2359296 | tf_op jit(solution)/shard_map/all_to_all | solution.py:352
  275.6 1.0 copy-start
  276.6 28.6 %copy-start.7 = (f32[128]{0:T(128)S(1)}, f32[128]{0:T(128)}, u32[]{:S(2)}) copy-start(f32[128]{0:T(128)} %param.14) | copy-start | bytes 1540
  297.6 5.0 %collective-permute-start.5 = (f32[32,128]{1,0:T(8,128)S(1)}, f32[32,128]{1,0:T(8,128)S(1)}, u32[]{:S(2)}, u32[]{:S(2)}) collective-permute-start(f32[32,128]{1,0:T(8,128)S(1)} %bitcast.9), channel_id=1, source_target_pairs={{3,0},{0,1},{1,2},{2,3},{7,4},{4,5},{5,6},{6,7},{11,8},{8,9},{9,10... | collective-permute-start | bytes 49160 | tf_op jit(solution)/shard_map/ppermute | solution.py:308
  299.6 5.2 %collective-permute-start.4 = (f32[32,128]{1,0:T(8,128)S(1)}, f32[32,128]{1,0:T(8,128)S(1)}, u32[]{:S(2)}, u32[]{:S(2)}) collective-permute-start(f32[32,128]{1,0:T(8,128)S(1)} %bitcast.10), channel_id=1, source_target_pairs={{2,0},{3,1},{0,2},{1,3},{6,4},{7,5},{4,6},{5,7},{10,8},{11,9},{8,1... | collective-permute-start | bytes 49160 | tf_op jit(solution)/shard_map/ppermute | solution.py:308
  301.4 3.7 %collective-permute-start.3 = (f32[32,128]{1,0:T(8,128)S(1)}, f32[32,128]{1,0:T(8,128)S(1)}, u32[]{:S(2)}, u32[]{:S(2)}) collective-permute-start(f32[32,128]{1,0:T(8,128)S(1)} %bitcast.11), channel_id=1, source_target_pairs={{1,0},{2,1},{3,2},{0,3},{5,4},{6,5},{7,6},{4,7},{9,8},{10,9},{11,1... | collective-permute-start | bytes 49160 | tf_op jit(solution)/shard_map/ppermute | solution.py:308

commit v2 on v1

--- a/solution.py
+++ b/solution.py
@@ -57,7 +57,7 @@
     steps = model_dim // depth
     per_part = cols // depth
     return pl.pallas_call(
-        functools.partial(mix_kernel, chunk=256),
+        functools.partial(mix_kernel, chunk=2048),
         out_shape=jax.ShapeDtypeStruct((blocks // 2, 2, model_dim, cols), BF),
         grid_spec=pltpu.PrefetchScalarGridSpec(
             num_scalar_prefetch=1,
@@ -77,135 +77,172 @@
     )(feat, lhs, bases)
 
 
-def adjacency_kernel(
-    src_tile_ref, dst_tile_ref, live_ref, src_ref, dst_ref, adj_ref, deg_ref, *, group
-):
-    step = pl.program_id(0)
-
-    @pl.when(step == 0)
-    def _():
-        deg_ref[...] = jnp.zeros_like(deg_ref)
-
-    slot = lax.broadcasted_iota(jnp.int32, (TILE, TILE), 0)
-    total = deg_ref[...]
-    for i in range(group):
-        block = step * group + i
-        dst_tile = dst_tile_ref[block]
-        base = jnp.where(block < live_ref[0], dst_tile * TILE, 1 << 20)
-        dst = dst_ref[i : i + 1, :] - base
-        src = src_ref[i : i + 1, :] - src_tile_ref[block] * TILE
-        dst_hot = jnp.where(slot == dst, 1.0, 0.0).astype(BF)
-        src_hot = jnp.where(slot == src, 1.0, 0.0).astype(BF)
-        mark = jnp.where(slot == dst_tile, 1.0, 0.0).astype(BF)
-        right = jnp.concatenate([src_hot, mark], axis=0)
-        out = lax.dot_general(
-            dst_hot, right, (((1,), (1,)), ((), ())), preferred_element_type=F32
-        )
-        adj_ref[i] = out[:, :TILE].astype(BF)
-        total = total + out[:, TILE:]
-    deg_ref[...] = total
-
-
-def adjacency(src_tile, dst_tile, live, edge_src, edge_dst):
-    blocks = edge_src.shape[0]
-    group = 8
-    return pl.pallas_call(
-        functools.partial(adjacency_kernel, group=group),
-        out_shape=(
-            jax.ShapeDtypeStruct((blocks, TILE, TILE), BF),
-            jax.ShapeDtypeStruct((TILE, TILE), F32),
-        ),
-        grid_spec=pltpu.PrefetchScalarGridSpec(
-            num_scalar_prefetch=3,
-            grid=(blocks // group,),
-            in_specs=[
-                pl.BlockSpec((group, TILE), lambda i, *_: (i, 0)),
-                pl.BlockSpec((group, TILE), lambda i, *_: (i, 0)),
-            ],
-            out_specs=(
-                pl.BlockSpec((group, TILE, TILE), lambda i, *_: (i, 0, 0)),
-                pl.BlockSpec((TILE, TILE), lambda i, *_: (0, 0)),
-            ),
-        ),
-        compiler_params=pltpu.CompilerParams(vmem_limit_bytes=VMEM_LIMIT),
-        name="adjacency",
-    )(src_tile, dst_tile, live, edge_src, edge_dst)
+def unpack(word):
+    return word & 511, (word >> 9) & 31, (word >> 14) & 63, word >> 20
 
 
 def blocks_kernel(
-    src_tile_ref,
-    dst_tile_ref,
-    live_ref,
-    w_ref,
-    adj_ref,
-    deg_ref,
+    word_ref,
+    span_ref,
+    src_ref,
+    dst_ref,
     x0_ref,
     x1_ref,
     x2_ref,
     x3_ref,
+    w_ref,
     out_ref,
     acc,
+    deg,
+    held,
+    sems,
     *,
     group,
+    owners,
+    split,
 ):
-    step = pl.program_id(0)
-
-    @pl.when(step == 0)
+    first_group, end_group = span_ref[0], span_ref[1]
+
+    def fetch(at):
+        side = at & 1
+        for k in range(2 * group):
+            block = word_ref[at * (2 * group) + k] & 511
+            pltpu.make_async_copy(
+                w_ref.at[block >> 1, block & 1], held.at[side, k // 2, k % 2], sems.at[side]
+            ).start()
+
+    @pl.when(first_group < end_group)
     def _():
-        acc[...] = jnp.zeros_like(acc)
-
-    @pl.when(step * group < live_ref[0])
-    def _():
-        for i in range(group):
-            block = step * group + i
-            row = pl.multiple_of(src_tile_ref[block] * TILE, TILE)
-            rows = pl.ds(row, TILE)
+        fetch(first_group)
+
+    acc[...] = jnp.zeros_like(acc)
+    deg[...] = jnp.zeros_like(deg)
+
+    def body(here, carry):
+        side = here & 1
+
+        @pl.when(here + 1 < end_group)
+        def _():
+            fetch(here + 1)
+
+        pltpu.make_async_copy(w_ref.at[pl.ds(0, group)], held.at[side], sems.at[side]).wait()
+        slot = lax.broadcasted_iota(jnp.int32, (TILE, TILE), 0).astype(F32).astype(BF)
+        lane = lax.broadcasted_iota(jnp.int32, (TILE, TILE), 1)
+        one = jnp.ones((TILE, TILE), BF)
+        zero = jnp.zeros((TILE, TILE), BF)
+
+        def diagonal(first, second):
+            top = jnp.concatenate([first, zero], axis=1)
+            bottom = jnp.concatenate([zero, second], axis=1)
+            return jnp.concatenate([top, bottom], axis=0)
+
+        def fields(pair, k):
+            return unpack(word_ref[(here * group + pair) * 2 + k])
+
+        def adjacency(pair):
+            dst_hot, src_hot, count = [], [], None
+            for k in range(2):
+                block, src_tile, dst_tile, used = fields(pair, k)
+                base = jnp.where(used > 0, dst_tile * TILE, 1 << 20)
+                dst = (dst_ref[pl.ds(block, 1), :] - base).astype(F32).astype(BF)
+                src = (src_ref[pl.ds(block, 1), :] - src_tile * TILE).astype(F32).astype(BF)
+                dst_hot.append(jnp.where(slot == dst, one, zero))
+                src_hot.append(jnp.where(slot == src, one, zero))
+                column = jnp.sum(dst_hot[k].astype(F32), axis=1, keepdims=True)
+                extra = jnp.where(lane == lax.rem(dst_tile, owners), column, 0.0)
+                count = extra if count is None else count + extra
+            found = lax.dot_general(
+                jnp.concatenate(dst_hot, axis=1),
+                diagonal(src_hot[0], src_hot[1]),
+                (((1,), (1,)), ((), ())),
+                preferred_element_type=F32,
+            )
+            return found.astype(BF), count
+
+        def message(pair):
+            src_tile = fields(pair, 0)[1]
+            rows = pl.ds(pl.multiple_of(src_tile * TILE, TILE), TILE)
             tile = jnp.concatenate(
                 [x0_ref[rows, :], x1_ref[rows, :], x2_ref[rows, :], x3_ref[rows, :]], axis=1
             )
-            message = jnp.dot(tile, w_ref[i // 2, i % 2], preferred_element_type=F32).astype(BF)
-            dst = dst_tile_ref[block]
-            acc[dst] = acc[dst] + jnp.dot(adj_ref[i], message, preferred_element_type=F32)
-
-    @pl.when(step == pl.num_programs(0) - 1)
-    def _():
-        owners = out_ref.shape[1]
-        degree = deg_ref[...].T
-        high = jnp.floor(degree * (1.0 / 256.0)) * 256.0
-        low = degree - high
-        line = lax.broadcasted_iota(jnp.int32, (owners, DEG_ROWS, TILE), 1)
-        for part in range(2):
-            here = slice(part * owners, (part + 1) * owners)
-            out_ref[part, :, :TILE, :] = acc[here].astype(BF)
-            rows = jnp.where(
-                line == 0, high[here][:, None, :], jnp.where(line == 1, low[here][:, None, :], 0.0)
-            )
-            out_ref[part, :, TILE:, :] = rows.astype(BF)
-
-
-def blocks_call(src_tile, dst_tile, live, weights, adj, deg, pieces, owners):
-    pairs, _, model_dim, cols = weights.shape
-    group = 8
-    whole = lambda shape: pl.BlockSpec(shape, lambda i, *_: (0,) * len(shape))
-    out = (2, owners, TILE + DEG_ROWS, cols)
+            weight = jnp.concatenate([held[side, pair, 0], held[side, pair, 1]], axis=1)
+            out = jnp.dot(tile, weight, preferred_element_type=F32).astype(BF)
+            return diagonal(out[:, :TILE], out[:, TILE:])
+
+        total = deg[...]
+        for first in range(0, group, split):
+            pairs = range(first, first + split)
+            found = [adjacency(pair) for pair in pairs]
+            messages = [message(pair) for pair in pairs]
+            sums = [
+                jnp.dot(f[0], m, preferred_element_type=F32) for f, m in zip(found, messages)
+            ]
+            for pair, both, part in zip(pairs, sums, found):
+                total = total + part[1]
+                for k in range(2):
+                    dst = lax.rem(fields(pair, k)[2], owners)
+                    acc[dst] = acc[dst] + both[:, k * TILE : (k + 1) * TILE]
+        deg[...] = total
+        return carry
+
+    lax.fori_loop(first_group, end_group, body, 0)
+
+    degree = deg[...].T[:owners]
+    high = jnp.floor(degree * (1.0 / 256.0)) * 256.0
+    low = degree - high
+    line = lax.broadcasted_iota(jnp.int32, (owners, DEG_ROWS, TILE), 1)
+    out_ref[:, :TILE, :] = acc[...].astype(BF)
+    rows = jnp.where(line == 0, high[:, None, :], jnp.where(line == 1, low[:, None, :], 0.0))
+    out_ref[:, TILE:, :] = rows.astype(BF)
+
+
+def blocks_call(words, span, weights, edge_src, edge_dst, pieces, owners, name, group=16, split=16):
+    _, _, model_dim, cols = weights.shape
+    vmem = pl.BlockSpec(memory_space=pltpu.VMEM)
+    smem = pl.BlockSpec(memory_space=pltpu.SMEM)
     return pl.pallas_call(
-        functools.partial(blocks_kernel, group=group),
-        out_shape=jax.ShapeDtypeStruct(out, BF),
-        grid_spec=pltpu.PrefetchScalarGridSpec(
-            num_scalar_prefetch=3,
-            grid=(pairs * 2 // group,),
-            in_specs=[
-                pl.BlockSpec((group // 2, 2, model_dim, cols), lambda i, *_: (i, 0, 0, 0)),
-                pl.BlockSpec((group, TILE, TILE), lambda i, *_: (i, 0, 0)),
-                whole(deg.shape),
-            ]
-            + [whole(p.shape) for p in pieces],
-            out_specs=whole(out),
-            scratch_shapes=[pltpu.VMEM((2 * owners, TILE, cols), F32)],
-        ),
+        functools.partial(blocks_kernel, group=group, owners=owners, split=split),
+        out_shape=jax.ShapeDtypeStruct((owners, TILE + DEG_ROWS, cols), BF),
+        in_specs=[smem, smem, vmem, vmem] + [vmem] * len(pieces) + [pl.BlockSpec(memory_space=pl.ANY)],
+        out_specs=vmem,
+        scratch_shapes=[
+            pltpu.VMEM((owners, TILE, cols), F32),
+            pltpu.VMEM((TILE, TILE), F32),
+            pltpu.VMEM((2, group, 2, model_dim, cols), BF),
+            pltpu.SemaphoreType.DMA((2,)),
+        ],
         compiler_params=pltpu.CompilerParams(vmem_limit_bytes=VMEM_LIMIT),
-        name="blocks",
-    )(src_tile, dst_tile, live, weights, adj, deg, *pieces)
+        name=name,
+    )(words, span, edge_src, edge_dst, *pieces, weights)
+
+
+def arrange(src_tile, dst_tile, live, owners, src_tiles, group):
+    blocks = src_tile.shape[0]
+    keys = 2 * src_tiles
+    slots = 2 * group * (-(-(blocks + keys) // (2 * group)) + 1)
+    index = jnp.arange(blocks, dtype=jnp.int32)
+    key_range = jnp.arange(keys, dtype=jnp.int32)
+    active = index < live
+    key = jnp.where(active, jnp.where(dst_tile < owners, src_tiles, 0) + src_tile, keys)
+    count = jnp.sum((key[None, :] == key_range[:, None]).astype(jnp.int32), axis=1)
+    pairs = (count + 1) >> 1
+    start = jnp.sum(jnp.where(key_range[None, :] < key_range[:, None], pairs[None, :], 0), axis=1)
+    mirror_pairs = jnp.sum(pairs[:src_tiles])
+    hub_pairs = jnp.sum(pairs[src_tiles:])
+    mirror_groups = (mirror_pairs + group - 1) // group
+    hub_groups = (hub_pairs + group - 1) // group
+    start = start + jnp.where(key_range >= src_tiles, mirror_groups * group - mirror_pairs, 0)
+    before = (key[None, :] == key[:, None]) & (index[None, :] < index[:, None])
+    rank = jnp.sum(before.astype(jnp.int32), axis=1)
+    place = jnp.sum(jnp.where(key[:, None] == key_range[None, :], start[None, :], 0), axis=1)
+    place = jnp.where(active, 2 * place + rank, -1)
+    word = index | (src_tile << 9) | (dst_tile << 14) | (1 << 20)
+    slot = jnp.arange(slots, dtype=jnp.int32)
+    words = jnp.sum(jnp.where(place[None, :] == slot[:, None], word[None, :], 0), axis=1)
+    zero = jnp.zeros((), jnp.int32)
+    mirror_span = jnp.stack([zero, mirror_groups])
+    hub_span = jnp.stack([mirror_groups, mirror_groups + hub_groups])
+    return words, mirror_span, hub_span
 
 
 def final_kernel(
@@ -344,12 +381,17 @@
     group = lax.broadcasted_iota(jnp.int32, lhs.shape, 1) // n_bases
     lhs = jnp.where(line == group, lhs, 0.0).astype(BF)
 
-    adj, deg = adjacency(src_tile, dst_tile, block_count, edge_src, edge_dst)
+    group_size = 16
+    words, mirror_span, hub_span = arrange(
+        src_tile, dst_tile, block_count[0], owners, n_local // TILE, group_size
+    )
     weights = mix(feat.reshape(1), lhs, bases, blocks)
-    partial = blocks_call(src_tile, dst_tile, block_count, weights, adj, deg, pieces, owners)
-
-    hub = lax.all_to_all(partial[0], "dom", split_axis=0, concat_axis=0, tiled=True)
-    mirror = lax.all_to_all(partial[1], "dom", split_axis=0, concat_axis=0, tiled=True)
+    edges = (edge_src, edge_dst)
+    mirror_part = blocks_call(words, mirror_span, weights, *edges, pieces, owners, "mirror_blocks")
+    mirror = lax.all_to_all(mirror_part, "dom", split_axis=0, concat_axis=0, tiled=True)
+    weights, _ = lax.optimization_barrier((weights, mirror_part))
+    hub_part = blocks_call(words, hub_span, weights, *edges, pieces, owners, "hub_blocks")
+    hub = lax.all_to_all(hub_part, "dom", split_axis=0, concat_axis=0, tiled=True)
 
     turned = jnp.roll(self_weight, -feat * cols, axis=0)
     mixed, squares = final(hub, mirror, mirror_master_rows.reshape(owners, TILE), turned, pieces)

time: 311 us -> 194 us (0.62)
  Pallas kernels: 202 us -> 110 us
  blocking collectives: 56 us -> 26.4 us
  other arithmetic: 4.49 us -> 8.87 us
    pallas_call x3, Pallas kernels: 182 us -> 89.9 us  [the longest x2 51.6 us: blocks_call(): pl.pallas_call(functools.partial(blocks_kernel, group=group, owners=owner...]
    all_to_all x1, blocking collectives: 56 us -> 26.4 us  [on_device(): lax.all_to_all(hub_part, 'dom', split_axis=0, concat_axis=0, tiled=True)]
  transfers between devices with their start and end apart: 7 -> 7, of which waited for: 4 -> 3; matrix products, arithmetic and copies ran while one was open for 2% -> 6% of each run, Pallas kernels for 36% -> 20%
where the time goes in v2:
time: 194 us; the launch traced here: 192 us
  Pallas kernels  110 us (57%)
  blocking collectives  26.4 us (14%)
  waiting for transfers between devices  22.1 us (11%)
  starting transfers between devices  12.7 us (7%)
  other arithmetic  8.87 us (5%)
  local copies, waits for them, and re-layouts  5.26 us (3%)
  matrix products  3.83 us (2%)
  between operations  2.92 us (2%)
    pallas_call x2, Pallas kernels, blocks_call(): pl.pallas_call(functools.partial(blocks_kernel, group=group, owners=owner...  51.6 us
    pallas_call x1, Pallas kernels, mix(): pl.pallas_call(functools.partial(mix_kernel, chunk=2048), out_shape=jax.S...  38.2 us
    all_to_all x1, blocking collectives, on_device(): lax.all_to_all(hub_part, 'dom', split_axis=0, concat_axis=0, tiled=True)  26.4 us
    pallas_call x1, Pallas kernels, final(): pl.pallas_call(functools.partial(final_kernel, chunk=chunk), out_shape=(j...  20.1 us
    all_to_all x1, waiting for transfers between devices, on_device(): lax.all_to_all(mirror_part, 'dom', split_axis=0, concat_axis=0, tiled=True)  17.2 us
    ppermute x6, starting transfers between devices, from_others(): lax.ppermute(x, 'feat', [((i + shift) % size, i) for i in range(size)])  8.72 us
    ppermute x6, waiting for transfers between devices, from_others(): lax.ppermute(x, 'feat', [((i + shift) % size, i) for i in range(size)])  4.95 us
    all_to_all x1, starting transfers between devices, on_device(): lax.all_to_all(mirror_part, 'dom', split_axis=0, concat_axis=0, tiled=True)  3.94 us
  transfers between devices with their start and end apart: 7, of which 3 were waited for; matrix products, arithmetic and copies ran while one was open for 6% of the time, Pallas kernels for 20%

profile of v2, /device:TPU:0, one launch (start us, length us, event | category | flops | bytes accessed | tf_op | source)
XLA Modules:
  0.0 192.1 jit_solution(17189651333660700107)
XLA Ops:
  0.0 3.1 %collective-permute-start = (bf16[4096,128]{1,0:T(8,128)(2,1)}, bf16[4096,128]{1,0:T(8,128)(2,1)S(1)}, u32[]{:S(2)}, u32[]{:S(2)}) collective-permute-start(bf16[4096,128]{1,0:T(8,128)(2,1)} %x0_ref.5), channel_id=1, source_target_pairs={{1,0},{2,1},{3,2},{0,3},{5,4},{6,5},{7,6},{4,7},{9,8},{10,9},{11,1... | collective-permute-start | bytes 3145736 | tf_op jit(solution)/shard_map/ppermute | solution.py:345
  3.1 0.6 collective-permute-start.1
  3.7 1.0 collective-permute-start.2
  5.4 1.6 fusion.17
  7.0 0.1 convert_reduce_fusion.1
  7.1 0.8 slice_reduce_fusion.2
  10.0 0.8 broadcast_in_dim.90
  10.8 0.2 eq.91
  11.0 0.6 pad_add_fusion.1.span_ref
  11.6 3.8 %fusion.3.lhs_ref = bf16[2048,256]{1,0:T(8,128)(2,1)} fusion(s32[2048]{0:T(1024)S(1)} %eq.91, s32[256]{0:T(256)S(1)} %get-tuple-element.20, s32[256]{0:T(256)S(1)} %get-tuple-element.21, s32[2048]{0:T(1024)S(1)} %get-tuple-element.18, s32[2048]{0:T(1024)S(1)} %get-tuple-element.19, pred[2048]{0:T(1024)(128)(4,1)S(1)} %fusion.24, ...), kind=kOutput, calls=%fused_computation.4 | convolution fusion | flops 867917824 | bytes 1182720 | tf_op jit(solution)/shard_map/dot_general | solution.py:379
  15.4 38.2 %mix.1.w_ref = bf16[256,2,512,128]{3,2,1,0:T(8,128)(2,1)} custom-call(s32[1]{0:T(128)} %bitcast.3.feat_ref, bf16[2048,256]{1,0:T(8,128)(2,1)} %fusion.3.lhs_ref, bf16[64,512,128]{2,1,0:T(8,128)(2,1)} %bases_ref.1), custom_call_target="tpu_custom_call" | custom-call | tf_op jit(solution)/shard_map/mix/pallas_call | solution.py:59
  53.7 0.6 pad_add_fusion.span_ref
  54.3 0.1 select_reduce_fusion.2
  54.4 0.1 select_reduce_fusion.1
  54.5 0.2 convert_reduce_fusion
  54.8 0.8 select_reduce_fusion.word_ref
  55.6 0.0 collective-permute-done.x1_ref
  55.6 0.0 copy-start
  55.6 0.0 collective-permute-done.1.x2_ref
  55.6 0.0 copy-start.1
  55.6 0.0 collective-permute-done.2.x3_ref
  55.6 0.9 copy-done
  56.6 0.4 copy-done.1
  56.9 0.0 copy-start.2
  56.9 1.0 copy-done.2
  57.9 32.8 %mirror_blocks.1 = bf16[32,144,128]{2,1,0:T(8,128)(2,1)} custom-call(s32[608]{0:T(1024)} %select_reduce_fusion.word_ref, s32[2]{0:T(128)} %pad_add_fusion.1.span_ref, s32[512,128]{1,0:T(8,128)} %src_ref.3, s32[512,128]{1,0:T(8,128)} %dst_ref.3, bf16[4096,128]{1,0:T(8,128)(2,1)} %x0_ref.5, bf16[4096,128]{1,0:T(8,128)(2,1)} %copy-done, ...), custom_call_target="tpu_custom_call" | custom-call | tf_op jit(solution)/shard_map/mirror_blocks/pallas_call | solution.py:203
  90.8 18.8 %hub_blocks.1 = bf16[32,144,128]{2,1,0:T(8,128)(2,1)} custom-call(s32[608]{0:T(1024)} %select_reduce_fusion.word_ref, s32[2]{0:T(128)} %pad_add_fusion.span_ref, s32[512,128]{1,0:T(8,128)} %src_ref.3, s32[512,128]{1,0:T(8,128)} %dst_ref.3, bf16[4096,128]{1,0:T(8,128)(2,1)} %x0_ref.5, bf16[4096,128]{1,0:T(8,128)(2,1)} %copy-done, ...), custom_call_target="tpu_custom_call" | custom-call | tf_op jit(solution)/shard_map/hub_blocks/pallas_call | solution.py:203
  109.6 0.0 copy-start.4
  109.6 26.4 %all_to_all.10.hub_ref = bf16[32,144,128]{2,1,0:T(8,128)(2,1)} all-to-all(bf16[32,144,128]{2,1,0:T(8,128)(2,1)} %hub_blocks.1), channel_id=1, replica_groups=mesh['dom'=32,'feat'=4] {'dom'}, dimensions={0} | all-to-all | bytes 2359296 | tf_op jit(solution)/shard_map/all_to_all | solution.py:394
  136.0 3.9 %all-to-all-start.1 = ((bf16[32,144,128]{2,1,0:T(8,128)(2,1)}), bf16[32,144,128]{2,1,0:T(8,128)(2,1)S(1)}, u32[]{:S(2)}, u32[]{:S(2)}) async-start(bf16[32,144,128]{2,1,0:T(8,128)(2,1)} %mirror_blocks.1), calls=%async_computation.1 | async-start | bytes 2359296 | tf_op jit(solution)/shard_map/all_to_all | solution.py:391
  139.9 0.0 copy-done.4
  140.0 1.1 fusion.20.self_ref
  141.1 17.2 %all-to-all-done.1.mirror_ref = bf16[32,144,128]{2,1,0:T(8,128)(2,1)S(1)} async-done(((bf16[32,144,128]{2,1,0:T(8,128)(2,1)}), bf16[32,144,128]{2,1,0:T(8,128)(2,1)S(1)}, u32[]{:S(2)}, u32[]{:S(2)}) %all-to-all-start.1) | async-done | bytes 1179680 | tf_op jit(solution)/shard_map/all_to_all | solution.py:391
  158.3 0.0 copy-start.3
  158.3 1.0 copy-done.3
  159.3 0.0 copy-start.5
  159.3 20.1 %final.1 = (f32[4096,128]{1,0:T(8,128)}, f32[8,4096]{1,0:T(8,128)}) custom-call(bf16[32,144,128]{2,1,0:T(8,128)(2,1)} %all_to_all.10.hub_ref, bf16[32,144,128]{2,1,0:T(8,128)(2,1)} %copy-done.3, s32[32,128]{1,0:T(8,128)} %bitcast.15, bf16[512,128]{1,0:T(8,128)(2,1)} %fusion.20.self_ref, bf16[4096,128]{1,0:T(8,128)(2,1)} %x0_ref.5, ...), custom_call_target="tpu_custom_call" | custom-call | tf_op jit(solution)/shard_map/final/pallas_call | solution.py:324
  179.5 0.9 slice.19
  180.4 2.3 %collective-permute-start.3 = (f32[32,128]{1,0:T(8,128)S(1)}, f32[32,128]{1,0:T(8,128)S(1)}, u32[]{:S(2)}, u32[]{:S(2)}) collective-permute-start(f32[32,128]{1,0:T(8,128)S(1)} %bitcast.11), channel_id=1, source_target_pairs={{1,0},{2,1},{3,2},{0,3},{5,4},{6,5},{7,6},{4,7},{9,8},{10,9},{11,1... | collective-permute-start | bytes 49160 | tf_op jit(solution)/shard_map/ppermute | solution.py:345
  182.7 1.7 collective-permute-start.4
  184.4 0.0 collective-permute-start.5
  184.4 0.0 collective-permute-done.3
  184.4 3.6 %collective-permute-done.4 = f32[32,128]{1,0:T(8,128)S(1)} collective-permute-done((f32[32,128]{1,0:T(8,128)S(1)}, f32[32,128]{1,0:T(8,128)S(1)}, u32[]{:S(2)}, u32[]{:S(2)}) %collective-permute-start.4) | collective-permute-done | bytes 16416 | tf_op jit(solution)/shard_map/ppermute | solution.py:345
  188.0 1.4 collective-permute-done.5
  189.4 0.0 copy-done.5
  189.4 2.7 %multiply_convert_fusion = bf16[4096,128]{1,0:T(8,128)(2,1)} fusion(f32[4096,128]{1,0:T(8,128)} %get-tuple-element.9, f32[128]{0:T(128)S(1)} %copy-done.5, f32[4096]{0:T(1024)S(1)} %rsqrt_bitcast_fusion), kind=kLoop, calls=%fused_computation.5 | loop fusion | flops 1572864 | bytes 3162624 | tf_op jit(solution)/shard_map/convert_element_type | solution.py:403
  (9 shorter events, 0.1 us)
Async XLA Ops:
  0.0 55.6 %collective-permute-start = (bf16[4096,128]{1,0:T(8,128)(2,1)}, bf16[4096,128]{1,0:T(8,128)(2,1)S(1)}, u32[]{:S(2)}, u32[]{:S(2)}) collective-permute-start(bf16[4096,128]{1,0:T(8,128)(2,1)} %x0_ref.5), channel_id=1, source_target_pairs={{1,0},{2,1},{3,2},{0,3},{5,4},{6,5},{7,6},{4,7},{9,8},{10,9},{11,1... | collective-permute-start | bytes 3145736 | tf_op jit(solution)/shard_map/ppermute | solution.py:345
  3.1 52.5 %collective-permute-start.1 = (bf16[4096,128]{1,0:T(8,128)(2,1)}, bf16[4096,128]{1,0:T(8,128)(2,1)S(1)}, u32[]{:S(2)}, u32[]{:S(2)}) collective-permute-start(bf16[4096,128]{1,0:T(8,128)(2,1)} %x0_ref.5), channel_id=1, source_target_pairs={{2,0},{3,1},{0,2},{1,3},{6,4},{7,5},{4,6},{5,7},{10,8},{11,9},{8,1... | collective-permute-start | bytes 3145736 | tf_op jit(solution)/shard_map/ppermute | solution.py:345
  3.7 51.9 %collective-permute-start.2 = (bf16[4096,128]{1,0:T(8,128)(2,1)}, bf16[4096,128]{1,0:T(8,128)(2,1)S(1)}, u32[]{:S(2)}, u32[]{:S(2)}) collective-permute-start(bf16[4096,128]{1,0:T(8,128)(2,1)} %x0_ref.5), channel_id=1, source_target_pairs={{3,0},{0,1},{1,2},{2,3},{7,4},{4,5},{5,6},{6,7},{11,8},{8,9},{9,10... | collective-permute-start | bytes 3145736 | tf_op jit(solution)/shard_map/ppermute | solution.py:345
  55.6 1.0 copy-start
  55.6 1.3 copy-start.1
  56.9 1.0 copy-start.2
  109.6 30.4 %copy-start.4 = (bf16[512,128]{1,0:T(8,128)(2,1)S(1)}, bf16[512,128]{1,0:T(8,128)(2,1)}, u32[]{:S(2)}) copy-start(bf16[512,128]{1,0:T(8,128)(2,1)} %param.11) | copy-start | bytes 393220
  136.0 22.3 %all-to-all-start.1 = ((bf16[32,144,128]{2,1,0:T(8,128)(2,1)}), bf16[32,144,128]{2,1,0:T(8,128)(2,1)S(1)}, u32[]{:S(2)}, u32[]{:S(2)}) async-start(bf16[32,144,128]{2,1,0:T(8,128)(2,1)} %mirror_blocks.1), calls=%async_computation.1 | async-start | bytes 2359296 | tf_op jit(solution)/shard_map/all_to_all | solution.py:391
  158.3 1.0 copy-start.3
  159.3 30.1 %copy-start.5 = (f32[128]{0:T(128)S(1)}, f32[128]{0:T(128)}, u32[]{:S(2)}) copy-start(f32[128]{0:T(128)} %param.14) | copy-start | bytes 1540
  180.4 4.0 %collective-permute-start.3 = (f32[32,128]{1,0:T(8,128)S(1)}, f32[32,128]{1,0:T(8,128)S(1)}, u32[]{:S(2)}, u32[]{:S(2)}) collective-permute-start(f32[32,128]{1,0:T(8,128)S(1)} %bitcast.11), channel_id=1, source_target_pairs={{1,0},{2,1},{3,2},{0,3},{5,4},{6,5},{7,6},{4,7},{9,8},{10,9},{11,1... | collective-permute-start | bytes 49160 | tf_op jit(solution)/shard_map/ppermute | solution.py:345
  182.7 5.2 %collective-permute-start.4 = (f32[32,128]{1,0:T(8,128)S(1)}, f32[32,128]{1,0:T(8,128)S(1)}, u32[]{:S(2)}, u32[]{:S(2)}) collective-permute-start(f32[32,128]{1,0:T(8,128)S(1)} %bitcast.12), channel_id=1, source_target_pairs={{2,0},{3,1},{0,2},{1,3},{6,4},{7,5},{4,6},{5,7},{10,8},{11,9},{8,1... | collective-permute-start | bytes 49160 | tf_op jit(solution)/shard_map/ppermute | solution.py:345
  184.4 4.9 %collective-permute-start.5 = (f32[32,128]{1,0:T(8,128)S(1)}, f32[32,128]{1,0:T(8,128)S(1)}, u32[]{:S(2)}, u32[]{:S(2)}) collective-permute-start(f32[32,128]{1,0:T(8,128)S(1)} %bitcast.13), channel_id=1, source_target_pairs={{3,0},{0,1},{1,2},{2,3},{7,4},{4,5},{5,6},{6,7},{11,8},{8,9},{9,10... | collective-permute-start | bytes 49160 | tf_op jit(solution)/shard_map/ppermute | solution.py:345

commit v3 on v2

--- a/solution.py
+++ b/solution.py
@@ -81,26 +81,11 @@
     return word & 511, (word >> 9) & 31, (word >> 14) & 63, word >> 20
 
 
-def blocks_kernel(
-    word_ref,
-    span_ref,
-    src_ref,
-    dst_ref,
-    x0_ref,
-    x1_ref,
-    x2_ref,
-    x3_ref,
-    w_ref,
-    out_ref,
-    acc,
-    deg,
-    held,
-    sems,
-    *,
-    group,
-    owners,
-    split,
-):
+def blocks_kernel(*refs, group, owners, split, n_out):
+    word_ref, span_ref, src_hbm, dst_hbm = refs[:4]
+    piece_refs, w_ref = refs[4:8], refs[8]
+    out_refs = refs[9 : 9 + n_out]
+    acc, deg, held, src_ref, dst_ref, table, sems = refs[9 + n_out :]
     first_group, end_group = span_ref[0], span_ref[1]
 
     def fetch(at):
@@ -115,8 +100,20 @@
     def _():
         fetch(first_group)
 
+    cols = table.shape[1] // len(piece_refs)
+    loads = [
+        pltpu.make_async_copy(src_hbm, src_ref, sems.at[2]),
+        pltpu.make_async_copy(dst_hbm, dst_ref, sems.at[3]),
+    ]
+    for p, piece in enumerate(piece_refs):
+        here = table.at[:, p * cols : (p + 1) * cols]
+        loads.append(pltpu.make_async_copy(piece, here, sems.at[4 + p]))
+    for load in loads:
+        load.start()
     acc[...] = jnp.zeros_like(acc)
     deg[...] = jnp.zeros_like(deg)
+    for load in loads:
+        load.wait()
 
     def body(here, carry):
         side = here & 1
@@ -162,9 +159,7 @@
         def message(pair):
             src_tile = fields(pair, 0)[1]
             rows = pl.ds(pl.multiple_of(src_tile * TILE, TILE), TILE)
-            tile = jnp.concatenate(
-                [x0_ref[rows, :], x1_ref[rows, :], x2_ref[rows, :], x3_ref[rows, :]], axis=1
-            )
+            tile = table[rows, :]
             weight = jnp.concatenate([held[side, pair, 0], held[side, pair, 1]], axis=1)
             out = jnp.dot(tile, weight, preferred_element_type=F32).astype(BF)
             return diagonal(out[:, :TILE], out[:, TILE:])
@@ -187,36 +182,54 @@
 
     lax.fori_loop(first_group, end_group, body, 0)
 
-    degree = deg[...].T[:owners]
-    high = jnp.floor(degree * (1.0 / 256.0)) * 256.0
-    low = degree - high
-    line = lax.broadcasted_iota(jnp.int32, (owners, DEG_ROWS, TILE), 1)
-    out_ref[:, :TILE, :] = acc[...].astype(BF)
-    rows = jnp.where(line == 0, high[:, None, :], jnp.where(line == 1, low[:, None, :], 0.0))
-    out_ref[:, TILE:, :] = rows.astype(BF)
-
-
-def blocks_call(words, span, weights, edge_src, edge_dst, pieces, owners, name, group=16, split=16):
+    deg[...] = deg[...].T
+    line = lax.broadcasted_iota(jnp.int32, (DEG_ROWS, TILE), 0)
+    core = span_ref[2]
+    for part, out_ref in enumerate(out_refs):
+        for i in range(owners // n_out):
+            at = i if n_out == 1 else 2 * i + (core ^ part)
+            degree = deg[pl.ds(at, 1), :]
+            high = jnp.floor(degree * (1.0 / 256.0)) * 256.0
+            low = degree - high
+            out_ref[i, :TILE, :] = acc[at].astype(BF)
+            rows = jnp.where(line == 0, high, jnp.where(line == 1, low, 0.0))
+            out_ref[i, TILE:, :] = rows.astype(BF)
+
+
+def blocks_call(
+    words, span, weights, edge_src, edge_dst, pieces, owners, name, n_out, group=16, split=16
+):
     _, _, model_dim, cols = weights.shape
     vmem = pl.BlockSpec(memory_space=pltpu.VMEM)
     smem = pl.BlockSpec(memory_space=pltpu.SMEM)
+    anywhere = pl.BlockSpec(memory_space=pl.ANY)
+    out = jax.ShapeDtypeStruct((owners // n_out, TILE + DEG_ROWS, cols), BF)
+    pairs = 512 // 2 // n_out
     return pl.pallas_call(
-        functools.partial(blocks_kernel, group=group, owners=owners, split=split),
-        out_shape=jax.ShapeDtypeStruct((owners, TILE + DEG_ROWS, cols), BF),
-        in_specs=[smem, smem, vmem, vmem] + [vmem] * len(pieces) + [pl.BlockSpec(memory_space=pl.ANY)],
-        out_specs=vmem,
+        functools.partial(blocks_kernel, group=group, owners=owners, split=split, n_out=n_out),
+        out_shape=(out,) * n_out,
+        in_specs=[smem, smem] + [anywhere] * (3 + len(pieces)),
+        out_specs=(vmem,) * n_out,
         scratch_shapes=[
             pltpu.VMEM((owners, TILE, cols), F32),
             pltpu.VMEM((TILE, TILE), F32),
             pltpu.VMEM((2, group, 2, model_dim, cols), BF),
-            pltpu.SemaphoreType.DMA((2,)),
+            pltpu.VMEM(edge_src.shape, jnp.int32),
+            pltpu.VMEM(edge_dst.shape, jnp.int32),
+            pltpu.VMEM((pieces[0].shape[0], model_dim), BF),
+            pltpu.SemaphoreType.DMA((4 + len(pieces),)),
         ],
+        cost_estimate=pl.CostEstimate(
+            flops=pairs * 2 * TILE * model_dim * cols * 4,
+            bytes_accessed=pairs * 2 * model_dim * cols * 2,
+            transcendentals=0,
+        ),
         compiler_params=pltpu.CompilerParams(vmem_limit_bytes=VMEM_LIMIT),
         name=name,
     )(words, span, edge_src, edge_dst, *pieces, weights)
 
 
-def arrange(src_tile, dst_tile, live, owners, src_tiles, group):
+def arrange(src_tile, dst_tile, live, core, owners, src_tiles, group):
     blocks = src_tile.shape[0]
     keys = 2 * src_tiles
     slots = 2 * group * (-(-(blocks + keys) // (2 * group)) + 1)
@@ -240,13 +253,20 @@
     slot = jnp.arange(slots, dtype=jnp.int32)
     words = jnp.sum(jnp.where(place[None, :] == slot[:, None], word[None, :], 0), axis=1)
     zero = jnp.zeros((), jnp.int32)
-    mirror_span = jnp.stack([zero, mirror_groups])
-    hub_span = jnp.stack([mirror_groups, mirror_groups + hub_groups])
+    mirror_span = jnp.stack([zero, mirror_groups, core])
+    hub_span = jnp.stack([mirror_groups, mirror_groups + hub_groups, core])
     return words, mirror_span, hub_span
 
 
-def final_kernel(
-    hub_ref,
+def square_lines(value):
+    squares = jnp.sum(value * value, axis=1, keepdims=True)
+    line = jnp.broadcast_to(squares, value.shape).T[:1, :]
+    pieces = [line[:, i : i + TILE] for i in range(0, value.shape[0], TILE)]
+    return jnp.concatenate(pieces, axis=0)
+
+
+def mirror_kernel(
+    feat_ref,
     mirror_ref,
     master_ref,
     self_ref,
@@ -257,17 +277,20 @@
     mixed_ref,
     squares_ref,
     right,
+    turned,
     *,
     chunk,
+    reach,
 ):
     step = pl.program_id(0)
     owners = mirror_ref.shape[0]
     cols = mirror_ref.shape[2]
-    slots = owners * TILE
-    last_chunks = pl.num_programs(0)
 
     @pl.when(step == 0)
     def _():
+        for p in range(4):
+            at = pl.multiple_of(lax.rem(feat_ref[0] + p, 4) * cols, cols)
+            turned[p * cols : (p + 1) * cols, :] = self_ref[pl.ds(at, cols), :]
         high = mirror_ref[:, TILE, :].astype(F32)
         low = mirror_ref[:, TILE + 1, :].astype(F32)
         pad = jnp.zeros((TILE - 2 * owners, TILE), F32)
@@ -283,61 +306,93 @@
     tile = jnp.concatenate(
         [x0_ref[rows, :], x1_ref[rows, :], x2_ref[rows, :], x3_ref[rows, :]], axis=1
     )
-    own = jnp.dot(tile, self_ref[...], preferred_element_type=F32)
-    entity = lax.broadcasted_iota(jnp.int32, (chunk, TILE), 0) + step * chunk
-    hot = jnp.concatenate(
-        [
-            jnp.where(entity == master_ref[p : p + 1, :], 1.0, 0.0).astype(BF)
-            for p in range(owners)
-        ],
-        axis=1,
-    )
-    sums = jnp.dot(hot, right[...], preferred_element_type=F32)
-    degree = jnp.sum(sums[:, cols:], axis=1, keepdims=True)
-    total = sums[:, :cols]
-    scale = lax.rsqrt(jnp.maximum(degree, 1.0))
-    mixed = own + total * scale
-    mixed_ref[...] = mixed
-
-    @pl.when(step == 0)
+    own = jnp.dot(tile, turned[...], preferred_element_type=F32)
+
+    @pl.when(step * chunk < reach)
     def _():
-        hub = jnp.sum(hub_ref[:, :TILE, :].astype(F32), axis=0)
-        line = jnp.sum(
-            hub_ref[:, TILE, :].astype(F32) + hub_ref[:, TILE + 1, :].astype(F32),
-            axis=0,
-            keepdims=True,
-        )
-        column = jnp.broadcast_to(line, (TILE, TILE)).T[:, :1]
-        hub_scale = lax.rsqrt(jnp.maximum(column + degree[:TILE], 1.0))
-        mixed_ref[:TILE, :] = own[:TILE] + (total[:TILE] + hub) * hub_scale
-
-    value = mixed_ref[...]
-    squares = jnp.sum(value * value, axis=1, keepdims=True)
-    squares_ref[...] = jnp.broadcast_to(squares, (chunk, TILE)).T[:8, :]
-
-
-def final(hub, mirror, master, self_weight, pieces):
+        local = lax.broadcasted_iota(jnp.int32, (TILE, TILE), 0).astype(F32).astype(BF)
+        one = jnp.ones((TILE, TILE), BF)
+        zero = jnp.zeros((TILE, TILE), BF)
+        columns = []
+        for p in range(owners):
+            column = []
+            for first in range(0, chunk, TILE):
+                target = master_ref[p : p + 1, :] - (step * chunk + first)
+                column.append(jnp.where(local == target.astype(F32).astype(BF), one, zero))
+            columns.append(jnp.concatenate(column, axis=0))
+        sums = jnp.dot(jnp.concatenate(columns, axis=1), right[...], preferred_element_type=F32)
+        degree = jnp.sum(sums[:, cols:], axis=1, keepdims=True)
+        mixed = own + sums[:, :cols] * lax.rsqrt(jnp.maximum(degree, 1.0))
+        mixed_ref[...] = mixed
+        squares_ref[0] = square_lines(mixed)
+
+    @pl.when(step * chunk >= reach)
+    def _():
+        mixed_ref[...] = own
+        squares_ref[0] = square_lines(own)
+
+
+def mirror_final(feat, mirror, master, self_weight, pieces):
     n_local, cols = pieces[0].shape
     owners = mirror.shape[0]
-    chunk = 256
-    whole = lambda shape: pl.BlockSpec(shape, lambda i: (0,) * len(shape))
+    chunk = 512
+    whole = lambda shape: pl.BlockSpec(shape, lambda i, *_: (0,) * len(shape))
     return pl.pallas_call(
-        functools.partial(final_kernel, chunk=chunk),
+        functools.partial(mirror_kernel, chunk=chunk, reach=n_local - n_local // 4),
         out_shape=(
             jax.ShapeDtypeStruct((n_local, cols), F32),
-            jax.ShapeDtypeStruct((8, n_local), F32),
-        ),
-        grid=(n_local // chunk,),
-        in_specs=[whole(hub.shape), whole(mirror.shape), whole(master.shape), whole(self_weight.shape)]
-        + [whole(p.shape) for p in pieces],
-        out_specs=(
-            pl.BlockSpec((chunk, cols), lambda i: (i, 0)),
-            pl.BlockSpec((8, chunk), lambda i: (0, i)),
-        ),
-        scratch_shapes=[pltpu.VMEM((owners * TILE, 2 * cols), BF)],
+            jax.ShapeDtypeStruct((n_local // chunk, chunk // TILE, TILE), F32),
+        ),
+        grid_spec=pltpu.PrefetchScalarGridSpec(
+            num_scalar_prefetch=1,
+            grid=(n_local // chunk,),
+            in_specs=[whole(mirror.shape), whole(master.shape), whole(self_weight.shape)]
+            + [whole(p.shape) for p in pieces],
+            out_specs=(
+                pl.BlockSpec((chunk, cols), lambda i, *_: (i, 0)),
+                pl.BlockSpec((1, chunk // TILE, TILE), lambda i, *_: (i, 0, 0)),
+            ),
+            scratch_shapes=[
+                pltpu.VMEM((owners * TILE, 2 * cols), BF),
+                pltpu.VMEM(self_weight.shape, BF),
+            ],
+        ),
+        cost_estimate=pl.CostEstimate(
+            flops=n_local * n_local * 4 * cols, bytes_accessed=8 << 20, transcendentals=0
+        ),
         compiler_params=pltpu.CompilerParams(vmem_limit_bytes=VMEM_LIMIT),
-        name="final",
-    )(hub, mirror, master, self_weight, *pieces)
+        name="mirror_final",
+    )(feat, mirror, master, self_weight, *pieces)
+
+
+def hub_kernel(hub_ref, mixed_ref, squares_ref, out_ref, lines_ref):
+    hub = jnp.sum(hub_ref[:, :TILE, :].astype(F32), axis=0)
+    counts = hub_ref[:, TILE : TILE + DEG_ROWS, :].astype(F32)
+    line = jnp.sum(jnp.sum(counts, axis=0), axis=0, keepdims=True)
+    column = jnp.broadcast_to(line, (TILE, TILE)).T[:, :1]
+    mixed = mixed_ref[...] + hub * lax.rsqrt(jnp.maximum(column, 1.0))
+    out_ref[...] = mixed
+    lines_ref[...] = squares_ref[...]
+    lines_ref[0, :1, :] = square_lines(mixed)
+
+
+def hub_final(hub, mixed, squares):
+    cols = mixed.shape[1]
+    hub_block = pl.BlockSpec(hub.shape, lambda i: (0, 0, 0))
+    mixed_block = pl.BlockSpec((HUB_MIRRORS, cols), lambda i: (0, 0))
+    line_block = pl.BlockSpec((1,) + squares.shape[1:], lambda i: (0, 0, 0))
+    return pl.pallas_call(
+        hub_kernel,
+        out_shape=(
+            jax.ShapeDtypeStruct(mixed.shape, mixed.dtype),
+            jax.ShapeDtypeStruct(squares.shape, squares.dtype),
+        ),
+        grid=(1,),
+        in_specs=[hub_block, mixed_block, line_block],
+        out_specs=(mixed_block, line_block),
+        input_output_aliases={1: 0, 2: 1},
+        name="hub_final",
+    )(hub, mixed, squares)
 
 
 def from_others(x, size):
@@ -382,20 +437,35 @@
     lhs = jnp.where(line == group, lhs, 0.0).astype(BF)
 
     group_size = 16
+    device = lax.axis_index("dom").astype(jnp.int32)
     words, mirror_span, hub_span = arrange(
-        src_tile, dst_tile, block_count[0], owners, n_local // TILE, group_size
+        src_tile, dst_tile, block_count[0], device & 1, owners, n_local // TILE, group_size
     )
     weights = mix(feat.reshape(1), lhs, bases, blocks)
     edges = (edge_src, edge_dst)
-    mirror_part = blocks_call(words, mirror_span, weights, *edges, pieces, owners, "mirror_blocks")
+    (mirror_part,) = blocks_call(
+        words, mirror_span, weights, *edges, pieces, owners, "mirror_blocks", 1
+    )
     mirror = lax.all_to_all(mirror_part, "dom", split_axis=0, concat_axis=0, tiled=True)
     weights, _ = lax.optimization_barrier((weights, mirror_part))
-    hub_part = blocks_call(words, hub_span, weights, *edges, pieces, owners, "hub_blocks")
-    hub = lax.all_to_all(hub_part, "dom", split_axis=0, concat_axis=0, tiled=True)
-
-    turned = jnp.roll(self_weight, -feat * cols, axis=0)
-    mixed, squares = final(hub, mirror, mirror_master_rows.reshape(owners, TILE), turned, pieces)
-    line = squares[0].reshape(n_local // TILE, TILE)
+    kept, sent = blocks_call(words, hub_span, weights, *edges, pieces, owners, "hub_blocks", 2)
+    came = lax.ppermute(sent, "dom", [(i, i ^ 1) for i in range(owners)])
+    hub_part = (kept.astype(F32) + came.astype(F32)).astype(BF)
+    hub_part, mirror = lax.optimization_barrier((hub_part, mirror))
+    hub = lax.all_to_all(
+        hub_part,
+        "dom",
+        split_axis=0,
+        concat_axis=0,
+        tiled=True,
+        axis_index_groups=[list(range(c, owners, 2)) for c in range(2)],
+    )
+
+    mixed, squares = mirror_final(
+        feat.reshape(1), mirror, mirror_master_rows.reshape(owners, TILE), self_weight, pieces
+    )
+    mixed, squares = hub_final(hub, mixed, squares)
+    line = squares.reshape(n_local // TILE, TILE)
     everyone = line
     for other in from_others(line, feat_size):
         everyone = everyone + other

time: 194 us -> 160 us (0.82)
  the two profiles are of different devices: /device:TPU:0 before, /device:TPU:10 now
where the time goes in v3:
time: 160 us; the launch traced here: 158 us
  Pallas kernels  89 us (56%)
  starting transfers between devices  41.3 us (26%)
  other arithmetic  10.6 us (7%)
  waiting for transfers between devices  6.16 us (4%)
  local copies, waits for them, and re-layouts  4.1 us (3%)
  matrix products  3.83 us (2%)
  between operations  2.75 us (2%)
    pallas_call x1, Pallas kernels, mix(): pl.pallas_call(functools.partial(mix_kernel, chunk=2048), out_shape=jax.S...  38.2 us
    pallas_call x2, Pallas kernels, blocks_call(): pl.pallas_call(functools.partial(blocks_kernel, group=group, owners=owner...  32.9 us
    all_to_all x1, starting transfers between devices, on_device(): lax.all_to_all(mirror_part, 'dom', split_axis=0, concat_axis=0, tiled=True)  19.9 us
    pallas_call x1, Pallas kernels, mirror_final(): pl.pallas_call(functools.partial(mirror_kernel, chunk=chunk, reach=n_loca...  15.8 us
    all_to_all x1, starting transfers between devices, on_device(): lax.all_to_all(hub_part, 'dom', split_axis=0, concat_axis=0, tiled=True,...  12.9 us
    ppermute x6, starting transfers between devices, from_others(): lax.ppermute(x, 'feat', [((i + shift) % size, i) for i in range(size)])  8.35 us
    ppermute x6, waiting for transfers between devices, from_others(): lax.ppermute(x, 'feat', [((i + shift) % size, i) for i in range(size)])  3.95 us
    dot_general x1, matrix products, on_device(): lhs = jnp.dot(one_hot, wide, preferred_element_type=F32)  3.83 us
  transfers between devices with their start and end apart: 9, of which 4 were waited for; matrix products, arithmetic and copies ran while one was open for 8% of the time, Pallas kernels for 42%

profile of v3, /device:TPU:10, one launch (start us, length us, event | category | flops | bytes accessed | tf_op | source)
XLA Modules:
  0.0 157.7 jit_solution(2105049100312297407)
XLA Ops:
  0.0 1.6 collective-permute-start.2
  1.6 0.9 collective-permute-start.1
  2.5 2.4 %collective-permute-start = (bf16[4096,128]{1,0:T(8,128)(2,1)}, bf16[4096,128]{1,0:T(8,128)(2,1)S(1)}, u32[]{:S(2)}, u32[]{:S(2)}) collective-permute-start(bf16[4096,128]{1,0:T(8,128)(2,1)} %x0_ref.1), channel_id=1, source_target_pairs={{1,0},{2,1},{3,2},{0,3},{5,4},{6,5},{7,6},{4,7},{9,8},{10,9},{11,1... | collective-permute-start | bytes 3145736 | tf_op jit(solution)/shard_map/ppermute | solution.py:400
  5.6 1.6 %fusion.17 = (s32[512]{0:T(512)S(1)}, s32[512]{0:T(512)S(1)}, s32[512]{0:T(512)S(1)}) fusion(s32[512,128]{1,0:T(8,128)} %refs_2_.3, s32[512,128]{1,0:T(8,128)} %refs_3_.3, s32[]{:T(128)} %bitcast.10), kind=kLoop, calls=%fused_computation.33 | loop fusion | flops 17920 | bytes 10244 | tf_op jit(solution)/shard_map/jit(_where)/select_n | solution.py:239
  7.2 0.1 convert_reduce_fusion.1
  7.3 0.8 slice_reduce_fusion.2
  10.1 0.8 broadcast_in_dim.90
  10.9 0.2 eq.88
  11.1 0.6 add_add_fusion.refs_1_
  11.7 3.8 %fusion.3.lhs_ref = bf16[2048,256]{1,0:T(8,128)(2,1)} fusion(s32[2048]{0:T(1024)S(1)} %eq.88, s32[256]{0:T(256)S(1)} %get-tuple-element.32, s32[256]{0:T(256)S(1)} %get-tuple-element.33, s32[2048]{0:T(1024)S(1)} %get-tuple-element.30, s32[2048]{0:T(1024)S(1)} %get-tuple-element.31, pred[2048]{0:T(1024)(128)(4,1)S(1)} %fusion.23, ...), kind=kOutput, calls=%fused_computation.4 | convolution fusion | flops 867917824 | bytes 1182720 | tf_op jit(solution)/shard_map/dot_general | solution.py:434
  15.5 38.2 %mix.1.refs_8_ = bf16[256,2,512,128]{3,2,1,0:T(8,128)(2,1)} custom-call(s32[1]{0:T(128)} %bitcast.4.feat_ref, bf16[2048,256]{1,0:T(8,128)(2,1)} %fusion.3.lhs_ref, bf16[64,512,128]{2,1,0:T(8,128)(2,1)} %bases_ref.1), custom_call_target="tpu_custom_call" | custom-call | tf_op jit(solution)/shard_map/mix/pallas_call | solution.py:59
  53.8 0.7 add_add_fusion.1.refs_1_
  54.4 0.1 select_reduce_fusion.2
  54.5 0.1 select_reduce_fusion.1
  54.6 0.3 convert_reduce_fusion
  54.9 0.8 select_reduce_fusion.refs_0_
  55.7 0.0 collective-permute-done.2.refs_7_.x3_ref
  55.7 0.0 copy-start
  55.7 0.0 collective-permute-done.1.refs_6_.x2_ref
  55.7 0.0 copy-start.1
  55.7 0.0 collective-permute-done.refs_5_.x1_ref
  55.7 1.0 copy-done
  56.7 0.4 copy-done.1
  57.1 0.0 copy-start.2
  57.1 1.0 copy-done.2
  58.1 20.9 %mirror_blocks.1 = bf16[32,144,128]{2,1,0:T(8,128)(2,1)} custom-call(s32[608]{0:T(1024)} %select_reduce_fusion.refs_0_, s32[3]{0:T(128)} %add_add_fusion.1.refs_1_, s32[512,128]{1,0:T(8,128)} %refs_2_.3, s32[512,128]{1,0:T(8,128)} %refs_3_.3, bf16[4096,128]{1,0:T(8,128)(2,1)} %x0_ref.1, bf16[4096,128]{1,0:T(8,128)(2,1)} %copy-done.2, ...), custom_call_target="tpu_custom_call" | custom-call | flops 17179869184 | bytes 67108864 | tf_op jit(solution)/shard_map/mirror_blocks/pallas_call | solution.py:208
  79.0 19.9 %all-to-all-start = ((bf16[32,144,128]{2,1,0:T(8,128)(2,1)}), bf16[32,144,128]{2,1,0:T(8,128)(2,1)S(1)}, u32[]{:S(2)}, u32[]{:S(2)}) async-start(bf16[32,144,128]{2,1,0:T(8,128)(2,1)} %mirror_blocks.1), calls=%async_computation | async-start | bytes 2359296 | tf_op jit(solution)/shard_map/all_to_all | solution.py:449
  98.9 12.1 %hub_blocks.1 = (bf16[16,144,128]{2,1,0:T(8,128)(2,1)}, bf16[16,144,128]{2,1,0:T(8,128)(2,1)}) custom-call(s32[608]{0:T(1024)} %select_reduce_fusion.refs_0_, s32[3]{0:T(128)} %add_add_fusion.refs_1_, s32[512,128]{1,0:T(8,128)} %refs_2_.3, s32[512,128]{1,0:T(8,128)} %refs_3_.3, bf16[4096,128]{1,0:T(8,128)(2,1)} %x0_ref.1, bf16[4096,128]{1,0:T(8,128)(2,1)} %copy-done.2, ...), custom_call_target="tpu_custom_call" | custom-call | flops 8589934592 | bytes 33554432 | tf_op jit(solution)/shard_map/hub_blocks/pallas_call | solution.py:208
  110.9 0.1 collective-permute-start.3
  111.0 2.2 %collective-permute-done.3 = bf16[16,144,128]{2,1,0:T(8,128)(2,1)S(1)} collective-permute-done((bf16[16,144,128]{2,1,0:T(8,128)(2,1)}, bf16[16,144,128]{2,1,0:T(8,128)(2,1)S(1)}, u32[]{:S(2)}, u32[]{:S(2)}) %collective-permute-start.3) | collective-permute-done | bytes 589856 | tf_op jit(solution)/shard_map/ppermute | solution.py:452
  113.2 2.1 %add_convert_fusion = bf16[16,144,128]{2,1,0:T(8,128)(2,1)} fusion(bf16[16,144,128]{2,1,0:T(8,128)(2,1)S(1)} %collective-permute-done.3, bf16[16,144,128]{2,1,0:T(8,128)(2,1)} %get-tuple-element.15), kind=kLoop, calls=%fused_computation.9 | loop fusion | flops 1179648 | bytes 1769472 | tf_op jit(solution)/shard_map/convert_element_type | solution.py:453
  115.3 0.0 all-to-all-done.mirror_ref
  115.3 12.9 %all-to-all-start.1 = ((bf16[16,144,128]{2,1,0:T(8,128)(2,1)}), bf16[16,144,128]{2,1,0:T(8,128)(2,1)S(1)}, u32[]{:S(2)}, u32[]{:S(2)}) async-start(bf16[16,144,128]{2,1,0:T(8,128)(2,1)} %add_convert_fusion), calls=%async_computation.1 | async-start | bytes 1179648 | tf_op jit(solution)/shard_map/all_to_all | solution.py:455
  128.2 0.0 copy-done.4
  128.3 15.8 %mirror_final.1 = (f32[4096,128]{1,0:T(8,128)}, f32[8,4,128]{2,1,0:T(4,128)}) custom-call(s32[1]{0:T(128)} %bitcast.4.feat_ref, bf16[32,144,128]{2,1,0:T(8,128)(2,1)} %copy-done.4, s32[32,128]{1,0:T(8,128)} %bitcast.16, bf16[512,128]{1,0:T(8,128)(2,1)} %self_ref.1, bf16[4096,128]{1,0:T(8,128)(2,1)} %x0_ref.1, bf16[4096,128]{1,0:T(8,128)(2,1)} %copy-done.2, ...), custom_call_target="tpu_custom_call" | custom-call | flops 8589934592 | bytes 8388608 | tf_op jit(solution)/shard_map/mirror_final/pallas_call | solution.py:340
  144.1 0.0 all-to-all-done.1.hub_ref
  144.1 0.0 copy-start.3
  144.1 0.8 copy-done.3
  144.9 2.0 %hub_final.1 = (f32[4096,128]{1,0:T(8,128)}, f32[8,4,128]{2,1,0:T(4,128)}) custom-call(bf16[16,144,128]{2,1,0:T(8,128)(2,1)} %copy-done.3, f32[4096,128]{1,0:T(8,128)} %get-tuple-element.19.mixed_ref, f32[8,4,128]{2,1,0:T(4,128)} %get-tuple-element.20.squares_ref), custom_call_target="tpu_custom_call", output_to_operand_aliasing={{0}: (1, {}), {1}: (2, {})} | custom-call | tf_op jit(solution)/shard_map/hub_final/pallas_call | solution.py:384
  146.9 0.0 collective-permute-start.6
  146.9 3.4 %collective-permute-start.5 = (f32[32,128]{1,0:T(8,128)}, f32[32,128]{1,0:T(8,128)S(1)}, u32[]{:S(2)}, u32[]{:S(2)}) collective-permute-start(f32[32,128]{1,0:T(8,128)} %bitcast.13), channel_id=1, source_target_pairs={{2,0},{3,1},{0,2},{1,3},{6,4},{7,5},{4,6},{5,7},{10,8},{11,9},{8,1... | collective-permute-start | bytes 49160 | tf_op jit(solution)/shard_map/ppermute | solution.py:400
  150.3 0.0 collective-permute-start.4
  150.3 0.5 collective-permute-done.6
  150.9 1.6 %collective-permute-done.5 = f32[32,128]{1,0:T(8,128)S(1)} collective-permute-done((f32[32,128]{1,0:T(8,128)}, f32[32,128]{1,0:T(8,128)S(1)}, u32[]{:S(2)}, u32[]{:S(2)}) %collective-permute-start.5) | collective-permute-done | bytes 16416 | tf_op jit(solution)/shard_map/ppermute | solution.py:400
  152.5 1.8 %collective-permute-done.4 = f32[32,128]{1,0:T(8,128)S(1)} collective-permute-done((f32[32,128]{1,0:T(8,128)}, f32[32,128]{1,0:T(8,128)S(1)}, u32[]{:S(2)}, u32[]{:S(2)}) %collective-permute-start.4) | collective-permute-done | bytes 16416 | tf_op jit(solution)/shard_map/ppermute | solution.py:400
  154.3 0.7 rsqrt_bitcast_fusion
  155.0 0.0 copy-done.5
  155.0 2.7 %multiply_convert_fusion = bf16[4096,128]{1,0:T(8,128)(2,1)} fusion(f32[4096,128]{1,0:T(8,128)} %get-tuple-element.21, f32[128]{0:T(128)S(1)} %copy-done.5, f32[4096]{0:T(1024)S(1)} %rsqrt_bitcast_fusion), kind=kLoop, calls=%fused_computation.5 | loop fusion | flops 1572864 | bytes 3162624 | tf_op jit(solution)/shard_map/convert_element_type | solution.py:473
  (10 shorter events, 0.1 us)
Async XLA Ops:
  0.0 55.7 %collective-permute-start.2 = (bf16[4096,128]{1,0:T(8,128)(2,1)}, bf16[4096,128]{1,0:T(8,128)(2,1)S(1)}, u32[]{:S(2)}, u32[]{:S(2)}) collective-permute-start(bf16[4096,128]{1,0:T(8,128)(2,1)} %x0_ref.1), channel_id=1, source_target_pairs={{3,0},{0,1},{1,2},{2,3},{7,4},{4,5},{5,6},{6,7},{11,8},{8,9},{9,10... | collective-permute-start | bytes 3145736 | tf_op jit(solution)/shard_map/ppermute | solution.py:400
  1.6 54.1 %collective-permute-start.1 = (bf16[4096,128]{1,0:T(8,128)(2,1)}, bf16[4096,128]{1,0:T(8,128)(2,1)S(1)}, u32[]{:S(2)}, u32[]{:S(2)}) collective-permute-start(bf16[4096,128]{1,0:T(8,128)(2,1)} %x0_ref.1), channel_id=1, source_target_pairs={{2,0},{3,1},{0,2},{1,3},{6,4},{7,5},{4,6},{5,7},{10,8},{11,9},{8,1... | collective-permute-start | bytes 3145736 | tf_op jit(solution)/shard_map/ppermute | solution.py:400
  2.5 53.2 %collective-permute-start = (bf16[4096,128]{1,0:T(8,128)(2,1)}, bf16[4096,128]{1,0:T(8,128)(2,1)S(1)}, u32[]{:S(2)}, u32[]{:S(2)}) collective-permute-start(bf16[4096,128]{1,0:T(8,128)(2,1)} %x0_ref.1), channel_id=1, source_target_pairs={{1,0},{2,1},{3,2},{0,3},{5,4},{6,5},{7,6},{4,7},{9,8},{10,9},{11,1... | collective-permute-start | bytes 3145736 | tf_op jit(solution)/shard_map/ppermute | solution.py:400
  55.7 1.0 copy-start
  55.7 1.4 copy-start.1
  57.1 1.0 copy-start.2
  79.0 36.3 %all-to-all-start = ((bf16[32,144,128]{2,1,0:T(8,128)(2,1)}), bf16[32,144,128]{2,1,0:T(8,128)(2,1)S(1)}, u32[]{:S(2)}, u32[]{:S(2)}) async-start(bf16[32,144,128]{2,1,0:T(8,128)(2,1)} %mirror_blocks.1), calls=%async_computation | async-start | bytes 2359296 | tf_op jit(solution)/shard_map/all_to_all | solution.py:449
  110.9 2.3 %collective-permute-start.3 = (bf16[16,144,128]{2,1,0:T(8,128)(2,1)}, bf16[16,144,128]{2,1,0:T(8,128)(2,1)S(1)}, u32[]{:S(2)}, u32[]{:S(2)}) collective-permute-start(bf16[16,144,128]{2,1,0:T(8,128)(2,1)} %get-tuple-element.16), channel_id=1, source_target_pairs={{0,4},{4,0},{8,12},{12,8},{16,20},{20,16},{24,28},{28,24},{32,36},... | collective-permute-start | bytes 1769480 | tf_op jit(solution)/shard_map/ppermute | solution.py:452
  115.3 13.0 %copy-start.4 = (bf16[32,144,128]{2,1,0:T(8,128)(2,1)}, bf16[32,144,128]{2,1,0:T(8,128)(2,1)S(1)}, u32[]{:S(2)}) copy-start(bf16[32,144,128]{2,1,0:T(8,128)(2,1)S(1)} %all-to-all-done.mirror_ref) | copy-start | bytes 3538948
  115.3 28.8 %all-to-all-start.1 = ((bf16[16,144,128]{2,1,0:T(8,128)(2,1)}), bf16[16,144,128]{2,1,0:T(8,128)(2,1)S(1)}, u32[]{:S(2)}, u32[]{:S(2)}) async-start(bf16[16,144,128]{2,1,0:T(8,128)(2,1)} %add_convert_fusion), calls=%async_computation.1 | async-start | bytes 1179648 | tf_op jit(solution)/shard_map/all_to_all | solution.py:455
  144.1 10.9 %copy-start.5 = (f32[128]{0:T(128)S(1)}, f32[128]{0:T(128)}, u32[]{:S(2)}) copy-start(f32[128]{0:T(128)} %param.14) | copy-start | bytes 1540
  144.1 0.8 copy-start.3
  146.9 3.9 %collective-permute-start.6 = (f32[32,128]{1,0:T(8,128)}, f32[32,128]{1,0:T(8,128)S(1)}, u32[]{:S(2)}, u32[]{:S(2)}) collective-permute-start(f32[32,128]{1,0:T(8,128)} %bitcast.12), channel_id=1, source_target_pairs={{3,0},{0,1},{1,2},{2,3},{7,4},{4,5},{5,6},{6,7},{11,8},{8,9},{9,10... | collective-permute-start | bytes 49160 | tf_op jit(solution)/shard_map/ppermute | solution.py:400
  146.9 5.6 %collective-permute-start.5 = (f32[32,128]{1,0:T(8,128)}, f32[32,128]{1,0:T(8,128)S(1)}, u32[]{:S(2)}, u32[]{:S(2)}) collective-permute-start(f32[32,128]{1,0:T(8,128)} %bitcast.13), channel_id=1, source_target_pairs={{2,0},{3,1},{0,2},{1,3},{6,4},{7,5},{4,6},{5,7},{10,8},{11,9},{8,1... | collective-permute-start | bytes 49160 | tf_op jit(solution)/shard_map/ppermute | solution.py:400
  150.3 3.9 %collective-permute-start.4 = (f32[32,128]{1,0:T(8,128)}, f32[32,128]{1,0:T(8,128)S(1)}, u32[]{:S(2)}, u32[]{:S(2)}) collective-permute-start(f32[32,128]{1,0:T(8,128)} %bitcast.14), channel_id=1, source_target_pairs={{1,0},{2,1},{3,2},{0,3},{5,4},{6,5},{7,6},{4,7},{9,8},{10,9},{11,1... | collective-permute-start | bytes 49160 | tf_op jit(solution)/shard_map/ppermute | solution.py:400

commit v4 on v3

--- a/solution.py
+++ b/solution.py
@@ -14,63 +14,155 @@
 VMEM_LIMIT = 56 * 1024 * 1024
 BF = jnp.bfloat16
 F32 = jnp.float32
-
-
-def mix_kernel(feat_ref, lhs_ref, bases_ref, w_ref, spread, *, chunk):
+HOT = jnp.float8_e4m3fn
+
+
+def prepare_kernel(
+    live_ref, src_ref, dst_ref, rel_ref, coef_ref, words_ref, lhs_ref, spread, *, owners, src_tiles, group
+):
+    blocks = src_ref.shape[0]
+    relations, n_bases = coef_ref.shape
+    live = live_ref[0]
+    src_tile = src_ref[:, :1] >> 7
+    dst_tile = dst_ref[:, :1] >> 7
+    index = lax.broadcasted_iota(jnp.int32, (blocks, 1), 0)
+    active = index < live
+    key = jnp.where(dst_tile < owners, src_tiles, 0) + src_tile
+    key = jnp.where(active, key, TILE - 1)
+    key_wide = jnp.broadcast_to(key, (blocks, TILE))
+    key_row = key_wide.astype(F32).T[:1, :]
+    lane = lax.broadcasted_iota(jnp.int32, (1, TILE), 1)
+    same_key = key_wide == lane
+    count = jnp.sum(same_key.astype(F32), axis=0, keepdims=True)
+    count = jnp.where(lane < 2 * src_tiles, count, 0.0).astype(jnp.int32)
+    pairs = (count + 1) >> 1
+    earlier = lax.broadcasted_iota(jnp.int32, (TILE, TILE), 0) < lax.broadcasted_iota(
+        jnp.int32, (TILE, TILE), 1
+    )
+    pairs_wide = jnp.broadcast_to(pairs, (8, TILE)).astype(F32).astype(BF)
+    start = jnp.dot(
+        pairs_wide, jnp.where(earlier, 1.0, 0.0).astype(BF), preferred_element_type=F32
+    )[:1].astype(jnp.int32)
+    zero = jnp.zeros_like(pairs)
+    mirror_pairs = jnp.sum(
+        jnp.where(lane < src_tiles, pairs, zero).astype(F32), axis=1, keepdims=True
+    ).astype(jnp.int32)
+    hub_pairs = jnp.sum(
+        jnp.where(lane >= src_tiles, pairs, zero).astype(F32), axis=1, keepdims=True
+    ).astype(jnp.int32)
+    shift = group.bit_length() - 1
+    mirror_groups = (mirror_pairs + group - 1) >> shift
+    hub_groups = (hub_pairs + group - 1) >> shift
+    start = start + jnp.where(lane >= src_tiles, mirror_groups * group - mirror_pairs, 0)
+    other = lax.broadcasted_iota(jnp.int32, (1, blocks), 1)
+    before = (key.astype(F32) == key_row) & (other < index)
+    rank = jnp.sum(before.astype(F32), axis=1, keepdims=True).astype(jnp.int32)
+    first = jnp.sum(
+        jnp.where(same_key, start, 0).astype(F32), axis=1, keepdims=True
+    ).astype(jnp.int32)
+    place = jnp.where(active, 2 * first + rank, -1)
+    word = index | (src_tile << 9) | (dst_tile << 14) | (1 << 20)
+    slots = words_ref.shape[1] - TILE
+    slot = lax.broadcasted_iota(jnp.int32, (1, slots), 1)
+    words_ref[:, :slots] = jnp.sum(jnp.where(place == slot, word, 0), axis=0, keepdims=True)
+    words_ref[:, slots:] = jnp.where(
+        lane == 0, mirror_groups, jnp.where(lane == 1, mirror_groups + hub_groups, 0)
+    )
+
+    rel_wide = jnp.broadcast_to(rel_ref[...].astype(F32), (TILE, blocks)).T[:, :1]
+    relation = rel_wide.astype(jnp.int32)
+    span = lax.broadcasted_iota(jnp.int32, (1, relations), 1)
+    one_hot = jnp.where(relation == span, 1.0, 0.0).astype(BF)
+    mixing = jnp.dot(one_hot, coef_ref[...], preferred_element_type=F32)
+    copies = lhs_ref.shape[1] // n_bases
+    blank = jnp.zeros_like(mixing)
+    for i in range(copies):
+        row = jnp.concatenate([mixing if k == i else blank for k in range(copies)], axis=1)
+        for half in range(copies * n_bases // TILE):
+            spread[half, pl.ds(i, blocks, stride=copies), :] = row[:, half * TILE : (half + 1) * TILE]
+    for half in range(copies * n_bases // TILE):
+        lhs_ref[:, half * TILE : (half + 1) * TILE] = spread[half].astype(BF)
+
+
+def prepare(live, edge_src, edge_dst, block_rel, basis_coef, owners, src_tiles, group):
+    blocks = edge_src.shape[0]
+    n_bases = basis_coef.shape[1]
+    slots = 2 * group * (-(-(blocks + 2 * src_tiles) // (2 * group)) + 1)
+    slots = -(-slots // TILE) * TILE
+    vmem = pl.BlockSpec(memory_space=pltpu.VMEM)
+    return pl.pallas_call(
+        functools.partial(prepare_kernel, owners=owners, src_tiles=src_tiles, group=group),
+        out_shape=(
+            jax.ShapeDtypeStruct((1, slots + TILE), jnp.int32),
+            jax.ShapeDtypeStruct((4 * blocks, 4 * n_bases), BF),
+        ),
+        in_specs=[pl.BlockSpec(memory_space=pltpu.SMEM)] + [vmem] * 4,
+        out_specs=(vmem, vmem),
+        scratch_shapes=[pltpu.VMEM((4 * n_bases // TILE, 4 * blocks, TILE), F32)],
+        compiler_params=pltpu.CompilerParams(vmem_limit_bytes=VMEM_LIMIT),
+        name="prepare",
+    )(live, edge_src, edge_dst, block_rel.reshape(1, blocks), basis_coef)
+
+
+def mix_kernel(feat_ref, lhs_ref, bases_ref, w_ref, spread, rights, *, chunk):
     n_bases, depth, cols = bases_ref.shape
+    side = pl.program_id(0) & 1
     spread[...] = bases_ref[...].astype(F32).reshape(n_bases * depth, cols)
-
-    def rows_of(d):
-        return spread[pl.ds(d, n_bases, stride=depth), :].astype(BF)
-
-    rights = []
-    for octet in range(depth // 8):
-        halves = []
-        for half in range(2):
-            first = octet * 8 + half * 4
-            halves.append(jnp.concatenate([rows_of(first + i) for i in range(4)], axis=0))
-        rights.append(jnp.concatenate(halves, axis=1))
+    for d in range(depth):
+        octet, half, row = d // 8, d % 8 // 4, d % 4
+        rows = slice(row * n_bases, (row + 1) * n_bases)
+        rights[side, octet, rows, half * cols : (half + 1) * cols] = spread[
+            pl.ds(d, n_bases, stride=depth), :
+        ].astype(BF)
     pairs = chunk // 8
     low = lax.broadcasted_iota(jnp.int32, (pairs, 8, cols), 1) < 4
-
-    def body(step, carry):
-        row = pl.multiple_of(step * chunk, chunk)
-        left = lhs_ref[pl.ds(row, chunk), :]
-        evens, odds = [], []
-        for right in rights:
-            out = jnp.dot(left, right, preferred_element_type=F32)
-            first = out[:, :cols].reshape(pairs, 8, cols)
-            second = out[:, cols:].reshape(pairs, 8, cols)
-            evens.append(jnp.where(low, first, pltpu.roll(second, 4, 1)))
-            odds.append(jnp.where(low, pltpu.roll(first, 4, 1), second))
-        pair = step * pairs
-        w_ref[pl.ds(pair, pairs), 0] = jnp.concatenate(evens, axis=1).astype(BF)
-        w_ref[pl.ds(pair, pairs), 1] = jnp.concatenate(odds, axis=1).astype(BF)
-        return carry
-
-    lax.fori_loop(0, lhs_ref.shape[0] // chunk, body, 0)
+    for row in range(0, lhs_ref.shape[0], chunk):
+        left = lhs_ref[row : row + chunk, :]
+        pair = row // 8
+        for first_octet in range(0, depth // 8, 2):
+            evens, odds = [], []
+            for octet in (first_octet, first_octet + 1):
+                out = jnp.dot(left, rights[1 - side, octet], preferred_element_type=F32)
+                first = out[:, :cols].reshape(pairs, 8, cols)
+                second = out[:, cols:].reshape(pairs, 8, cols)
+                evens.append(jnp.where(low, first, pltpu.roll(second, 4, 1)))
+                odds.append(jnp.where(low, pltpu.roll(first, 4, 1), second))
+            at = slice(first_octet * 8, first_octet * 8 + 16)
+            w_ref[pair : pair + pairs, 0, at] = jnp.concatenate(evens, axis=1).astype(BF)
+            w_ref[pair : pair + pairs, 1, at] = jnp.concatenate(odds, axis=1).astype(BF)
 
 
 def mix(feat, lhs, bases, blocks):
     n_bases, model_dim, cols = bases.shape
-    depth = 16
+    depth = 32
     steps = model_dim // depth
     per_part = cols // depth
+
+    def bases_at(i, f):
+        return (0, lax.rem(jnp.minimum(i, steps - 1) + f[0] * per_part, steps), 0)
+
     return pl.pallas_call(
-        functools.partial(mix_kernel, chunk=2048),
+        functools.partial(mix_kernel, chunk=512),
         out_shape=jax.ShapeDtypeStruct((blocks // 2, 2, model_dim, cols), BF),
         grid_spec=pltpu.PrefetchScalarGridSpec(
             num_scalar_prefetch=1,
-            grid=(steps,),
+            grid=(steps + 1,),
             in_specs=[
                 pl.BlockSpec(lhs.shape, lambda i, f: (0, 0)),
-                pl.BlockSpec(
-                    (n_bases, depth, cols),
-                    lambda i, f: (0, lax.rem(i + f[0] * per_part, steps), 0),
-                ),
+                pl.BlockSpec((n_bases, depth, cols), bases_at),
             ],
-            out_specs=pl.BlockSpec((blocks // 2, 2, depth, cols), lambda i, f: (0, 0, i, 0)),
-            scratch_shapes=[pltpu.VMEM((n_bases * depth, cols), F32)],
+            out_specs=pl.BlockSpec(
+                (blocks // 2, 2, depth, cols), lambda i, f: (0, 0, jnp.maximum(i - 1, 0), 0)
+            ),
+            scratch_shapes=[
+                pltpu.VMEM((n_bases * depth, cols), F32),
+                pltpu.VMEM((2, depth // 8, 4 * n_bases, 2 * cols), BF),
+            ],
+        ),
+        cost_estimate=pl.CostEstimate(
+            flops=8 * blocks * n_bases * model_dim * cols,
+            bytes_accessed=blocks * model_dim * cols * 2,
+            transcendentals=0,
         ),
         compiler_params=pltpu.CompilerParams(vmem_limit_bytes=VMEM_LIMIT),
         name="mix",
@@ -81,17 +173,18 @@
     return word & 511, (word >> 9) & 31, (word >> 14) & 63, word >> 20
 
 
-def blocks_kernel(*refs, group, owners, split, n_out):
-    word_ref, span_ref, src_hbm, dst_hbm = refs[:4]
-    piece_refs, w_ref = refs[4:8], refs[8]
-    out_refs = refs[9 : 9 + n_out]
-    acc, deg, held, src_ref, dst_ref, table, sems = refs[9 + n_out :]
-    first_group, end_group = span_ref[0], span_ref[1]
+def blocks_kernel(*refs, group, owners, split, hubs):
+    word_ref, src_ref, dst_ref = refs[:3]
+    piece_refs, w_ref, out_ref = refs[3:7], refs[7], refs[8]
+    acc, deg, held, table, sems = refs[9:]
+    spans = word_ref.shape[1] - TILE
+    first_group = word_ref[0, spans] if hubs else 0
+    end_group = word_ref[0, spans + int(hubs)]
 
     def fetch(at):
         side = at & 1
         for k in range(2 * group):
-            block = word_ref[at * (2 * group) + k] & 511
+            block = word_ref[0, at * (2 * group) + k] & 511
             pltpu.make_async_copy(
                 w_ref.at[block >> 1, block & 1], held.at[side, k // 2, k % 2], sems.at[side]
             ).start()
@@ -101,13 +194,10 @@
         fetch(first_group)
 
     cols = table.shape[1] // len(piece_refs)
-    loads = [
-        pltpu.make_async_copy(src_hbm, src_ref, sems.at[2]),
-        pltpu.make_async_copy(dst_hbm, dst_ref, sems.at[3]),
-    ]
+    loads = []
     for p, piece in enumerate(piece_refs):
         here = table.at[:, p * cols : (p + 1) * cols]
-        loads.append(pltpu.make_async_copy(piece, here, sems.at[4 + p]))
+        loads.append(pltpu.make_async_copy(piece, here, sems.at[2 + p]))
     for load in loads:
         load.start()
     acc[...] = jnp.zeros_like(acc)
@@ -134,7 +224,7 @@
             return jnp.concatenate([top, bottom], axis=0)
 
         def fields(pair, k):
-            return unpack(word_ref[(here * group + pair) * 2 + k])
+            return unpack(word_ref[0, (here * group + pair) * 2 + k])
 
         def adjacency(pair):
             dst_hot, src_hot, count = [], [], None
@@ -149,8 +239,8 @@
                 extra = jnp.where(lane == lax.rem(dst_tile, owners), column, 0.0)
                 count = extra if count is None else count + extra
             found = lax.dot_general(
-                jnp.concatenate(dst_hot, axis=1),
-                diagonal(src_hot[0], src_hot[1]),
+                jnp.concatenate(dst_hot, axis=1).astype(HOT),
+                diagonal(src_hot[0], src_hot[1]).astype(HOT),
                 (((1,), (1,)), ((), ())),
                 preferred_element_type=F32,
             )
@@ -184,78 +274,40 @@
 
     deg[...] = deg[...].T
     line = lax.broadcasted_iota(jnp.int32, (DEG_ROWS, TILE), 0)
-    core = span_ref[2]
-    for part, out_ref in enumerate(out_refs):
-        for i in range(owners // n_out):
-            at = i if n_out == 1 else 2 * i + (core ^ part)
-            degree = deg[pl.ds(at, 1), :]
-            high = jnp.floor(degree * (1.0 / 256.0)) * 256.0
-            low = degree - high
-            out_ref[i, :TILE, :] = acc[at].astype(BF)
-            rows = jnp.where(line == 0, high, jnp.where(line == 1, low, 0.0))
-            out_ref[i, TILE:, :] = rows.astype(BF)
-
-
-def blocks_call(
-    words, span, weights, edge_src, edge_dst, pieces, owners, name, n_out, group=16, split=16
-):
-    _, _, model_dim, cols = weights.shape
+    for at in range(owners):
+        degree = deg[at : at + 1, :]
+        high = jnp.floor(degree * (1.0 / 256.0)) * 256.0
+        low = degree - high
+        out_ref[at, :TILE, :] = acc[at].astype(BF)
+        rows = jnp.where(line == 0, high, jnp.where(line == 1, low, 0.0))
+        out_ref[at, TILE:, :] = rows.astype(BF)
+
+
+def blocks_call(words, weights, edge_src, edge_dst, pieces, owners, hubs, group=16, split=16):
+    pair_count, _, model_dim, cols = weights.shape
     vmem = pl.BlockSpec(memory_space=pltpu.VMEM)
     smem = pl.BlockSpec(memory_space=pltpu.SMEM)
     anywhere = pl.BlockSpec(memory_space=pl.ANY)
-    out = jax.ShapeDtypeStruct((owners // n_out, TILE + DEG_ROWS, cols), BF)
-    pairs = 512 // 2 // n_out
     return pl.pallas_call(
-        functools.partial(blocks_kernel, group=group, owners=owners, split=split, n_out=n_out),
-        out_shape=(out,) * n_out,
-        in_specs=[smem, smem] + [anywhere] * (3 + len(pieces)),
-        out_specs=(vmem,) * n_out,
+        functools.partial(blocks_kernel, group=group, owners=owners, split=split, hubs=hubs),
+        out_shape=jax.ShapeDtypeStruct((owners, TILE + DEG_ROWS, cols), BF),
+        in_specs=[smem, vmem, vmem] + [anywhere] * (1 + len(pieces)),
+        out_specs=vmem,
         scratch_shapes=[
             pltpu.VMEM((owners, TILE, cols), F32),
             pltpu.VMEM((TILE, TILE), F32),
             pltpu.VMEM((2, group, 2, model_dim, cols), BF),
-            pltpu.VMEM(edge_src.shape, jnp.int32),
-            pltpu.VMEM(edge_dst.shape, jnp.int32),
             pltpu.VMEM((pieces[0].shape[0], model_dim), BF),
-            pltpu.SemaphoreType.DMA((4 + len(pieces),)),
+            pltpu.SemaphoreType.DMA((2 + len(pieces),)),
         ],
         cost_estimate=pl.CostEstimate(
-            flops=pairs * 2 * TILE * model_dim * cols * 4,
-            bytes_accessed=pairs * 2 * model_dim * cols * 2,
+            flops=pair_count * 4 * TILE * model_dim * cols,
+            bytes_accessed=pair_count * model_dim * cols * 2,
             transcendentals=0,
         ),
         compiler_params=pltpu.CompilerParams(vmem_limit_bytes=VMEM_LIMIT),
-        name=name,
-    )(words, span, edge_src, edge_dst, *pieces, weights)
-
-
-def arrange(src_tile, dst_tile, live, core, owners, src_tiles, group):
-    blocks = src_tile.shape[0]
-    keys = 2 * src_tiles
-    slots = 2 * group * (-(-(blocks + keys) // (2 * group)) + 1)
-    index = jnp.arange(blocks, dtype=jnp.int32)
-    key_range = jnp.arange(keys, dtype=jnp.int32)
-    active = index < live
-    key = jnp.where(active, jnp.where(dst_tile < owners, src_tiles, 0) + src_tile, keys)
-    count = jnp.sum((key[None, :] == key_range[:, None]).astype(jnp.int32), axis=1)
-    pairs = (count + 1) >> 1
-    start = jnp.sum(jnp.where(key_range[None, :] < key_range[:, None], pairs[None, :], 0), axis=1)
-    mirror_pairs = jnp.sum(pairs[:src_tiles])
-    hub_pairs = jnp.sum(pairs[src_tiles:])
-    mirror_groups = (mirror_pairs + group - 1) // group
-    hub_groups = (hub_pairs + group - 1) // group
-    start = start + jnp.where(key_range >= src_tiles, mirror_groups * group - mirror_pairs, 0)
-    before = (key[None, :] == key[:, None]) & (index[None, :] < index[:, None])
-    rank = jnp.sum(before.astype(jnp.int32), axis=1)
-    place = jnp.sum(jnp.where(key[:, None] == key_range[None, :], start[None, :], 0), axis=1)
-    place = jnp.where(active, 2 * place + rank, -1)
-    word = index | (src_tile << 9) | (dst_tile << 14) | (1 << 20)
-    slot = jnp.arange(slots, dtype=jnp.int32)
-    words = jnp.sum(jnp.where(place[None, :] == slot[:, None], word[None, :], 0), axis=1)
-    zero = jnp.zeros((), jnp.int32)
-    mirror_span = jnp.stack([zero, mirror_groups, core])
-    hub_span = jnp.stack([mirror_groups, mirror_groups + hub_groups, core])
-    return words, mirror_span, hub_span
+        name="hub_blocks" if hubs else "mirror_blocks",
+    )(words, edge_src, edge_dst, *pieces, weights)
 
 
 def square_lines(value):
@@ -335,7 +387,7 @@
 def mirror_final(feat, mirror, master, self_weight, pieces):
     n_local, cols = pieces[0].shape
     owners = mirror.shape[0]
-    chunk = 512
+    chunk = 1024
     whole = lambda shape: pl.BlockSpec(shape, lambda i, *_: (0,) * len(shape))
     return pl.pallas_call(
         functools.partial(mirror_kernel, chunk=chunk, reach=n_local - n_local // 4),
@@ -419,47 +471,19 @@
     feat = lax.axis_index("feat").astype(jnp.int32)
     blocks = edge_src.shape[0]
     n_local, cols = embeddings.shape
-    n_bases, model_dim, _ = bases.shape
-    relations = basis_coef.shape[0]
-
+    model_dim = bases.shape[1]
     pieces = [embeddings] + from_others(embeddings, feat_size)
-
-    src_tile = edge_src[:, 0] // TILE
-    dst_tile = edge_dst[:, 0] // TILE
-
-    spread = 4
-    relation = jnp.repeat(block_rel, spread)
-    one_hot = (relation[:, None] == jnp.arange(relations)[None, :]).astype(BF)
-    wide = jnp.concatenate([basis_coef] * spread, axis=1)
-    lhs = jnp.dot(one_hot, wide, preferred_element_type=F32)
-    line = lax.broadcasted_iota(jnp.int32, lhs.shape, 0) % spread
-    group = lax.broadcasted_iota(jnp.int32, lhs.shape, 1) // n_bases
-    lhs = jnp.where(line == group, lhs, 0.0).astype(BF)
-
-    group_size = 16
-    device = lax.axis_index("dom").astype(jnp.int32)
-    words, mirror_span, hub_span = arrange(
-        src_tile, dst_tile, block_count[0], device & 1, owners, n_local // TILE, group_size
+    words, lhs = prepare(
+        block_count, edge_src, edge_dst, block_rel, basis_coef, owners, n_local // TILE, 16
     )
     weights = mix(feat.reshape(1), lhs, bases, blocks)
     edges = (edge_src, edge_dst)
-    (mirror_part,) = blocks_call(
-        words, mirror_span, weights, *edges, pieces, owners, "mirror_blocks", 1
-    )
+    mirror_part = blocks_call(words, weights, *edges, pieces, owners, False)
     mirror = lax.all_to_all(mirror_part, "dom", split_axis=0, concat_axis=0, tiled=True)
     weights, _ = lax.optimization_barrier((weights, mirror_part))
-    kept, sent = blocks_call(words, hub_span, weights, *edges, pieces, owners, "hub_blocks", 2)
-    came = lax.ppermute(sent, "dom", [(i, i ^ 1) for i in range(owners)])
-    hub_part = (kept.astype(F32) + came.astype(F32)).astype(BF)
+    hub_part = blocks_call(words, weights, *edges, pieces, owners, True)
     hub_part, mirror = lax.optimization_barrier((hub_part, mirror))
-    hub = lax.all_to_all(
-        hub_part,
-        "dom",
-        split_axis=0,
-        concat_axis=0,
-        tiled=True,
-        axis_index_groups=[list(range(c, owners, 2)) for c in range(2)],
-    )
+    hub = lax.all_to_all(hub_part, "dom", split_axis=0, concat_axis=0, tiled=True)
 
     mixed, squares = mirror_final(
         feat.reshape(1), mirror, mirror_master_rows.reshape(owners, TILE), self_weight, pieces

time: 160 us -> 148 us (0.925)
  the two profiles are of different devices: /device:TPU:10 before, /device:TPU:0 now
where the time goes in v4:
time: 148 us; the launch traced here: 149 us
  Pallas kernels  91 us (61%)
  starting transfers between devices  34.6 us (23%)
  waiting for transfers between devices  15 us (10%)
  local copies, waits for them, and re-layouts  4.06 us (3%)
  other arithmetic  3.45 us (2%)
    pallas_call x1, Pallas kernels, mix(): pl.pallas_call(functools.partial(mix_kernel, chunk=512), out_shape=jax.Sh...  35.5 us
    pallas_call x2, Pallas kernels, blocks_call(): pl.pallas_call(functools.partial(blocks_kernel, group=group, owners=owner...  35.4 us
    all_to_all x1, starting transfers between devices, on_device(): lax.all_to_all(mirror_part, 'dom', split_axis=0, concat_axis=0, tiled=True)  16.5 us
    pallas_call x1, Pallas kernels, mirror_final(): pl.pallas_call(functools.partial(mirror_kernel, chunk=chunk, reach=n_loca...  14.1 us
    ppermute x6, starting transfers between devices, from_others(): lax.ppermute(x, 'feat', [((i + shift) % size, i) for i in range(size)])  11.4 us
    all_to_all x1, starting transfers between devices, on_device(): lax.all_to_all(hub_part, 'dom', split_axis=0, concat_axis=0, tiled=True)  6.72 us
    all_to_all x1, waiting for transfers between devices, on_device(): lax.all_to_all(mirror_part, 'dom', split_axis=0, concat_axis=0, tiled=True)  6.35 us
    ppermute x6, waiting for transfers between devices, from_others(): lax.ppermute(x, 'feat', [((i + shift) % size, i) for i in range(size)])  4.53 us
  transfers between devices with their start and end apart: 8, of which 4 were waited for; matrix products, arithmetic and copies ran while one was open for 1% of the time, Pallas kernels for 44%

profile of v4, /device:TPU:0, one launch (start us, length us, event | category | flops | bytes accessed | tf_op | source)
XLA Modules:
  0.0 148.8 jit_solution(10822736810123148335)
XLA Ops:
  0.0 1.7 %collective-permute-start.2 = (bf16[4096,128]{1,0:T(8,128)(2,1)}, bf16[4096,128]{1,0:T(8,128)(2,1)S(1)}, u32[]{:S(2)}, u32[]{:S(2)}) collective-permute-start(bf16[4096,128]{1,0:T(8,128)(2,1)} %x0_ref.1), channel_id=1, source_target_pairs={{3,0},{0,1},{1,2},{2,3},{7,4},{4,5},{5,6},{6,7},{11,8},{8,9},{9,10... | collective-permute-start | bytes 3145736 | tf_op jit(solution)/shard_map/ppermute | solution.py:452
  1.7 2.9 %collective-permute-start.1 = (bf16[4096,128]{1,0:T(8,128)(2,1)}, bf16[4096,128]{1,0:T(8,128)(2,1)S(1)}, u32[]{:S(2)}, u32[]{:S(2)}) collective-permute-start(bf16[4096,128]{1,0:T(8,128)(2,1)} %x0_ref.1), channel_id=1, source_target_pairs={{2,0},{3,1},{0,2},{1,3},{6,4},{7,5},{4,6},{5,7},{10,8},{11,9},{8,1... | collective-permute-start | bytes 3145736 | tf_op jit(solution)/shard_map/ppermute | solution.py:452
  4.6 1.3 collective-permute-start
  6.6 1.7 %copy.13.coef_ref = bf16[822,64]{1,0:T(8,128)(2,1)} copy(bf16[822,64]{0,1:T(8,128)(2,1)} %param.13) | data formatting | bytes 210432 | tf_op args[3]
  8.3 3.7 %prepare.1 = (s32[1,768]{1,0:T(1,128)}, bf16[2048,256]{1,0:T(8,128)(2,1)}) custom-call(s32[1]{0:T(128)S(6)} %copy.16.live_ref, s32[512,128]{1,0:T(8,128)} %refs_1_.3, s32[512,128]{1,0:T(8,128)} %refs_2_.3, s32[1,512]{1,0:T(1,128)} %bitcast.10, bf16[822,64]{1,0:T(8,128)(2,1)} %copy.13.coef_ref), custom_call_target="tpu_custom_call" | custom-call | tf_op jit(solution)/shard_map/prepare/pallas_call | solution.py:93
  12.0 35.5 %mix.1.refs_7_ = bf16[256,2,512,128]{3,2,1,0:T(8,128)(2,1)} custom-call(s32[1]{0:T(128)} %bitcast.1.feat_ref, bf16[2048,256]{1,0:T(8,128)(2,1)} %get-tuple-element.15.lhs_ref, bf16[64,512,128]{2,1,0:T(8,128)(2,1)} %bases_ref.1), custom_call_target="tpu_custom_call" | custom-call | flops 17179869184 | bytes 67108864 | tf_op jit(solution)/shard_map/mix/pallas_call | solution.py:144
  47.5 0.0 collective-permute-done.2.refs_6_.x3_ref
  47.5 0.0 copy-start.1
  47.5 2.6 %collective-permute-done.1.refs_5_.x2_ref = bf16[4096,128]{1,0:T(8,128)(2,1)S(1)} collective-permute-done((bf16[4096,128]{1,0:T(8,128)(2,1)}, bf16[4096,128]{1,0:T(8,128)(2,1)S(1)}, u32[]{:S(2)}, u32[]{:S(2)}) %collective-permute-start.1) | collective-permute-done | bytes 1048608 | tf_op jit(solution)/shard_map/ppermute | solution.py:452
  50.1 0.0 copy-start.2
  50.1 0.0 collective-permute-done.refs_4_.x1_ref
  50.1 0.0 copy-start.3
  50.1 0.0 copy-done.1
  50.1 0.9 copy-done.2
  51.1 0.4 copy-done.3
  51.4 23.4 %mirror_blocks.1 = bf16[32,144,128]{2,1,0:T(8,128)(2,1)} custom-call(s32[1,768]{1,0:T(1,128)} %get-tuple-element.14.refs_0_, s32[512,128]{1,0:T(8,128)} %refs_1_.3, s32[512,128]{1,0:T(8,128)} %refs_2_.3, bf16[4096,128]{1,0:T(8,128)(2,1)} %x0_ref.1, bf16[4096,128]{1,0:T(8,128)(2,1)} %copy-done.3, bf16[4096,128]{1,0:T(8,128)(2,1)} %copy-done.2, ...), custom_call_target="tpu_custom_call" | custom-call | flops 8589934592 | bytes 33554432 | tf_op jit(solution)/shard_map/mirror_blocks/pallas_call | solution.py:291
  74.9 16.5 %all-to-all-start = ((bf16[32,144,128]{2,1,0:T(8,128)(2,1)}), bf16[32,144,128]{2,1,0:T(8,128)(2,1)S(1)}, u32[]{:S(2)}, u32[]{:S(2)}) async-start(bf16[32,144,128]{2,1,0:T(8,128)(2,1)} %mirror_blocks.1), calls=%async_computation | async-start | bytes 2359296 | tf_op jit(solution)/shard_map/all_to_all | solution.py:482
  91.4 12.0 %hub_blocks.1 = bf16[32,144,128]{2,1,0:T(8,128)(2,1)} custom-call(s32[1,768]{1,0:T(1,128)} %get-tuple-element.14.refs_0_, s32[512,128]{1,0:T(8,128)} %refs_1_.3, s32[512,128]{1,0:T(8,128)} %refs_2_.3, bf16[4096,128]{1,0:T(8,128)(2,1)} %x0_ref.1, bf16[4096,128]{1,0:T(8,128)(2,1)} %copy-done.3, bf16[4096,128]{1,0:T(8,128)(2,1)} %copy-done.2, ...), custom_call_target="tpu_custom_call" | custom-call | flops 8589934592 | bytes 33554432 | tf_op jit(solution)/shard_map/hub_blocks/pallas_call | solution.py:291
  103.4 6.4 %all-to-all-done.mirror_ref = bf16[32,144,128]{2,1,0:T(8,128)(2,1)S(1)} async-done(((bf16[32,144,128]{2,1,0:T(8,128)(2,1)}), bf16[32,144,128]{2,1,0:T(8,128)(2,1)S(1)}, u32[]{:S(2)}, u32[]{:S(2)}) %all-to-all-start) | async-done | bytes 1179680 | tf_op jit(solution)/shard_map/all_to_all | solution.py:482
  109.8 0.0 copy-start.4
  109.8 6.7 %all-to-all-start.1 = ((bf16[32,144,128]{2,1,0:T(8,128)(2,1)}), bf16[32,144,128]{2,1,0:T(8,128)(2,1)S(1)}, u32[]{:S(2)}, u32[]{:S(2)}) async-start(bf16[32,144,128]{2,1,0:T(8,128)(2,1)} %hub_blocks.1), calls=%async_computation.1 | async-start | bytes 2359296 | tf_op jit(solution)/shard_map/all_to_all | solution.py:486
  116.5 0.0 copy-done.4
  116.5 14.1 %mirror_final.1 = (f32[4096,128]{1,0:T(8,128)}, f32[4,8,128]{2,1,0:T(8,128)}) custom-call(s32[1]{0:T(128)} %bitcast.1.feat_ref, bf16[32,144,128]{2,1,0:T(8,128)(2,1)} %copy-done.4, s32[32,128]{1,0:T(8,128)} %bitcast.11, bf16[512,128]{1,0:T(8,128)(2,1)} %self_ref.1, bf16[4096,128]{1,0:T(8,128)(2,1)} %x0_ref.1, bf16[4096,128]{1,0:T(8,128)(2,1)} %copy-done.3, ...), custom_call_target="tpu_custom_call" | custom-call | flops 8589934592 | bytes 8388608 | tf_op jit(solution)/shard_map/mirror_final/pallas_call | solution.py:392
  130.6 0.0 copy-start.5
  130.6 4.1 %all-to-all-done.1.hub_ref = bf16[32,144,128]{2,1,0:T(8,128)(2,1)S(1)} async-done(((bf16[32,144,128]{2,1,0:T(8,128)(2,1)}), bf16[32,144,128]{2,1,0:T(8,128)(2,1)S(1)}, u32[]{:S(2)}, u32[]{:S(2)}) %all-to-all-start.1) | async-done | bytes 1179680 | tf_op jit(solution)/shard_map/all_to_all | solution.py:486
  134.7 0.0 copy-start
  134.7 1.0 copy-done
  135.7 2.3 %hub_final.1 = (f32[4096,128]{1,0:T(8,128)}, f32[4,8,128]{2,1,0:T(8,128)}) custom-call(bf16[32,144,128]{2,1,0:T(8,128)(2,1)} %copy-done, f32[4096,128]{1,0:T(8,128)} %get-tuple-element.19.mixed_ref, f32[4,8,128]{2,1,0:T(8,128)} %get-tuple-element.20.squares_ref), custom_call_target="tpu_custom_call", output_to_operand_aliasing={{0}: (1, {}), {1}: (2, {})} | custom-call | tf_op jit(solution)/shard_map/hub_final/pallas_call | solution.py:436
  138.0 2.2 %collective-permute-start.4 = (f32[32,128]{1,0:T(8,128)}, f32[32,128]{1,0:T(8,128)S(1)}, u32[]{:S(2)}, u32[]{:S(2)}) collective-permute-start(f32[32,128]{1,0:T(8,128)} %bitcast.7), channel_id=1, source_target_pairs={{2,0},{3,1},{0,2},{1,3},{6,4},{7,5},{4,6},{5,7},{10,8},{11,9},{8,1... | collective-permute-start | bytes 49160 | tf_op jit(solution)/shard_map/ppermute | solution.py:452
  140.2 0.3 collective-permute-start.5
  140.5 2.9 %collective-permute-start.3 = (f32[32,128]{1,0:T(8,128)}, f32[32,128]{1,0:T(8,128)S(1)}, u32[]{:S(2)}, u32[]{:S(2)}) collective-permute-start(f32[32,128]{1,0:T(8,128)} %bitcast.9), channel_id=1, source_target_pairs={{1,0},{2,1},{3,2},{0,3},{5,4},{6,5},{7,6},{4,7},{9,8},{10,9},{11,1... | collective-permute-start | bytes 49160 | tf_op jit(solution)/shard_map/ppermute | solution.py:452
  143.4 0.0 collective-permute-done.4
  143.4 1.9 %collective-permute-done.5 = f32[32,128]{1,0:T(8,128)S(1)} collective-permute-done((f32[32,128]{1,0:T(8,128)}, f32[32,128]{1,0:T(8,128)S(1)}, u32[]{:S(2)}, u32[]{:S(2)}) %collective-permute-start.5) | collective-permute-done | bytes 16416 | tf_op jit(solution)/shard_map/ppermute | solution.py:452
  145.4 0.0 collective-permute-done.3
  145.4 0.7 rsqrt_bitcast_fusion
  146.1 0.0 copy-done.5
  146.1 2.7 %multiply_convert_fusion = bf16[4096,128]{1,0:T(8,128)(2,1)} fusion(f32[4096,128]{1,0:T(8,128)} %get-tuple-element.21, f32[128]{0:T(128)S(1)} %copy-done.5, f32[4096]{0:T(1024)S(1)} %rsqrt_bitcast_fusion), kind=kLoop, calls=%fused_computation | loop fusion | flops 1572864 | bytes 3162624 | tf_op jit(solution)/shard_map/convert_element_type | solution.py:497
Async XLA Ops:
  0.0 47.5 %collective-permute-start.2 = (bf16[4096,128]{1,0:T(8,128)(2,1)}, bf16[4096,128]{1,0:T(8,128)(2,1)S(1)}, u32[]{:S(2)}, u32[]{:S(2)}) collective-permute-start(bf16[4096,128]{1,0:T(8,128)(2,1)} %x0_ref.1), channel_id=1, source_target_pairs={{3,0},{0,1},{1,2},{2,3},{7,4},{4,5},{5,6},{6,7},{11,8},{8,9},{9,10... | collective-permute-start | bytes 3145736 | tf_op jit(solution)/shard_map/ppermute | solution.py:452
  1.7 48.5 %collective-permute-start.1 = (bf16[4096,128]{1,0:T(8,128)(2,1)}, bf16[4096,128]{1,0:T(8,128)(2,1)S(1)}, u32[]{:S(2)}, u32[]{:S(2)}) collective-permute-start(bf16[4096,128]{1,0:T(8,128)(2,1)} %x0_ref.1), channel_id=1, source_target_pairs={{2,0},{3,1},{0,2},{1,3},{6,4},{7,5},{4,6},{5,7},{10,8},{11,9},{8,1... | collective-permute-start | bytes 3145736 | tf_op jit(solution)/shard_map/ppermute | solution.py:452
  4.6 45.6 %collective-permute-start = (bf16[4096,128]{1,0:T(8,128)(2,1)}, bf16[4096,128]{1,0:T(8,128)(2,1)S(1)}, u32[]{:S(2)}, u32[]{:S(2)}) collective-permute-start(bf16[4096,128]{1,0:T(8,128)(2,1)} %x0_ref.1), channel_id=1, source_target_pairs={{1,0},{2,1},{3,2},{0,3},{5,4},{6,5},{7,6},{4,7},{9,8},{10,9},{11,1... | collective-permute-start | bytes 3145736 | tf_op jit(solution)/shard_map/ppermute | solution.py:452
  47.5 2.6 %copy-start.1 = (bf16[4096,128]{1,0:T(8,128)(2,1)}, bf16[4096,128]{1,0:T(8,128)(2,1)S(1)}, u32[]{:S(2)}) copy-start(bf16[4096,128]{1,0:T(8,128)(2,1)S(1)} %collective-permute-done.2.refs_6_.x3_ref) | copy-start | bytes 3145732
  50.1 1.0 copy-start.2
  50.1 1.3 copy-start.3
  74.9 34.9 %all-to-all-start = ((bf16[32,144,128]{2,1,0:T(8,128)(2,1)}), bf16[32,144,128]{2,1,0:T(8,128)(2,1)S(1)}, u32[]{:S(2)}, u32[]{:S(2)}) async-start(bf16[32,144,128]{2,1,0:T(8,128)(2,1)} %mirror_blocks.1), calls=%async_computation | async-start | bytes 2359296 | tf_op jit(solution)/shard_map/all_to_all | solution.py:482
  109.8 6.7 %copy-start.4 = (bf16[32,144,128]{2,1,0:T(8,128)(2,1)}, bf16[32,144,128]{2,1,0:T(8,128)(2,1)S(1)}, u32[]{:S(2)}) copy-start(bf16[32,144,128]{2,1,0:T(8,128)(2,1)S(1)} %all-to-all-done.mirror_ref) | copy-start | bytes 3538948
  109.8 24.9 %all-to-all-start.1 = ((bf16[32,144,128]{2,1,0:T(8,128)(2,1)}), bf16[32,144,128]{2,1,0:T(8,128)(2,1)S(1)}, u32[]{:S(2)}, u32[]{:S(2)}) async-start(bf16[32,144,128]{2,1,0:T(8,128)(2,1)} %hub_blocks.1), calls=%async_computation.1 | async-start | bytes 2359296 | tf_op jit(solution)/shard_map/all_to_all | solution.py:486
  130.6 15.5 %copy-start.5 = (f32[128]{0:T(128)S(1)}, f32[128]{0:T(128)}, u32[]{:S(2)}) copy-start(f32[128]{0:T(128)} %param.14) | copy-start | bytes 1540
  134.7 1.0 copy-start
  138.0 5.5 %collective-permute-start.4 = (f32[32,128]{1,0:T(8,128)}, f32[32,128]{1,0:T(8,128)S(1)}, u32[]{:S(2)}, u32[]{:S(2)}) collective-permute-start(f32[32,128]{1,0:T(8,128)} %bitcast.7), channel_id=1, source_target_pairs={{2,0},{3,1},{0,2},{1,3},{6,4},{7,5},{4,6},{5,7},{10,8},{11,9},{8,1... | collective-permute-start | bytes 49160 | tf_op jit(solution)/shard_map/ppermute | solution.py:452
  140.2 5.2 %collective-permute-start.5 = (f32[32,128]{1,0:T(8,128)}, f32[32,128]{1,0:T(8,128)S(1)}, u32[]{:S(2)}, u32[]{:S(2)}) collective-permute-start(f32[32,128]{1,0:T(8,128)} %bitcast.8), channel_id=1, source_target_pairs={{3,0},{0,1},{1,2},{2,3},{7,4},{4,5},{5,6},{6,7},{11,8},{8,9},{9,10... | collective-permute-start | bytes 49160 | tf_op jit(solution)/shard_map/ppermute | solution.py:452
  140.5 4.8 %collective-permute-start.3 = (f32[32,128]{1,0:T(8,128)}, f32[32,128]{1,0:T(8,128)S(1)}, u32[]{:S(2)}, u32[]{:S(2)}) collective-permute-start(f32[32,128]{1,0:T(8,128)} %bitcast.9), channel_id=1, source_target_pairs={{1,0},{2,1},{3,2},{0,3},{5,4},{6,5},{7,6},{4,7},{9,8},{10,9},{11,1... | collective-permute-start | bytes 49160 | tf_op jit(solution)/shard_map/ppermute | solution.py:452

commit v5 on v4

--- a/solution.py
+++ b/solution.py
@@ -11,7 +11,7 @@
 HUB_MIRRORS = 128
 CAP = 128
 DEG_ROWS = 16
-VMEM_LIMIT = 56 * 1024 * 1024
+VMEM_LIMIT = 44 * 1024 * 1024
 BF = jnp.bfloat16
 F32 = jnp.float32
 HOT = jnp.float8_e4m3fn
@@ -21,7 +21,7 @@
     live_ref, src_ref, dst_ref, rel_ref, coef_ref, words_ref, lhs_ref, spread, *, owners, src_tiles, group
 ):
     blocks = src_ref.shape[0]
-    relations, n_bases = coef_ref.shape
+    n_bases, relations = coef_ref.shape
     live = live_ref[0]
     src_tile = src_ref[:, :1] >> 7
     dst_tile = dst_ref[:, :1] >> 7
@@ -73,7 +73,9 @@
     relation = rel_wide.astype(jnp.int32)
     span = lax.broadcasted_iota(jnp.int32, (1, relations), 1)
     one_hot = jnp.where(relation == span, 1.0, 0.0).astype(BF)
-    mixing = jnp.dot(one_hot, coef_ref[...], preferred_element_type=F32)
+    mixing = lax.dot_general(
+        one_hot, coef_ref[...], (((1,), (1,)), ((), ())), preferred_element_type=F32
+    )
     copies = lhs_ref.shape[1] // n_bases
     blank = jnp.zeros_like(mixing)
     for i in range(copies):
@@ -101,72 +103,105 @@
         scratch_shapes=[pltpu.VMEM((4 * n_bases // TILE, 4 * blocks, TILE), F32)],
         compiler_params=pltpu.CompilerParams(vmem_limit_bytes=VMEM_LIMIT),
         name="prepare",
-    )(live, edge_src, edge_dst, block_rel.reshape(1, blocks), basis_coef)
-
-
-def mix_kernel(feat_ref, lhs_ref, bases_ref, w_ref, spread, rights, *, chunk):
+    )(live, edge_src, edge_dst, block_rel.reshape(1, blocks), basis_coef.T)
+
+
+def mix_kernel(feat_ref, lhs_ref, bases_ref, *rest, chunk):
+    w_ref, spread, rights = rest[-3:]
     n_bases, depth, cols = bases_ref.shape
-    side = pl.program_id(0) & 1
-    spread[...] = bases_ref[...].astype(F32).reshape(n_bases * depth, cols)
-    for d in range(depth):
-        octet, half, row = d // 8, d % 8 // 4, d % 4
-        rows = slice(row * n_bases, (row + 1) * n_bases)
-        rights[side, octet, rows, half * cols : (half + 1) * cols] = spread[
-            pl.ds(d, n_bases, stride=depth), :
-        ].astype(BF)
-    pairs = chunk // 8
-    low = lax.broadcasted_iota(jnp.int32, (pairs, 8, cols), 1) < 4
-    for row in range(0, lhs_ref.shape[0], chunk):
-        left = lhs_ref[row : row + chunk, :]
-        pair = row // 8
-        for first_octet in range(0, depth // 8, 2):
-            evens, odds = [], []
-            for octet in (first_octet, first_octet + 1):
-                out = jnp.dot(left, rights[1 - side, octet], preferred_element_type=F32)
-                first = out[:, :cols].reshape(pairs, 8, cols)
-                second = out[:, cols:].reshape(pairs, 8, cols)
-                evens.append(jnp.where(low, first, pltpu.roll(second, 4, 1)))
-                odds.append(jnp.where(low, pltpu.roll(first, 4, 1), second))
-            at = slice(first_octet * 8, first_octet * 8 + 16)
-            w_ref[pair : pair + pairs, 0, at] = jnp.concatenate(evens, axis=1).astype(BF)
-            w_ref[pair : pair + pairs, 1, at] = jnp.concatenate(odds, axis=1).astype(BF)
-
-
-def mix(feat, lhs, bases, blocks):
+    step = pl.program_id(0)
+    side = step & 1
+
+    def turn():
+        spread[...] = bases_ref[...].astype(F32).reshape(n_bases * depth, cols)
+        for d in range(depth):
+            octet, half, row = d // 8, d % 8 // 4, d % 4
+            rows = slice(row * n_bases, (row + 1) * n_bases)
+            rights[side, octet, rows, half * cols : (half + 1) * cols] = spread[
+                pl.ds(d, n_bases, stride=depth), :
+            ].astype(BF)
+
+    @pl.when(step == 0)
+    def _():
+        turn()
+
+    @pl.when(step > 0)
+    def _():
+        turn()
+        pairs = chunk // 8
+        low = lax.broadcasted_iota(jnp.int32, (pairs, 8, cols), 1) < 4
+        for row in range(0, lhs_ref.shape[0], chunk):
+            left = lhs_ref[row : row + chunk, :]
+            pair = row // 8
+            for first_octet in range(0, depth // 8, 2):
+                evens, odds = [], []
+                for octet in (first_octet, first_octet + 1):
+                    out = jnp.dot(left, rights[1 - side, octet], preferred_element_type=F32)
+                    first = out[:, :cols].reshape(pairs, 8, cols)
+                    second = out[:, cols:].reshape(pairs, 8, cols)
+                    evens.append(jnp.where(low, first, pltpu.roll(second, 4, 1)))
+                    odds.append(jnp.where(low, pltpu.roll(first, 4, 1), second))
+                at = slice(first_octet * 8, first_octet * 8 + 16)
+                w_ref[pair : pair + pairs, 0, at] = jnp.concatenate(evens, axis=1).astype(BF)
+                w_ref[pair : pair + pairs, 1, at] = jnp.concatenate(odds, axis=1).astype(BF)
+
+
+def mix(feat, lhs, bases, blocks, begin=0, end=None, earlier=None):
     n_bases, model_dim, cols = bases.shape
     depth = 32
     steps = model_dim // depth
+    end = steps if end is None else end
     per_part = cols // depth
 
     def bases_at(i, f):
-        return (0, lax.rem(jnp.minimum(i, steps - 1) + f[0] * per_part, steps), 0)
-
+        return (0, lax.rem(jnp.minimum(i + begin, end - 1) + f[0] * per_part, steps), 0)
+
+    more = [] if earlier is None else [earlier]
     return pl.pallas_call(
         functools.partial(mix_kernel, chunk=512),
         out_shape=jax.ShapeDtypeStruct((blocks // 2, 2, model_dim, cols), BF),
         grid_spec=pltpu.PrefetchScalarGridSpec(
             num_scalar_prefetch=1,
-            grid=(steps + 1,),
+            grid=(end - begin + 1,),
             in_specs=[
                 pl.BlockSpec(lhs.shape, lambda i, f: (0, 0)),
                 pl.BlockSpec((n_bases, depth, cols), bases_at),
-            ],
+            ]
+            + [pl.BlockSpec(memory_space=pl.ANY)] * len(more),
             out_specs=pl.BlockSpec(
-                (blocks // 2, 2, depth, cols), lambda i, f: (0, 0, jnp.maximum(i - 1, 0), 0)
+                (blocks // 2, 2, depth, cols),
+                lambda i, f: (0, 0, jnp.maximum(i - 1, 0) + begin, 0),
             ),
             scratch_shapes=[
                 pltpu.VMEM((n_bases * depth, cols), F32),
                 pltpu.VMEM((2, depth // 8, 4 * n_bases, 2 * cols), BF),
             ],
         ),
+        input_output_aliases={3: 0} if more else {},
         cost_estimate=pl.CostEstimate(
-            flops=8 * blocks * n_bases * model_dim * cols,
-            bytes_accessed=blocks * model_dim * cols * 2,
+            flops=8 * blocks * n_bases * depth * (end - begin) * cols,
+            bytes_accessed=blocks * depth * (end - begin) * cols * 2,
             transcendentals=0,
         ),
         compiler_params=pltpu.CompilerParams(vmem_limit_bytes=VMEM_LIMIT),
-        name="mix",
-    )(feat, lhs, bases)
+        name="mix" if earlier is None else "mix_rest",
+    )(feat, lhs, in_hbm(bases), *more)
+
+
+def in_vmem(x):
+    return pltpu.with_memory_space_constraint(x, pltpu.VMEM)
+
+
+def in_hbm(x):
+    return pltpu.with_memory_space_constraint(x, pltpu.HBM)
+
+
+def joins(joined, halves, sems, first_sem):
+    rows = halves[0].shape[0]
+    return [
+        pltpu.make_async_copy(half, joined.at[pl.ds(i * rows, rows)], sems.at[first_sem + i])
+        for i, half in enumerate(halves)
+    ]
 
 
 def unpack(word):
@@ -175,8 +210,8 @@
 
 def blocks_kernel(*refs, group, owners, split, hubs):
     word_ref, src_ref, dst_ref = refs[:3]
-    piece_refs, w_ref, out_ref = refs[3:7], refs[7], refs[8]
-    acc, deg, held, table, sems = refs[9:]
+    pieces, halves = refs[3:6], refs[6:8]
+    w_ref, out_ref, acc, deg, held, joined, sems = refs[8:]
     spans = word_ref.shape[1] - TILE
     first_group = word_ref[0, spans] if hubs else 0
     end_group = word_ref[0, spans + int(hubs)]
@@ -193,11 +228,7 @@
     def _():
         fetch(first_group)
 
-    cols = table.shape[1] // len(piece_refs)
-    loads = []
-    for p, piece in enumerate(piece_refs):
-        here = table.at[:, p * cols : (p + 1) * cols]
-        loads.append(pltpu.make_async_copy(piece, here, sems.at[2 + p]))
+    loads = joins(joined, halves, sems, 2)
     for load in loads:
         load.start()
     acc[...] = jnp.zeros_like(acc)
@@ -249,7 +280,10 @@
         def message(pair):
             src_tile = fields(pair, 0)[1]
             rows = pl.ds(pl.multiple_of(src_tile * TILE, TILE), TILE)
-            tile = table[rows, :]
+            tile = jnp.concatenate(
+                [pieces[0][rows, :], pieces[1][rows, :], joined[rows, :], pieces[2][rows, :]],
+                axis=1,
+            )
             weight = jnp.concatenate([held[side, pair, 0], held[side, pair, 1]], axis=1)
             out = jnp.dot(tile, weight, preferred_element_type=F32).astype(BF)
             return diagonal(out[:, :TILE], out[:, TILE:])
@@ -291,14 +325,14 @@
     return pl.pallas_call(
         functools.partial(blocks_kernel, group=group, owners=owners, split=split, hubs=hubs),
         out_shape=jax.ShapeDtypeStruct((owners, TILE + DEG_ROWS, cols), BF),
-        in_specs=[smem, vmem, vmem] + [anywhere] * (1 + len(pieces)),
+        in_specs=[smem, vmem, vmem] + [vmem] * 3 + [anywhere] * 3,
         out_specs=vmem,
         scratch_shapes=[
             pltpu.VMEM((owners, TILE, cols), F32),
             pltpu.VMEM((TILE, TILE), F32),
             pltpu.VMEM((2, group, 2, model_dim, cols), BF),
-            pltpu.VMEM((pieces[0].shape[0], model_dim), BF),
-            pltpu.SemaphoreType.DMA((2 + len(pieces),)),
+            pltpu.VMEM(pieces[0].shape, BF),
+            pltpu.SemaphoreType.DMA((4,)),
         ],
         cost_estimate=pl.CostEstimate(
             flops=pair_count * 4 * TILE * model_dim * cols,
@@ -324,12 +358,15 @@
     self_ref,
     x0_ref,
     x1_ref,
-    x2_ref,
     x3_ref,
+    first_ref,
+    second_ref,
     mixed_ref,
     squares_ref,
     right,
     turned,
+    x2_ref,
+    sems,
     *,
     chunk,
     reach,
@@ -340,6 +377,9 @@
 
     @pl.when(step == 0)
     def _():
+        loads = joins(x2_ref, (first_ref, second_ref), sems, 0)
+        for load in loads:
+            load.start()
         for p in range(4):
             at = pl.multiple_of(lax.rem(feat_ref[0] + p, 4) * cols, cols)
             turned[p * cols : (p + 1) * cols, :] = self_ref[pl.ds(at, cols), :]
@@ -353,6 +393,8 @@
             right[rows, :cols] = mirror_ref[p, :TILE, :]
             keep = (lane == p) | (lane == p + owners)
             right[rows, cols:] = jnp.where(keep, table, 0.0).astype(BF)
+        for load in loads:
+            load.wait()
 
     rows = pl.ds(pl.multiple_of(step * chunk, chunk), chunk)
     tile = jnp.concatenate(
@@ -376,12 +418,12 @@
         degree = jnp.sum(sums[:, cols:], axis=1, keepdims=True)
         mixed = own + sums[:, :cols] * lax.rsqrt(jnp.maximum(degree, 1.0))
         mixed_ref[...] = mixed
-        squares_ref[0] = square_lines(mixed)
+        squares_ref[...] = square_lines(mixed)
 
     @pl.when(step * chunk >= reach)
     def _():
         mixed_ref[...] = own
-        squares_ref[0] = square_lines(own)
+        squares_ref[...] = square_lines(own)
 
 
 def mirror_final(feat, mirror, master, self_weight, pieces):
@@ -393,20 +435,23 @@
         functools.partial(mirror_kernel, chunk=chunk, reach=n_local - n_local // 4),
         out_shape=(
             jax.ShapeDtypeStruct((n_local, cols), F32),
-            jax.ShapeDtypeStruct((n_local // chunk, chunk // TILE, TILE), F32),
+            jax.ShapeDtypeStruct((n_local // TILE, TILE), F32),
         ),
         grid_spec=pltpu.PrefetchScalarGridSpec(
             num_scalar_prefetch=1,
             grid=(n_local // chunk,),
             in_specs=[whole(mirror.shape), whole(master.shape), whole(self_weight.shape)]
-            + [whole(p.shape) for p in pieces],
+            + [whole(p.shape) for p in pieces[:3]]
+            + [pl.BlockSpec(memory_space=pl.ANY)] * 2,
             out_specs=(
                 pl.BlockSpec((chunk, cols), lambda i, *_: (i, 0)),
-                pl.BlockSpec((1, chunk // TILE, TILE), lambda i, *_: (i, 0, 0)),
+                pl.BlockSpec((chunk // TILE, TILE), lambda i, *_: (i, 0)),
             ),
             scratch_shapes=[
                 pltpu.VMEM((owners * TILE, 2 * cols), BF),
                 pltpu.VMEM(self_weight.shape, BF),
+                pltpu.VMEM(pieces[0].shape, BF),
+                pltpu.SemaphoreType.DMA((2,)),
             ],
         ),
         cost_estimate=pl.CostEstimate(
@@ -422,29 +467,49 @@
     counts = hub_ref[:, TILE : TILE + DEG_ROWS, :].astype(F32)
     line = jnp.sum(jnp.sum(counts, axis=0), axis=0, keepdims=True)
     column = jnp.broadcast_to(line, (TILE, TILE)).T[:, :1]
-    mixed = mixed_ref[...] + hub * lax.rsqrt(jnp.maximum(column, 1.0))
+    mixed = mixed_ref[:HUB_MIRRORS, :] + hub * lax.rsqrt(jnp.maximum(column, 1.0))
     out_ref[...] = mixed
     lines_ref[...] = squares_ref[...]
-    lines_ref[0, :1, :] = square_lines(mixed)
+    lines_ref[:1, :] = square_lines(mixed)
 
 
 def hub_final(hub, mixed, squares):
-    cols = mixed.shape[1]
-    hub_block = pl.BlockSpec(hub.shape, lambda i: (0, 0, 0))
-    mixed_block = pl.BlockSpec((HUB_MIRRORS, cols), lambda i: (0, 0))
-    line_block = pl.BlockSpec((1,) + squares.shape[1:], lambda i: (0, 0, 0))
+    vmem = pl.BlockSpec(memory_space=pltpu.VMEM)
     return pl.pallas_call(
         hub_kernel,
         out_shape=(
-            jax.ShapeDtypeStruct(mixed.shape, mixed.dtype),
-            jax.ShapeDtypeStruct(squares.shape, squares.dtype),
-        ),
-        grid=(1,),
-        in_specs=[hub_block, mixed_block, line_block],
-        out_specs=(mixed_block, line_block),
-        input_output_aliases={1: 0, 2: 1},
+            jax.ShapeDtypeStruct((HUB_MIRRORS, mixed.shape[1]), F32),
+            jax.ShapeDtypeStruct(squares.shape, F32),
+        ),
+        in_specs=[vmem] * 3,
+        out_specs=(vmem, vmem),
+        compiler_params=pltpu.CompilerParams(vmem_limit_bytes=VMEM_LIMIT),
         name="hub_final",
-    )(hub, mixed, squares)
+    )(hub, in_vmem(mixed), in_vmem(squares))
+
+
+def scale_kernel(mixed_ref, hub_ref, a_ref, b_ref, c_ref, d_ref, gain_ref, out_ref, *, model_dim):
+    lines = a_ref[...] + b_ref[...] + c_ref[...] + d_ref[...]
+    norm = lax.rsqrt(lines / model_dim + 1e-05)
+    gain = gain_ref[...]
+    tiles, width = norm.shape
+    for i in range(tiles):
+        rows = slice(i * width, (i + 1) * width)
+        value = hub_ref[...] if i == 0 else mixed_ref[rows, :]
+        column = jnp.broadcast_to(norm[i : i + 1, :], (width, width)).T
+        out_ref[rows, :] = (value * column * gain).astype(BF)
+
+
+def scale(mixed, hub_mixed, lines, gain, model_dim):
+    vmem = pl.BlockSpec(memory_space=pltpu.VMEM)
+    return pl.pallas_call(
+        functools.partial(scale_kernel, model_dim=model_dim),
+        out_shape=jax.ShapeDtypeStruct(mixed.shape, BF),
+        in_specs=[vmem] * 7,
+        out_specs=vmem,
+        compiler_params=pltpu.CompilerParams(vmem_limit_bytes=VMEM_LIMIT),
+        name="scale",
+    )(in_vmem(mixed), in_vmem(hub_mixed), *[in_vmem(x) for x in lines], gain)
 
 
 def from_others(x, size):
@@ -472,11 +537,25 @@
     blocks = edge_src.shape[0]
     n_local, cols = embeddings.shape
     model_dim = bases.shape[1]
-    pieces = [embeddings] + from_others(embeddings, feat_size)
+    feat_at = feat.reshape(1)
+    ahead = [((i + 1) % feat_size, i) for i in range(feat_size)]
+    behind = [(i, (i + 1) % feat_size) for i in range(feat_size)]
+    after = lax.ppermute(embeddings, "feat", ahead)
+    before = lax.ppermute(embeddings, "feat", behind)
+
     words, lhs = prepare(
         block_count, edge_src, edge_dst, block_rel, basis_coef, owners, n_local // TILE, 16
     )
-    weights = mix(feat.reshape(1), lhs, bases, blocks)
+    steps = 10
+    weights = mix(feat_at, lhs, bases, blocks, 0, steps)
+    weights, after, before = lax.optimization_barrier((weights, after, before))
+    half = n_local // 2
+    halves = [
+        lax.ppermute(after[:half], "feat", ahead),
+        lax.ppermute(before[half:], "feat", behind),
+    ]
+    weights = mix(feat_at, lhs, bases, blocks, steps, None, weights)
+    pieces = [in_vmem(x) for x in (embeddings, after, before)] + [in_hbm(x) for x in halves]
     edges = (edge_src, edge_dst)
     mirror_part = blocks_call(words, weights, *edges, pieces, owners, False)
     mirror = lax.all_to_all(mirror_part, "dom", split_axis=0, concat_axis=0, tiled=True)
@@ -488,13 +567,9 @@
     mixed, squares = mirror_final(
         feat.reshape(1), mirror, mirror_master_rows.reshape(owners, TILE), self_weight, pieces
     )
-    mixed, squares = hub_final(hub, mixed, squares)
-    line = squares.reshape(n_local // TILE, TILE)
-    everyone = line
-    for other in from_others(line, feat_size):
-        everyone = everyone + other
-    norm = lax.rsqrt(everyone.reshape(n_local) / model_dim + 1e-05)
-    return (mixed * norm[:, None] * out_gain).astype(BF)
+    hub_mixed, line = hub_final(hub, mixed, squares)
+    lines = [line] + from_others(line, feat_size)
+    return scale(mixed, hub_mixed, lines, out_gain.reshape(1, cols), model_dim)
 
 
 def solution(mesh):

time: 148 us -> 143 us (0.966); the launches traced: 149 us -> 142 us
  waiting for transfers between devices: 15 us -> 8.66 us
  local copies, waits for them, and re-layouts: 4.06 us -> 7.95 us
  other arithmetic: 3.45 us -> 0 us
  starting transfers between devices: 34.6 us -> 32.4 us
    ppermute x6 -> x3, starting transfers between devices: 11.4 us -> 3.42 us  [from_others(): lax.ppermute(x, 'feat', [((i + shift) % size, i) for i in range(size)])]
    ppermute x0 -> x4, starting transfers between devices: none -> 6.54 us  [the longest x1 2.79 us: on_device(): lax.ppermute(after[:half], 'feat', ahead)]
    unnamed x13 -> x32, local copies, waits for them, and re-layouts: 4.06 us -> 7.88 us
    all_to_all x1, waiting for transfers between devices: 6.35 us -> 2.96 us  [on_device(): lax.all_to_all(mirror_part, 'dom', split_axis=0, concat_axis=0, tiled=True)]
    convert_element_type x1 -> x0, other arithmetic: 2.72 us -> none  [on_device(): return (mixed * norm[:, None] * out_gain).astype(BF)]
    pallas_call x1 -> x2, Pallas kernels: 35.5 us -> 37.9 us  [mix(): pl.pallas_call(functools.partial(mix_kernel, chunk=512), out_shape=jax.Sh...]
    pallas_call x1, Pallas kernels: 3.7 us -> 1.7 us  [prepare(): pl.pallas_call(functools.partial(prepare_kernel, owners=owners, src_tiles...]
    ppermute x6 -> x3, waiting for transfers between devices: 4.53 us -> 2.58 us  [from_others(): lax.ppermute(x, 'feat', [((i + shift) % size, i) for i in range(size)])]
  transfers between devices with their start and end apart: 8 -> 9, of which waited for: 4 -> 5; matrix products, arithmetic and copies ran while one was open for 1% -> 0% of each run, Pallas kernels for 44% -> 47%
where the time goes in v5:
time: 143 us; the launch traced here: 142 us
  Pallas kernels  92.2 us (64%)
  starting transfers between devices  32.4 us (23%)
  waiting for transfers between devices  8.66 us (6%)
  local copies, waits for them, and re-layouts  7.95 us (6%)
    pallas_call x2, Pallas kernels, mix(): pl.pallas_call(functools.partial(mix_kernel, chunk=512), out_shape=jax.Sh...  37.9 us
    pallas_call x2, Pallas kernels, blocks_call(): pl.pallas_call(functools.partial(blocks_kernel, group=group, owners=owner...  36.7 us
    all_to_all x1, starting transfers between devices, on_device(): lax.all_to_all(mirror_part, 'dom', split_axis=0, concat_axis=0, tiled=True)  15.1 us
    pallas_call x1, Pallas kernels, mirror_final(): pl.pallas_call(functools.partial(mirror_kernel, chunk=chunk, reach=n_loca...  12.8 us
    unnamed x32, local copies, waits for them, and re-layouts  7.88 us
    all_to_all x1, starting transfers between devices, on_device(): lax.all_to_all(hub_part, 'dom', split_axis=0, concat_axis=0, tiled=True)  7.3 us
    ppermute x3, starting transfers between devices, from_others(): lax.ppermute(x, 'feat', [((i + shift) % size, i) for i in range(size)])  3.42 us
    all_to_all x1, waiting for transfers between devices, on_device(): lax.all_to_all(hub_part, 'dom', split_axis=0, concat_axis=0, tiled=True)  3.12 us
  transfers between devices with their start and end apart: 9, of which 5 were waited for; matrix products, arithmetic and copies ran while one was open for 0% of the time, Pallas kernels for 47%

profile of v5, /device:TPU:0, one launch (start us, length us, event | category | flops | bytes accessed | tf_op | source)
XLA Modules:
  0.0 142.1 jit_solution(12224252860997192226)
XLA Ops:
  0.0 1.7 %collective-permute-start.1 = (bf16[4096,128]{1,0:T(8,128)(2,1)}, bf16[4096,128]{1,0:T(8,128)(2,1)S(1)}, u32[]{:S(2)}, u32[]{:S(2)}) collective-permute-start(bf16[4096,128]{1,0:T(8,128)(2,1)} %x0_ref.1), channel_id=1, source_target_pairs={{0,1},{1,2},{2,3},{3,0},{4,5},{5,6},{6,7},{7,4},{8,9},{9,10},{10,1... | collective-permute-start | bytes 3145736 | tf_op jit(solution)/shard_map/ppermute | solution.py:544
  1.7 1.6 %collective-permute-start = (bf16[4096,128]{1,0:T(8,128)(2,1)}, bf16[4096,128]{1,0:T(8,128)(2,1)S(1)}, u32[]{:S(2)}, u32[]{:S(2)}) collective-permute-start(bf16[4096,128]{1,0:T(8,128)(2,1)} %x0_ref.1), channel_id=1, source_target_pairs={{1,0},{2,1},{3,2},{0,3},{5,4},{6,5},{7,6},{4,7},{9,8},{10,9},{11,1... | collective-permute-start | bytes 3145736 | tf_op jit(solution)/shard_map/ppermute | solution.py:543
  3.9 0.0 copy-start.4
  3.9 0.9 copy-done.4
  4.8 0.9 copy-done.6
  5.8 0.9 copy-done.9
  6.7 0.7 copy-done.10
  7.4 1.7 %prepare.1 = (s32[1,768]{1,0:T(1,128)S(1)}, bf16[2048,256]{1,0:T(8,128)(2,1)S(1)}) custom-call(s32[1]{0:T(128)S(6)} %copy.13.live_ref, s32[512,128]{1,0:T(8,128)S(1)} %copy-done.4, s32[512,128]{1,0:T(8,128)S(1)} %copy-done.6, s32[1,512]{1,0:T(1,128)S(1)} %bitcast.6, bf16[64,822]{1,0:T(8,128)(2,1)S(1)} %bitcast.5), custom_call_target="tpu_custom_call" | custom-call | tf_op jit(solution)/shard_map/prepare/pallas_call | solution.py:95
  9.1 22.8 %mix.1.rest_0_ = bf16[256,2,512,128]{3,2,1,0:T(8,128)(2,1)} custom-call(s32[1]{0:T(128)} %bitcast.feat_ref, bf16[2048,256]{1,0:T(8,128)(2,1)S(1)} %get-tuple-element.18.lhs_ref, bf16[64,512,128]{2,1,0:T(8,128)(2,1)} %bases_ref.3), custom_call_target="tpu_custom_call" | custom-call | flops 10737418240 | bytes 41943040 | tf_op jit(solution)/shard_map/mix/pallas_call | solution.py:160
  31.9 0.0 collective-permute-done.1.refs_5_.x3_ref
  31.9 0.0 collective-permute-done.refs_4_.x1_ref
  32.0 0.0 copy-start.2
  32.0 0.0 copy-start.5
  32.0 0.0 copy-start.7
  32.0 0.5 collective-permute-start.3
  32.5 2.8 %collective-permute-start.2 = (bf16[2048,128]{1,0:T(8,128)(2,1)S(1)}, bf16[2048,128]{1,0:T(8,128)(2,1)S(1)}, u32[]{:S(2)}, u32[]{:S(2)}) collective-permute-start(bf16[2048,128]{1,0:T(8,128)(2,1)S(1)} %slice.6), channel_id=1, source_target_pairs={{1,0},{2,1},{3,2},{0,3},{5,4},{6,5},{7,6},{4,7},{9,8},{10,9},{11,1... | collective-permute-start | bytes 1572872 | tf_op jit(solution)/shard_map/ppermute | solution.py:554
  35.3 15.1 %mix_rest.1.refs_8_ = bf16[256,2,512,128]{3,2,1,0:T(8,128)(2,1)} custom-call(s32[1]{0:T(128)} %bitcast.feat_ref, bf16[2048,256]{1,0:T(8,128)(2,1)S(1)} %get-tuple-element.18.lhs_ref, bf16[64,512,128]{2,1,0:T(8,128)(2,1)} %bases_ref.3, bf16[256,2,512,128]{3,2,1,0:T(8,128)(2,1)} %mix.1.rest_0_), custom_call_target="tpu_custom_call", output_to_operand_aliasing={{}: (3, {})} | custom-call | flops 6442450944 | bytes 25165824 | tf_op jit(solution)/shard_map/mix_rest/pallas_call | solution.py:160
  50.4 0.0 collective-permute-done.3.refs_7_.second_ref
  50.4 0.0 collective-permute-done.2.refs_6_.first_ref
  50.4 0.0 copy-start.15
  50.4 0.8 copy-done.14
  51.2 0.2 copy-done.15
  51.4 0.0 copy-done.2
  51.4 0.0 copy-done.5
  51.4 0.0 copy-done.7
  51.4 22.3 %mirror_blocks.1 = bf16[32,144,128]{2,1,0:T(8,128)(2,1)} custom-call(s32[1,768]{1,0:T(1,128)S(1)} %get-tuple-element.17.refs_0_, s32[512,128]{1,0:T(8,128)S(1)} %copy-done.5, s32[512,128]{1,0:T(8,128)S(1)} %copy-done.7, bf16[4096,128]{1,0:T(8,128)(2,1)S(1)} %copy-done.2, bf16[4096,128]{1,0:T(8,128)(2,1)S(1)} %collective-permute-done.refs_4_.x1_ref, ...), custom_call_target="tpu_custom_call" | custom-call | flops 8589934592 | bytes 33554432 | tf_op jit(solution)/shard_map/mirror_blocks/pallas_call | solution.py:325
  73.7 15.1 %all-to-all-start = ((bf16[32,144,128]{2,1,0:T(8,128)(2,1)}), bf16[32,144,128]{2,1,0:T(8,128)(2,1)}, u32[]{:S(2)}, u32[]{:S(2)}) async-start(bf16[32,144,128]{2,1,0:T(8,128)(2,1)} %mirror_blocks.1), calls=%async_computation | async-start | bytes 2359296 | tf_op jit(solution)/shard_map/all_to_all | solution.py:561
  88.8 0.0 copy-start.8
  88.8 0.9 copy-done.8
  89.8 14.4 %hub_blocks.1 = bf16[32,144,128]{2,1,0:T(8,128)(2,1)} custom-call(s32[1,768]{1,0:T(1,128)S(1)} %get-tuple-element.17.refs_0_, s32[512,128]{1,0:T(8,128)S(1)} %copy-done.5, s32[512,128]{1,0:T(8,128)S(1)} %copy-done.8, bf16[4096,128]{1,0:T(8,128)(2,1)S(1)} %copy-done.2, bf16[4096,128]{1,0:T(8,128)(2,1)S(1)} %collective-permute-done.refs_4_.x1_ref, ...), custom_call_target="tpu_custom_call" | custom-call | flops 8589934592 | bytes 33554432 | tf_op jit(solution)/shard_map/hub_blocks/pallas_call | solution.py:325
  104.2 0.0 copy-start.12
  104.2 0.0 copy-start.13
  104.2 3.0 %all-to-all-done.mirror_ref = bf16[32,144,128]{2,1,0:T(8,128)(2,1)} async-done(((bf16[32,144,128]{2,1,0:T(8,128)(2,1)}), bf16[32,144,128]{2,1,0:T(8,128)(2,1)}, u32[]{:S(2)}, u32[]{:S(2)}) %all-to-all-start) | async-done | bytes 1179680 | tf_op jit(solution)/shard_map/all_to_all | solution.py:561
  107.2 7.3 %all-to-all-start.1 = ((bf16[32,144,128]{2,1,0:T(8,128)(2,1)}), bf16[32,144,128]{2,1,0:T(8,128)(2,1)}, u32[]{:S(2)}, u32[]{:S(2)}) async-start(bf16[32,144,128]{2,1,0:T(8,128)(2,1)} %hub_blocks.1), calls=%async_computation.1 | async-start | bytes 2359296 | tf_op jit(solution)/shard_map/all_to_all | solution.py:565
  114.5 0.0 copy-start.1
  114.5 1.2 copy-done.1
  115.7 1.2 copy-done.3
  117.0 12.8 %mirror_final.1 = (f32[4096,128]{1,0:T(8,128)S(1)}, f32[32,128]{1,0:T(8,128)S(1)}) custom-call(s32[1]{0:T(128)} %bitcast.feat_ref, bf16[32,144,128]{2,1,0:T(8,128)(2,1)} %all-to-all-done.mirror_ref, s32[32,128]{1,0:T(8,128)S(1)} %bitcast.8, bf16[512,128]{1,0:T(8,128)(2,1)S(1)} %copy-done.12, bf16[4096,128]{1,0:T(8,128)(2,1)S(1)} %copy-done.3, ...), custom_call_target="tpu_custom_call" | custom-call | flops 8589934592 | bytes 8388608 | tf_op jit(solution)/shard_map/mirror_final/pallas_call | solution.py:434
  129.7 0.0 copy-start.11
  129.7 3.1 %all-to-all-done.1.hub_ref = bf16[32,144,128]{2,1,0:T(8,128)(2,1)} async-done(((bf16[32,144,128]{2,1,0:T(8,128)(2,1)}), bf16[32,144,128]{2,1,0:T(8,128)(2,1)}, u32[]{:S(2)}, u32[]{:S(2)}) %all-to-all-start.1) | async-done | bytes 1179680 | tf_op jit(solution)/shard_map/all_to_all | solution.py:565
  132.8 1.6 %hub_final.1 = (f32[128,128]{1,0:T(8,128)S(1)}, f32[32,128]{1,0:T(8,128)S(1)}) custom-call(bf16[32,144,128]{2,1,0:T(8,128)(2,1)} %all-to-all-done.1.hub_ref, f32[4096,128]{1,0:T(8,128)S(1)} %get-tuple-element.24.mixed_ref, f32[32,128]{1,0:T(8,128)S(1)} %get-tuple-element.26.squares_ref), custom_call_target="tpu_custom_call" | custom-call | tf_op jit(solution)/shard_map/hub_final/pallas_call | solution.py:478
  134.5 0.0 collective-permute-start.6
  134.5 2.1 %collective-permute-start.5 = (f32[32,128]{1,0:T(8,128)S(1)}, f32[32,128]{1,0:T(8,128)S(1)}, u32[]{:S(2)}, u32[]{:S(2)}) collective-permute-start(f32[32,128]{1,0:T(8,128)S(1)} %get-tuple-element.28.a_ref), channel_id=1, source_target_pairs={{2,0},{3,1},{0,2},{1,3},{6,4},{7,5},{4,6},{5,7},{10,8},{11,9},{8,1... | collective-permute-start | bytes 49160 | tf_op jit(solution)/shard_map/ppermute | solution.py:517
  136.6 1.3 collective-permute-start.4
  137.9 1.5 %collective-permute-done.6.d_ref = f32[32,128]{1,0:T(8,128)S(1)} collective-permute-done((f32[32,128]{1,0:T(8,128)S(1)}, f32[32,128]{1,0:T(8,128)S(1)}, u32[]{:S(2)}, u32[]{:S(2)}) %collective-permute-start.6) | collective-permute-done | bytes 16416 | tf_op jit(solution)/shard_map/ppermute | solution.py:517
  139.4 0.4 collective-permute-done.5.c_ref
  139.8 0.6 collective-permute-done.4.b_ref
  140.5 1.6 %scale.1 = bf16[4096,128]{1,0:T(8,128)(2,1)} custom-call(f32[4096,128]{1,0:T(8,128)S(1)} %get-tuple-element.24.mixed_ref, f32[128,128]{1,0:T(8,128)S(1)} %get-tuple-element.27.hub_ref, f32[32,128]{1,0:T(8,128)S(1)} %get-tuple-element.28.a_ref, f32[32,128]{1,0:T(8,128)S(1)} %collective-permute-done.4.b_ref, f32[32,128]{1,0:T(8,128)S(1)} %collective-permute-done.5.c_ref, ...), custom_call_target="tpu_custom_call" | custom-call | tf_op jit(solution)/shard_map/scale/pallas_call | solution.py:505
  (12 shorter events, 0.1 us)
Async XLA Ops:
  0.0 31.9 %collective-permute-start.1 = (bf16[4096,128]{1,0:T(8,128)(2,1)}, bf16[4096,128]{1,0:T(8,128)(2,1)S(1)}, u32[]{:S(2)}, u32[]{:S(2)}) collective-permute-start(bf16[4096,128]{1,0:T(8,128)(2,1)} %x0_ref.1), channel_id=1, source_target_pairs={{0,1},{1,2},{2,3},{3,0},{4,5},{5,6},{6,7},{7,4},{8,9},{9,10},{10,1... | collective-permute-start | bytes 3145736 | tf_op jit(solution)/shard_map/ppermute | solution.py:544
  1.7 30.2 %collective-permute-start = (bf16[4096,128]{1,0:T(8,128)(2,1)}, bf16[4096,128]{1,0:T(8,128)(2,1)S(1)}, u32[]{:S(2)}, u32[]{:S(2)}) collective-permute-start(bf16[4096,128]{1,0:T(8,128)(2,1)} %x0_ref.1), channel_id=1, source_target_pairs={{1,0},{2,1},{3,2},{0,3},{5,4},{6,5},{7,6},{4,7},{9,8},{10,9},{11,1... | collective-permute-start | bytes 3145736 | tf_op jit(solution)/shard_map/ppermute | solution.py:543
  3.9 1.0 copy-start.4
  4.8 0.9 copy-start.6
  5.8 0.9 copy-start.9
  6.7 0.7 copy-start.10
  31.9 56.9 %copy-start = (bf16[4096,128]{1,0:T(8,128)(2,1)}, bf16[4096,128]{1,0:T(8,128)(2,1)S(1)}, u32[]{:S(2)}) copy-start(bf16[4096,128]{1,0:T(8,128)(2,1)S(1)} %collective-permute-done.refs_4_.x1_ref) | copy-start | bytes 3145732
  32.0 19.4 %copy-start.2 = (bf16[4096,128]{1,0:T(8,128)(2,1)S(1)}, bf16[4096,128]{1,0:T(8,128)(2,1)}, u32[]{:S(2)}) copy-start(bf16[4096,128]{1,0:T(8,128)(2,1)} %x0_ref.1) | copy-start | bytes 3145732
  32.0 19.4 %copy-start.5 = (s32[512,128]{1,0:T(8,128)S(1)}, s32[512,128]{1,0:T(8,128)}, u32[]{:S(2)}) copy-start(s32[512,128]{1,0:T(8,128)} %refs_1_.3) | copy-start | bytes 786436
  32.0 19.4 %copy-start.7 = (s32[512,128]{1,0:T(8,128)S(1)}, s32[512,128]{1,0:T(8,128)}, u32[]{:S(2)}) copy-start(s32[512,128]{1,0:T(8,128)} %refs_2_.3) | copy-start | bytes 786436
  32.0 18.4 %collective-permute-start.3 = (bf16[2048,128]{1,0:T(8,128)(2,1)S(1)}, bf16[2048,128]{1,0:T(8,128)(2,1)S(1)}, u32[]{:S(2)}, u32[]{:S(2)}) collective-permute-start(bf16[2048,128]{1,0:T(8,128)(2,1)S(1)} %slice.7), channel_id=1, source_target_pairs={{0,1},{1,2},{2,3},{3,0},{4,5},{5,6},{6,7},{7,4},{8,9},{9,10},{10,1... | collective-permute-start | bytes 1572872 | tf_op jit(solution)/shard_map/ppermute | solution.py:555
  32.5 17.9 %collective-permute-start.2 = (bf16[2048,128]{1,0:T(8,128)(2,1)S(1)}, bf16[2048,128]{1,0:T(8,128)(2,1)S(1)}, u32[]{:S(2)}, u32[]{:S(2)}) collective-permute-start(bf16[2048,128]{1,0:T(8,128)(2,1)S(1)} %slice.6), channel_id=1, source_target_pairs={{1,0},{2,1},{3,2},{0,3},{5,4},{6,5},{7,6},{4,7},{9,8},{10,9},{11,1... | collective-permute-start | bytes 1572872 | tf_op jit(solution)/shard_map/ppermute | solution.py:554
  50.4 0.8 copy-start.14
  50.4 1.0 copy-start.15
  73.7 33.5 %all-to-all-start = ((bf16[32,144,128]{2,1,0:T(8,128)(2,1)}), bf16[32,144,128]{2,1,0:T(8,128)(2,1)}, u32[]{:S(2)}, u32[]{:S(2)}) async-start(bf16[32,144,128]{2,1,0:T(8,128)(2,1)} %mirror_blocks.1), calls=%async_computation | async-start | bytes 2359296 | tf_op jit(solution)/shard_map/all_to_all | solution.py:561
  88.8 1.0 copy-start.8
  104.2 10.3 %copy-start.12 = (bf16[512,128]{1,0:T(8,128)(2,1)S(1)}, bf16[512,128]{1,0:T(8,128)(2,1)}, u32[]{:S(2)}) copy-start(bf16[512,128]{1,0:T(8,128)(2,1)} %self_ref.1) | copy-start | bytes 393220
  104.2 10.3 %copy-start.13 = (s32[4096]{0:T(1024)S(1)}, s32[4096]{0:T(1024)}, u32[]{:S(2)}) copy-start(s32[4096]{0:T(1024)} %param.18) | copy-start | bytes 49156
  107.2 25.7 %all-to-all-start.1 = ((bf16[32,144,128]{2,1,0:T(8,128)(2,1)}), bf16[32,144,128]{2,1,0:T(8,128)(2,1)}, u32[]{:S(2)}, u32[]{:S(2)}) async-start(bf16[32,144,128]{2,1,0:T(8,128)(2,1)} %hub_blocks.1), calls=%async_computation.1 | async-start | bytes 2359296 | tf_op jit(solution)/shard_map/all_to_all | solution.py:565
  114.5 1.2 copy-start.1
  115.7 1.2 copy-start.3
  129.7 10.8 %copy-start.11 = (f32[128]{0:T(128)S(1)}, f32[128]{0:T(128)}, u32[]{:S(2)}) copy-start(f32[128]{0:T(128)} %param.14) | copy-start | bytes 1540
  134.5 5.0 %collective-permute-start.6 = (f32[32,128]{1,0:T(8,128)S(1)}, f32[32,128]{1,0:T(8,128)S(1)}, u32[]{:S(2)}, u32[]{:S(2)}) collective-permute-start(f32[32,128]{1,0:T(8,128)S(1)} %get-tuple-element.28.a_ref), channel_id=1, source_target_pairs={{3,0},{0,1},{1,2},{2,3},{7,4},{4,5},{5,6},{6,7},{11,8},{8,9},{9,10... | collective-permute-start | bytes 49160 | tf_op jit(solution)/shard_map/ppermute | solution.py:517
  134.5 5.3 %collective-permute-start.5 = (f32[32,128]{1,0:T(8,128)S(1)}, f32[32,128]{1,0:T(8,128)S(1)}, u32[]{:S(2)}, u32[]{:S(2)}) collective-permute-start(f32[32,128]{1,0:T(8,128)S(1)} %get-tuple-element.28.a_ref), channel_id=1, source_target_pairs={{2,0},{3,1},{0,2},{1,3},{6,4},{7,5},{4,6},{5,7},{10,8},{11,9},{8,1... | collective-permute-start | bytes 49160 | tf_op jit(solution)/shard_map/ppermute | solution.py:517
  136.6 3.9 %collective-permute-start.4 = (f32[32,128]{1,0:T(8,128)S(1)}, f32[32,128]{1,0:T(8,128)S(1)}, u32[]{:S(2)}, u32[]{:S(2)}) collective-permute-start(f32[32,128]{1,0:T(8,128)S(1)} %get-tuple-element.28.a_ref), channel_id=1, source_target_pairs={{1,0},{2,1},{3,2},{0,3},{5,4},{6,5},{7,6},{4,7},{9,8},{10,9},{11,1... | collective-permute-start | bytes 49160 | tf_op jit(solution)/shard_map/ppermute | solution.py:517

commit v6 on v5

--- a/solution.py
+++ b/solution.py
@@ -18,8 +18,34 @@
 
 
 def prepare_kernel(
-    live_ref, src_ref, dst_ref, rel_ref, coef_ref, words_ref, lhs_ref, spread, *, owners, src_tiles, group
+    live_ref,
+    src_hbm,
+    dst_hbm,
+    rel_hbm,
+    coef_hbm,
+    words_ref,
+    lhs_ref,
+    spread,
+    src_ref,
+    dst_ref,
+    rel_ref,
+    coef_ref,
+    sems,
+    *,
+    owners,
+    src_tiles,
+    group,
 ):
+    loads = [
+        pltpu.make_async_copy(a, b, sems.at[i])
+        for i, (a, b) in enumerate(
+            [(src_hbm, src_ref), (dst_hbm, dst_ref), (rel_hbm, rel_ref), (coef_hbm, coef_ref)]
+        )
+    ]
+    for load in loads:
+        load.start()
+    for load in loads:
+        load.wait()
     blocks = src_ref.shape[0]
     n_bases, relations = coef_ref.shape
     live = live_ref[0]
@@ -98,12 +124,25 @@
             jax.ShapeDtypeStruct((1, slots + TILE), jnp.int32),
             jax.ShapeDtypeStruct((4 * blocks, 4 * n_bases), BF),
         ),
-        in_specs=[pl.BlockSpec(memory_space=pltpu.SMEM)] + [vmem] * 4,
+        in_specs=[pl.BlockSpec(memory_space=pltpu.SMEM)] + [pl.BlockSpec(memory_space=pl.ANY)] * 4,
         out_specs=(vmem, vmem),
-        scratch_shapes=[pltpu.VMEM((4 * n_bases // TILE, 4 * blocks, TILE), F32)],
+        scratch_shapes=[
+            pltpu.VMEM((4 * n_bases // TILE, 4 * blocks, TILE), F32),
+            pltpu.VMEM(edge_src.shape, jnp.int32),
+            pltpu.VMEM(edge_dst.shape, jnp.int32),
+            pltpu.VMEM((1, blocks), jnp.int32),
+            pltpu.VMEM(basis_coef.shape[::-1], BF),
+            pltpu.SemaphoreType.DMA((4,)),
+        ],
         compiler_params=pltpu.CompilerParams(vmem_limit_bytes=VMEM_LIMIT),
         name="prepare",
-    )(live, edge_src, edge_dst, block_rel.reshape(1, blocks), basis_coef.T)
+    )(
+        live,
+        in_hbm(edge_src),
+        in_hbm(edge_dst),
+        in_hbm(block_rel.reshape(1, blocks)),
+        in_hbm(basis_coef.T),
+    )
 
 
 def mix_kernel(feat_ref, lhs_ref, bases_ref, *rest, chunk):
@@ -113,12 +152,14 @@
     side = step & 1
 
     def turn():
-        spread[...] = bases_ref[...].astype(F32).reshape(n_bases * depth, cols)
+        spread[:, :depth, :] = bases_ref[...].astype(F32)
+        pitch = spread.shape[1]
+        flat = spread.reshape(n_bases * pitch, cols)
         for d in range(depth):
             octet, half, row = d // 8, d % 8 // 4, d % 4
             rows = slice(row * n_bases, (row + 1) * n_bases)
-            rights[side, octet, rows, half * cols : (half + 1) * cols] = spread[
-                pl.ds(d, n_bases, stride=depth), :
+            rights[side, octet, rows, half * cols : (half + 1) * cols] = flat[
+                pl.ds(d, n_bases, stride=pitch), :
             ].astype(BF)
 
     @pl.when(step == 0)
@@ -173,7 +214,7 @@
                 lambda i, f: (0, 0, jnp.maximum(i - 1, 0) + begin, 0),
             ),
             scratch_shapes=[
-                pltpu.VMEM((n_bases * depth, cols), F32),
+                pltpu.VMEM((n_bases, depth + 8, cols), F32),
                 pltpu.VMEM((2, depth // 8, 4 * n_bases, 2 * cols), BF),
             ],
         ),
@@ -209,9 +250,9 @@
 
 
 def blocks_kernel(*refs, group, owners, split, hubs):
-    word_ref, src_ref, dst_ref = refs[:3]
+    word_ref, src_hbm, dst_hbm = refs[:3]
     pieces, halves = refs[3:6], refs[6:8]
-    w_ref, out_ref, acc, deg, held, joined, sems = refs[8:]
+    w_ref, out_ref, acc, deg, held, joined, src_ref, dst_ref, sems = refs[8:]
     spans = word_ref.shape[1] - TILE
     first_group = word_ref[0, spans] if hubs else 0
     end_group = word_ref[0, spans + int(hubs)]
@@ -229,6 +270,8 @@
         fetch(first_group)
 
     loads = joins(joined, halves, sems, 2)
+    loads.append(pltpu.make_async_copy(src_hbm, src_ref, sems.at[4]))
+    loads.append(pltpu.make_async_copy(dst_hbm, dst_ref, sems.at[5]))
     for load in loads:
         load.start()
     acc[...] = jnp.zeros_like(acc)
@@ -325,14 +368,16 @@
     return pl.pallas_call(
         functools.partial(blocks_kernel, group=group, owners=owners, split=split, hubs=hubs),
         out_shape=jax.ShapeDtypeStruct((owners, TILE + DEG_ROWS, cols), BF),
-        in_specs=[smem, vmem, vmem] + [vmem] * 3 + [anywhere] * 3,
+        in_specs=[smem, anywhere, anywhere] + [vmem] * 3 + [anywhere] * 3,
         out_specs=vmem,
         scratch_shapes=[
             pltpu.VMEM((owners, TILE, cols), F32),
             pltpu.VMEM((TILE, TILE), F32),
             pltpu.VMEM((2, group, 2, model_dim, cols), BF),
             pltpu.VMEM(pieces[0].shape, BF),
-            pltpu.SemaphoreType.DMA((4,)),
+            pltpu.VMEM(edge_src.shape, jnp.int32),
+            pltpu.VMEM(edge_dst.shape, jnp.int32),
+            pltpu.SemaphoreType.DMA((6,)),
         ],
         cost_estimate=pl.CostEstimate(
             flops=pair_count * 4 * TILE * model_dim * cols,
@@ -341,7 +386,14 @@
         ),
         compiler_params=pltpu.CompilerParams(vmem_limit_bytes=VMEM_LIMIT),
         name="hub_blocks" if hubs else "mirror_blocks",
-    )(words, edge_src, edge_dst, *pieces, weights)
+    )(
+        words,
+        in_hbm(edge_src),
+        in_hbm(edge_dst),
+        *[in_vmem(x) for x in pieces[:3]],
+        *[in_hbm(x) for x in pieces[3:]],
+        weights,
+    )
 
 
 def square_lines(value):
@@ -353,19 +405,20 @@
 
 def mirror_kernel(
     feat_ref,
-    mirror_ref,
+    mirror_hbm,
     master_ref,
     self_ref,
-    x0_ref,
-    x1_ref,
-    x3_ref,
-    first_ref,
-    second_ref,
+    x0_hbm,
+    x1_hbm,
+    x3_hbm,
+    first_hbm,
+    second_hbm,
     mixed_ref,
     squares_ref,
     right,
     turned,
-    x2_ref,
+    mirror_ref,
+    table,
     sems,
     *,
     chunk,
@@ -377,30 +430,40 @@
 
     @pl.when(step == 0)
     def _():
-        loads = joins(x2_ref, (first_ref, second_ref), sems, 0)
+        arrival = pltpu.make_async_copy(mirror_hbm, mirror_ref, sems.at[0])
+        arrival.start()
+        half = first_hbm.shape[0]
+        targets = [
+            (x0_hbm, table.at[:, :cols]),
+            (x1_hbm, table.at[:, cols : 2 * cols]),
+            (x3_hbm, table.at[:, 3 * cols :]),
+            (first_hbm, table.at[:half, 2 * cols : 3 * cols]),
+            (second_hbm, table.at[half:, 2 * cols : 3 * cols]),
+        ]
+        loads = [
+            pltpu.make_async_copy(a, b, sems.at[1 + i]) for i, (a, b) in enumerate(targets)
+        ]
         for load in loads:
             load.start()
         for p in range(4):
             at = pl.multiple_of(lax.rem(feat_ref[0] + p, 4) * cols, cols)
             turned[p * cols : (p + 1) * cols, :] = self_ref[pl.ds(at, cols), :]
+        arrival.wait()
         high = mirror_ref[:, TILE, :].astype(F32)
         low = mirror_ref[:, TILE + 1, :].astype(F32)
         pad = jnp.zeros((TILE - 2 * owners, TILE), F32)
-        table = jnp.concatenate([high, low, pad], axis=0).T
+        turned_counts = jnp.concatenate([high, low, pad], axis=0).T
         lane = lax.broadcasted_iota(jnp.int32, (TILE, TILE), 1)
         for p in range(owners):
             rows = slice(p * TILE, (p + 1) * TILE)
             right[rows, :cols] = mirror_ref[p, :TILE, :]
             keep = (lane == p) | (lane == p + owners)
-            right[rows, cols:] = jnp.where(keep, table, 0.0).astype(BF)
+            right[rows, cols:] = jnp.where(keep, turned_counts, 0.0).astype(BF)
         for load in loads:
             load.wait()
 
     rows = pl.ds(pl.multiple_of(step * chunk, chunk), chunk)
-    tile = jnp.concatenate(
-        [x0_ref[rows, :], x1_ref[rows, :], x2_ref[rows, :], x3_ref[rows, :]], axis=1
-    )
-    own = jnp.dot(tile, turned[...], preferred_element_type=F32)
+    own = jnp.dot(table[rows, :], turned[...], preferred_element_type=F32)
 
     @pl.when(step * chunk < reach)
     def _():
@@ -430,6 +493,7 @@
     n_local, cols = pieces[0].shape
     owners = mirror.shape[0]
     chunk = 1024
+    anywhere = pl.BlockSpec(memory_space=pl.ANY)
     whole = lambda shape: pl.BlockSpec(shape, lambda i, *_: (0,) * len(shape))
     return pl.pallas_call(
         functools.partial(mirror_kernel, chunk=chunk, reach=n_local - n_local // 4),
@@ -440,9 +504,8 @@
         grid_spec=pltpu.PrefetchScalarGridSpec(
             num_scalar_prefetch=1,
             grid=(n_local // chunk,),
-            in_specs=[whole(mirror.shape), whole(master.shape), whole(self_weight.shape)]
-            + [whole(p.shape) for p in pieces[:3]]
-            + [pl.BlockSpec(memory_space=pl.ANY)] * 2,
+            in_specs=[anywhere, whole(master.shape), whole(self_weight.shape)]
+            + [anywhere] * len(pieces),
             out_specs=(
                 pl.BlockSpec((chunk, cols), lambda i, *_: (i, 0)),
                 pl.BlockSpec((chunk // TILE, TILE), lambda i, *_: (i, 0)),
@@ -450,8 +513,9 @@
             scratch_shapes=[
                 pltpu.VMEM((owners * TILE, 2 * cols), BF),
                 pltpu.VMEM(self_weight.shape, BF),
-                pltpu.VMEM(pieces[0].shape, BF),
-                pltpu.SemaphoreType.DMA((2,)),
+                pltpu.VMEM(mirror.shape, BF),
+                pltpu.VMEM((n_local, 4 * cols), BF),
+                pltpu.SemaphoreType.DMA((1 + len(pieces),)),
             ],
         ),
         cost_estimate=pl.CostEstimate(
@@ -459,7 +523,7 @@
         ),
         compiler_params=pltpu.CompilerParams(vmem_limit_bytes=VMEM_LIMIT),
         name="mirror_final",
-    )(feat, mirror, master, self_weight, *pieces)
+    )(feat, in_hbm(mirror), master, self_weight, *[in_hbm(p) for p in pieces])
 
 
 def hub_kernel(hub_ref, mixed_ref, squares_ref, out_ref, lines_ref):
@@ -546,7 +610,7 @@
     words, lhs = prepare(
         block_count, edge_src, edge_dst, block_rel, basis_coef, owners, n_local // TILE, 16
     )
-    steps = 10
+    steps = 9
     weights = mix(feat_at, lhs, bases, blocks, 0, steps)
     weights, after, before = lax.optimization_barrier((weights, after, before))
     half = n_local // 2
@@ -555,7 +619,7 @@
         lax.ppermute(before[half:], "feat", behind),
     ]
     weights = mix(feat_at, lhs, bases, blocks, steps, None, weights)
-    pieces = [in_vmem(x) for x in (embeddings, after, before)] + [in_hbm(x) for x in halves]
+    pieces = [embeddings, after, before] + halves
     edges = (edge_src, edge_dst)
     mirror_part = blocks_call(words, weights, *edges, pieces, owners, False)
     mirror = lax.all_to_all(mirror_part, "dom", split_axis=0, concat_axis=0, tiled=True)

time: 143 us -> 136 us (0.951)
  Pallas kernels: 92.2 us -> 81.7 us
  waiting for transfers between devices: 8.66 us -> 16.6 us
  local copies, waits for them, and re-layouts: 7.95 us -> 2.09 us
  starting transfers between devices: 32.4 us -> 34.7 us
    pallas_call x2, Pallas kernels: 36.7 us -> 30.7 us  [blocks_call(): pl.pallas_call(functools.partial(blocks_kernel, group=group, owners=owner...]
    unnamed x32 -> x18, local copies, waits for them, and re-layouts: 7.88 us -> 2.02 us
    all_to_all x1, starting transfers between devices: 15.1 us -> 19.6 us  [on_device(): lax.all_to_all(mirror_part, 'dom', split_axis=0, concat_axis=0, tiled=True)]
    pallas_call x2, Pallas kernels: 37.9 us -> 33.5 us  [mix(): pl.pallas_call(functools.partial(mix_kernel, chunk=512), out_shape=jax.Sh...]
    all_to_all x1, waiting for transfers between devices: 2.96 us -> 7.32 us  [on_device(): lax.all_to_all(mirror_part, 'dom', split_axis=0, concat_axis=0, tiled=True)]
    all_to_all x1, starting transfers between devices: 7.3 us -> 4.12 us  [on_device(): lax.all_to_all(hub_part, 'dom', split_axis=0, concat_axis=0, tiled=True)]
    all_to_all x1, waiting for transfers between devices: 3.12 us -> 5.28 us  [on_device(): lax.all_to_all(hub_part, 'dom', split_axis=0, concat_axis=0, tiled=True)]
  transfers between devices with their start and end apart: 9 -> 9, of which waited for: 5 -> 6; matrix products, arithmetic and copies ran while one was open for 0% -> 0% of each run, Pallas kernels for 47% -> 43%
where the time goes in v6:
time: 136 us
  Pallas kernels  81.7 us (60%)
  starting transfers between devices  34.7 us (26%)
  waiting for transfers between devices  16.6 us (12%)
  local copies, waits for them, and re-layouts  2.09 us (2%)
    pallas_call x2, Pallas kernels, mix(): pl.pallas_call(functools.partial(mix_kernel, chunk=512), out_shape=jax.Sh...  33.5 us
    pallas_call x2, Pallas kernels, blocks_call(): pl.pallas_call(functools.partial(blocks_kernel, group=group, owners=owner...  30.7 us
    all_to_all x1, starting transfers between devices, on_device(): lax.all_to_all(mirror_part, 'dom', split_axis=0, concat_axis=0, tiled=True)  19.6 us
    pallas_call x1, Pallas kernels, mirror_final(): pl.pallas_call(functools.partial(mirror_kernel, chunk=chunk, reach=n_loca...  12.8 us
    all_to_all x1, waiting for transfers between devices, on_device(): lax.all_to_all(mirror_part, 'dom', split_axis=0, concat_axis=0, tiled=True)  7.32 us
    all_to_all x1, waiting for transfers between devices, on_device(): lax.all_to_all(hub_part, 'dom', split_axis=0, concat_axis=0, tiled=True)  5.28 us
    ppermute x3, starting transfers between devices, from_others(): lax.ppermute(x, 'feat', [((i + shift) % size, i) for i in range(size)])  4.34 us
    all_to_all x1, starting transfers between devices, on_device(): lax.all_to_all(hub_part, 'dom', split_axis=0, concat_axis=0, tiled=True)  4.12 us
  transfers between devices with their start and end apart: 9, of which 6 were waited for; matrix products, arithmetic and copies ran while one was open for 0% of the time, Pallas kernels for 43%

profile of v6, /device:TPU:0, one launch (start us, length us, event | category | flops | bytes accessed | tf_op | source)
XLA Modules:
  0.0 135.8 jit_solution(6573053577340652447)
XLA Ops:
  0.0 1.7 %collective-permute-start.1 = (bf16[4096,128]{1,0:T(8,128)(2,1)}, bf16[4096,128]{1,0:T(8,128)(2,1)S(1)}, u32[]{:S(2)}, u32[]{:S(2)}) collective-permute-start(bf16[4096,128]{1,0:T(8,128)(2,1)} %x0_hbm.1), channel_id=1, source_target_pairs={{0,1},{1,2},{2,3},{3,0},{4,5},{5,6},{6,7},{7,4},{8,9},{9,10},{10,1... | collective-permute-start | bytes 3145736 | tf_op jit(solution)/shard_map/ppermute | solution.py:608
  1.7 1.6 %collective-permute-start = (bf16[4096,128]{1,0:T(8,128)(2,1)}, bf16[4096,128]{1,0:T(8,128)(2,1)S(1)}, u32[]{:S(2)}, u32[]{:S(2)}) collective-permute-start(bf16[4096,128]{1,0:T(8,128)(2,1)} %x0_hbm.1), channel_id=1, source_target_pairs={{1,0},{2,1},{3,2},{0,3},{5,4},{6,5},{7,6},{4,7},{9,8},{10,9},{11,1... | collective-permute-start | bytes 3145736 | tf_op jit(solution)/shard_map/ppermute | solution.py:607
  3.9 2.8 %prepare.1 = (s32[1,768]{1,0:T(1,128)S(1)}, bf16[2048,256]{1,0:T(8,128)(2,1)S(1)}) custom-call(s32[1]{0:T(128)S(6)} %copy.13.live_ref, s32[512,128]{1,0:T(8,128)} %refs_1_.3, s32[512,128]{1,0:T(8,128)} %refs_2_.3, s32[1,512]{1,0:T(1,128)} %bitcast.8, bf16[64,822]{1,0:T(8,128)(2,1)} %bitcast.7), custom_call_target="tpu_custom_call" | custom-call | tf_op jit(solution)/shard_map/prepare/pallas_call | solution.py:121
  6.7 18.5 %mix.1.rest_0_ = bf16[256,2,512,128]{3,2,1,0:T(8,128)(2,1)} custom-call(s32[1]{0:T(128)} %bitcast.feat_ref, bf16[2048,256]{1,0:T(8,128)(2,1)S(1)} %get-tuple-element.18.lhs_ref, bf16[64,512,128]{2,1,0:T(8,128)(2,1)} %bases_ref.3), custom_call_target="tpu_custom_call" | custom-call | flops 9663676416 | bytes 37748736 | tf_op jit(solution)/shard_map/mix/pallas_call | solution.py:201
  25.1 1.3 collective-permute-done.1.refs_5_.x3_hbm
  26.5 0.0 copy-start
  26.5 0.0 collective-permute-done.refs_4_.x1_hbm
  26.5 0.0 copy-start.1
  26.6 0.0 copy-start.3
  26.6 1.6 %collective-permute-start.3 = (bf16[2048,128]{1,0:T(8,128)(2,1)S(1)}, bf16[2048,128]{1,0:T(8,128)(2,1)S(1)}, u32[]{:S(2)}, u32[]{:S(2)}) collective-permute-start(bf16[2048,128]{1,0:T(8,128)(2,1)S(1)} %slice.7), channel_id=1, source_target_pairs={{0,1},{1,2},{2,3},{3,0},{4,5},{5,6},{6,7},{7,4},{8,9},{9,10},{10,1... | collective-permute-start | bytes 1572872 | tf_op jit(solution)/shard_map/ppermute | solution.py:619
  28.2 1.7 %collective-permute-start.2 = (bf16[2048,128]{1,0:T(8,128)(2,1)S(1)}, bf16[2048,128]{1,0:T(8,128)(2,1)S(1)}, u32[]{:S(2)}, u32[]{:S(2)}) collective-permute-start(bf16[2048,128]{1,0:T(8,128)(2,1)S(1)} %slice.6), channel_id=1, source_target_pairs={{1,0},{2,1},{3,2},{0,3},{5,4},{6,5},{7,6},{4,7},{9,8},{10,9},{11,1... | collective-permute-start | bytes 1572872 | tf_op jit(solution)/shard_map/ppermute | solution.py:618
  29.9 15.0 %mix_rest.1.refs_8_ = bf16[256,2,512,128]{3,2,1,0:T(8,128)(2,1)} custom-call(s32[1]{0:T(128)} %bitcast.feat_ref, bf16[2048,256]{1,0:T(8,128)(2,1)S(1)} %get-tuple-element.18.lhs_ref, bf16[64,512,128]{2,1,0:T(8,128)(2,1)} %bases_ref.3, bf16[256,2,512,128]{3,2,1,0:T(8,128)(2,1)} %mix.1.rest_0_), custom_call_target="tpu_custom_call", output_to_operand_aliasing={{}: (3, {})} | custom-call | flops 7516192768 | bytes 29360128 | tf_op jit(solution)/shard_map/mix_rest/pallas_call | solution.py:201
  44.9 0.0 collective-permute-done.3.refs_7_.second_hbm
  44.9 0.0 copy-start.7
  44.9 0.0 collective-permute-done.2.refs_6_.first_hbm
  44.9 0.0 copy-start.8
  44.9 0.8 copy-done.7
  45.7 0.2 copy-done.8
  45.9 0.0 copy-done.3
  45.9 20.7 %mirror_blocks.1 = bf16[32,144,128]{2,1,0:T(8,128)(2,1)} custom-call(s32[1,768]{1,0:T(1,128)S(1)} %get-tuple-element.17.refs_0_, s32[512,128]{1,0:T(8,128)} %refs_1_.3, s32[512,128]{1,0:T(8,128)} %refs_2_.3, bf16[4096,128]{1,0:T(8,128)(2,1)S(1)} %copy-done.3, bf16[4096,128]{1,0:T(8,128)(2,1)S(1)} %collective-permute-done.refs_4_.x1_hbm, ...), custom_call_target="tpu_custom_call" | custom-call | flops 8589934592 | bytes 33554432 | tf_op jit(solution)/shard_map/mirror_blocks/pallas_call | solution.py:368
  66.6 19.6 %all-to-all-start = ((bf16[32,144,128]{2,1,0:T(8,128)(2,1)}), bf16[32,144,128]{2,1,0:T(8,128)(2,1)}, u32[]{:S(2)}, u32[]{:S(2)}) async-start(bf16[32,144,128]{2,1,0:T(8,128)(2,1)} %mirror_blocks.1), calls=%async_computation | async-start | bytes 2359296 | tf_op jit(solution)/shard_map/all_to_all | solution.py:625
  86.2 0.0 copy-done
  86.2 0.0 copy-done.1
  86.2 10.0 %hub_blocks.1 = bf16[32,144,128]{2,1,0:T(8,128)(2,1)S(1)} custom-call(s32[1,768]{1,0:T(1,128)S(1)} %get-tuple-element.17.refs_0_, s32[512,128]{1,0:T(8,128)} %refs_1_.3, s32[512,128]{1,0:T(8,128)} %refs_2_.3, bf16[4096,128]{1,0:T(8,128)(2,1)S(1)} %copy-done.3, bf16[4096,128]{1,0:T(8,128)(2,1)S(1)} %collective-permute-done.refs_4_.x1_hbm, ...), custom_call_target="tpu_custom_call" | custom-call | flops 8589934592 | bytes 33554432 | tf_op jit(solution)/shard_map/hub_blocks/pallas_call | solution.py:368
  96.2 0.0 copy-start.2
  96.2 1.0 copy-done.2
  97.3 0.0 copy-start.5
  97.3 0.0 copy-start.6
  97.3 7.3 %all-to-all-done.mirror_hbm = bf16[32,144,128]{2,1,0:T(8,128)(2,1)} async-done(((bf16[32,144,128]{2,1,0:T(8,128)(2,1)}), bf16[32,144,128]{2,1,0:T(8,128)(2,1)}, u32[]{:S(2)}, u32[]{:S(2)}) %all-to-all-start) | async-done | bytes 1179680 | tf_op jit(solution)/shard_map/all_to_all | solution.py:625
  104.6 4.1 %all-to-all-start.1 = ((bf16[32,144,128]{2,1,0:T(8,128)(2,1)}), bf16[32,144,128]{2,1,0:T(8,128)(2,1)S(1)}, u32[]{:S(2)}, u32[]{:S(2)}) async-start(bf16[32,144,128]{2,1,0:T(8,128)(2,1)} %copy-done.2), calls=%async_computation.1 | async-start | bytes 2359296 | tf_op jit(solution)/shard_map/all_to_all | solution.py:629
  108.7 0.0 copy-done.5
  108.7 0.0 copy-done.6
  108.7 12.8 %mirror_final.1 = (f32[4096,128]{1,0:T(8,128)S(1)}, f32[32,128]{1,0:T(8,128)S(1)}) custom-call(s32[1]{0:T(128)} %bitcast.feat_ref, bf16[32,144,128]{2,1,0:T(8,128)(2,1)} %all-to-all-done.mirror_hbm, s32[32,128]{1,0:T(8,128)S(1)} %bitcast.6, bf16[512,128]{1,0:T(8,128)(2,1)S(1)} %copy-done.5, bf16[4096,128]{1,0:T(8,128)(2,1)} %x0_hbm.1, ...), custom_call_target="tpu_custom_call" | custom-call | flops 8589934592 | bytes 8388608 | tf_op jit(solution)/shard_map/mirror_final/pallas_call | solution.py:498
  121.6 0.0 copy-start.4
  121.6 5.3 %all-to-all-done.1.hub_ref = bf16[32,144,128]{2,1,0:T(8,128)(2,1)S(1)} async-done(((bf16[32,144,128]{2,1,0:T(8,128)(2,1)}), bf16[32,144,128]{2,1,0:T(8,128)(2,1)S(1)}, u32[]{:S(2)}, u32[]{:S(2)}) %all-to-all-start.1) | async-done | bytes 1179680 | tf_op jit(solution)/shard_map/all_to_all | solution.py:629
  126.9 0.3 hub_final.1
  127.2 0.4 collective-permute-start.6
  127.6 2.8 %collective-permute-start.5 = (f32[32,128]{1,0:T(8,128)S(1)}, f32[32,128]{1,0:T(8,128)S(1)}, u32[]{:S(2)}, u32[]{:S(2)}) collective-permute-start(f32[32,128]{1,0:T(8,128)S(1)} %get-tuple-element.28.a_ref), channel_id=1, source_target_pairs={{2,0},{3,1},{0,2},{1,3},{6,4},{7,5},{4,6},{5,7},{10,8},{11,9},{8,1... | collective-permute-start | bytes 49160 | tf_op jit(solution)/shard_map/ppermute | solution.py:581
  130.4 1.1 collective-permute-start.4
  131.6 0.6 collective-permute-done.6.d_ref
  132.2 0.6 collective-permute-done.5.c_ref
  132.8 1.3 collective-permute-done.4.b_ref
  134.2 0.0 copy-done.4
  134.2 1.6 %scale.1 = bf16[4096,128]{1,0:T(8,128)(2,1)} custom-call(f32[4096,128]{1,0:T(8,128)S(1)} %get-tuple-element.24.mixed_ref, f32[128,128]{1,0:T(8,128)S(1)} %get-tuple-element.27.hub_ref, f32[32,128]{1,0:T(8,128)S(1)} %get-tuple-element.28.a_ref, f32[32,128]{1,0:T(8,128)S(1)} %collective-permute-done.4.b_ref, f32[32,128]{1,0:T(8,128)S(1)} %collective-permute-done.5.c_ref, ...), custom_call_target="tpu_custom_call" | custom-call | tf_op jit(solution)/shard_map/scale/pallas_call | solution.py:569
  (2 shorter events, 0.1 us)
Async XLA Ops:
  0.0 26.5 %collective-permute-start.1 = (bf16[4096,128]{1,0:T(8,128)(2,1)}, bf16[4096,128]{1,0:T(8,128)(2,1)S(1)}, u32[]{:S(2)}, u32[]{:S(2)}) collective-permute-start(bf16[4096,128]{1,0:T(8,128)(2,1)} %x0_hbm.1), channel_id=1, source_target_pairs={{0,1},{1,2},{2,3},{3,0},{4,5},{5,6},{6,7},{7,4},{8,9},{9,10},{10,1... | collective-permute-start | bytes 3145736 | tf_op jit(solution)/shard_map/ppermute | solution.py:608
  1.7 24.8 %collective-permute-start = (bf16[4096,128]{1,0:T(8,128)(2,1)}, bf16[4096,128]{1,0:T(8,128)(2,1)S(1)}, u32[]{:S(2)}, u32[]{:S(2)}) collective-permute-start(bf16[4096,128]{1,0:T(8,128)(2,1)} %x0_hbm.1), channel_id=1, source_target_pairs={{1,0},{2,1},{3,2},{0,3},{5,4},{6,5},{7,6},{4,7},{9,8},{10,9},{11,1... | collective-permute-start | bytes 3145736 | tf_op jit(solution)/shard_map/ppermute | solution.py:607
  26.5 59.8 %copy-start = (bf16[4096,128]{1,0:T(8,128)(2,1)}, bf16[4096,128]{1,0:T(8,128)(2,1)S(1)}, u32[]{:S(2)}) copy-start(bf16[4096,128]{1,0:T(8,128)(2,1)S(1)} %collective-permute-done.1.refs_5_.x3_hbm) | copy-start | bytes 3145732
  26.5 59.7 %copy-start.1 = (bf16[4096,128]{1,0:T(8,128)(2,1)}, bf16[4096,128]{1,0:T(8,128)(2,1)S(1)}, u32[]{:S(2)}) copy-start(bf16[4096,128]{1,0:T(8,128)(2,1)S(1)} %collective-permute-done.refs_4_.x1_hbm) | copy-start | bytes 3145732
  26.6 19.3 %copy-start.3 = (bf16[4096,128]{1,0:T(8,128)(2,1)S(1)}, bf16[4096,128]{1,0:T(8,128)(2,1)}, u32[]{:S(2)}) copy-start(bf16[4096,128]{1,0:T(8,128)(2,1)} %x0_hbm.1) | copy-start | bytes 3145732
  26.6 18.3 %collective-permute-start.3 = (bf16[2048,128]{1,0:T(8,128)(2,1)S(1)}, bf16[2048,128]{1,0:T(8,128)(2,1)S(1)}, u32[]{:S(2)}, u32[]{:S(2)}) collective-permute-start(bf16[2048,128]{1,0:T(8,128)(2,1)S(1)} %slice.7), channel_id=1, source_target_pairs={{0,1},{1,2},{2,3},{3,0},{4,5},{5,6},{6,7},{7,4},{8,9},{9,10},{10,1... | collective-permute-start | bytes 1572872 | tf_op jit(solution)/shard_map/ppermute | solution.py:619
  28.2 16.7 %collective-permute-start.2 = (bf16[2048,128]{1,0:T(8,128)(2,1)S(1)}, bf16[2048,128]{1,0:T(8,128)(2,1)S(1)}, u32[]{:S(2)}, u32[]{:S(2)}) collective-permute-start(bf16[2048,128]{1,0:T(8,128)(2,1)S(1)} %slice.6), channel_id=1, source_target_pairs={{1,0},{2,1},{3,2},{0,3},{5,4},{6,5},{7,6},{4,7},{9,8},{10,9},{11,1... | collective-permute-start | bytes 1572872 | tf_op jit(solution)/shard_map/ppermute | solution.py:618
  44.9 0.8 copy-start.7
  44.9 1.0 copy-start.8
  66.6 38.0 %all-to-all-start = ((bf16[32,144,128]{2,1,0:T(8,128)(2,1)}), bf16[32,144,128]{2,1,0:T(8,128)(2,1)}, u32[]{:S(2)}, u32[]{:S(2)}) async-start(bf16[32,144,128]{2,1,0:T(8,128)(2,1)} %mirror_blocks.1), calls=%async_computation | async-start | bytes 2359296 | tf_op jit(solution)/shard_map/all_to_all | solution.py:625
  96.2 1.0 copy-start.2
  97.3 11.5 %copy-start.5 = (bf16[512,128]{1,0:T(8,128)(2,1)S(1)}, bf16[512,128]{1,0:T(8,128)(2,1)}, u32[]{:S(2)}) copy-start(bf16[512,128]{1,0:T(8,128)(2,1)} %self_ref.1) | copy-start | bytes 393220
  97.3 11.5 %copy-start.6 = (s32[4096]{0:T(1024)S(1)}, s32[4096]{0:T(1024)}, u32[]{:S(2)}) copy-start(s32[4096]{0:T(1024)} %param.18) | copy-start | bytes 49156
  104.6 22.3 %all-to-all-start.1 = ((bf16[32,144,128]{2,1,0:T(8,128)(2,1)}), bf16[32,144,128]{2,1,0:T(8,128)(2,1)S(1)}, u32[]{:S(2)}, u32[]{:S(2)}) async-start(bf16[32,144,128]{2,1,0:T(8,128)(2,1)} %copy-done.2), calls=%async_computation.1 | async-start | bytes 2359296 | tf_op jit(solution)/shard_map/all_to_all | solution.py:629
  121.6 12.6 %copy-start.4 = (f32[128]{0:T(128)S(1)}, f32[128]{0:T(128)}, u32[]{:S(2)}) copy-start(f32[128]{0:T(128)} %param.14) | copy-start | bytes 1540
  127.2 5.0 %collective-permute-start.6 = (f32[32,128]{1,0:T(8,128)S(1)}, f32[32,128]{1,0:T(8,128)S(1)}, u32[]{:S(2)}, u32[]{:S(2)}) collective-permute-start(f32[32,128]{1,0:T(8,128)S(1)} %get-tuple-element.28.a_ref), channel_id=1, source_target_pairs={{3,0},{0,1},{1,2},{2,3},{7,4},{4,5},{5,6},{6,7},{11,8},{8,9},{9,10... | collective-permute-start | bytes 49160 | tf_op jit(solution)/shard_map/ppermute | solution.py:581
  127.6 5.2 %collective-permute-start.5 = (f32[32,128]{1,0:T(8,128)S(1)}, f32[32,128]{1,0:T(8,128)S(1)}, u32[]{:S(2)}, u32[]{:S(2)}) collective-permute-start(f32[32,128]{1,0:T(8,128)S(1)} %get-tuple-element.28.a_ref), channel_id=1, source_target_pairs={{2,0},{3,1},{0,2},{1,3},{6,4},{7,5},{4,6},{5,7},{10,8},{11,9},{8,1... | collective-permute-start | bytes 49160 | tf_op jit(solution)/shard_map/ppermute | solution.py:581
  130.4 3.7 %collective-permute-start.4 = (f32[32,128]{1,0:T(8,128)S(1)}, f32[32,128]{1,0:T(8,128)S(1)}, u32[]{:S(2)}, u32[]{:S(2)}) collective-permute-start(f32[32,128]{1,0:T(8,128)S(1)} %get-tuple-element.28.a_ref), channel_id=1, source_target_pairs={{1,0},{2,1},{3,2},{0,3},{5,4},{6,5},{7,6},{4,7},{9,8},{10,9},{11,1... | collective-permute-start | bytes 49160 | tf_op jit(solution)/shard_map/ppermute | solution.py:581

commit v7 on v6

--- a/solution.py
+++ b/solution.py
@@ -90,7 +90,9 @@
     word = index | (src_tile << 9) | (dst_tile << 14) | (1 << 20)
     slots = words_ref.shape[1] - TILE
     slot = lax.broadcasted_iota(jnp.int32, (1, slots), 1)
-    words_ref[:, :slots] = jnp.sum(jnp.where(place == slot, word, 0), axis=0, keepdims=True)
+    words = jnp.sum(jnp.where(place == slot, word, 0), axis=0, keepdims=True)
+    padding = lax.rem(slot, blocks) | ((slot & 31) << 14)
+    words_ref[:, :slots] = jnp.where(words == 0, padding, words)
     words_ref[:, slots:] = jnp.where(
         lane == 0, mirror_groups, jnp.where(lane == 1, mirror_groups + hub_groups, 0)
     )
@@ -148,43 +150,31 @@
 def mix_kernel(feat_ref, lhs_ref, bases_ref, *rest, chunk):
     w_ref, spread, rights = rest[-3:]
     n_bases, depth, cols = bases_ref.shape
-    step = pl.program_id(0)
-    side = step & 1
-
-    def turn():
-        spread[:, :depth, :] = bases_ref[...].astype(F32)
-        pitch = spread.shape[1]
-        flat = spread.reshape(n_bases * pitch, cols)
-        for d in range(depth):
-            octet, half, row = d // 8, d % 8 // 4, d % 4
-            rows = slice(row * n_bases, (row + 1) * n_bases)
-            rights[side, octet, rows, half * cols : (half + 1) * cols] = flat[
-                pl.ds(d, n_bases, stride=pitch), :
-            ].astype(BF)
-
-    @pl.when(step == 0)
-    def _():
-        turn()
-
-    @pl.when(step > 0)
-    def _():
-        turn()
-        pairs = chunk // 8
-        low = lax.broadcasted_iota(jnp.int32, (pairs, 8, cols), 1) < 4
-        for row in range(0, lhs_ref.shape[0], chunk):
-            left = lhs_ref[row : row + chunk, :]
-            pair = row // 8
-            for first_octet in range(0, depth // 8, 2):
-                evens, odds = [], []
-                for octet in (first_octet, first_octet + 1):
-                    out = jnp.dot(left, rights[1 - side, octet], preferred_element_type=F32)
-                    first = out[:, :cols].reshape(pairs, 8, cols)
-                    second = out[:, cols:].reshape(pairs, 8, cols)
-                    evens.append(jnp.where(low, first, pltpu.roll(second, 4, 1)))
-                    odds.append(jnp.where(low, pltpu.roll(first, 4, 1), second))
-                at = slice(first_octet * 8, first_octet * 8 + 16)
-                w_ref[pair : pair + pairs, 0, at] = jnp.concatenate(evens, axis=1).astype(BF)
-                w_ref[pair : pair + pairs, 1, at] = jnp.concatenate(odds, axis=1).astype(BF)
+    spread[:, :depth, :] = bases_ref[...].astype(F32)
+    pitch = spread.shape[1]
+    flat = spread.reshape(n_bases * pitch, cols)
+    for d in range(depth):
+        octet, half, row = d // 8, d % 8 // 4, d % 4
+        rows = slice(row * n_bases, (row + 1) * n_bases)
+        rights[octet, rows, half * cols : (half + 1) * cols] = flat[
+            pl.ds(d, n_bases, stride=pitch), :
+        ].astype(BF)
+    pairs = chunk // 8
+    low = lax.broadcasted_iota(jnp.int32, (pairs, 8, cols), 1) < 4
+    for row in range(0, lhs_ref.shape[0], chunk):
+        left = lhs_ref[row : row + chunk, :]
+        pair = row // 8
+        for first_octet in range(0, depth // 8, 2):
+            evens, odds = [], []
+            for octet in (first_octet, first_octet + 1):
+                out = jnp.dot(left, rights[octet], preferred_element_type=F32)
+                first = out[:, :cols].reshape(pairs, 8, cols)
+                second = out[:, cols:].reshape(pairs, 8, cols)
+                evens.append(jnp.where(low, first, pltpu.roll(second, 4, 1)))
+                odds.append(jnp.where(low, pltpu.roll(first, 4, 1), second))
+            at = slice(first_octet * 8, first_octet * 8 + 16)
+            w_ref[pair : pair + pairs, 0, at] = jnp.concatenate(evens, axis=1).astype(BF)
+            w_ref[pair : pair + pairs, 1, at] = jnp.concatenate(odds, axis=1).astype(BF)
 
 
 def mix(feat, lhs, bases, blocks, begin=0, end=None, earlier=None):
@@ -195,7 +185,7 @@
     per_part = cols // depth
 
     def bases_at(i, f):
-        return (0, lax.rem(jnp.minimum(i + begin, end - 1) + f[0] * per_part, steps), 0)
+        return (0, lax.rem(i + begin + f[0] * per_part, steps), 0)
 
     more = [] if earlier is None else [earlier]
     return pl.pallas_call(
@@ -203,7 +193,7 @@
         out_shape=jax.ShapeDtypeStruct((blocks // 2, 2, model_dim, cols), BF),
         grid_spec=pltpu.PrefetchScalarGridSpec(
             num_scalar_prefetch=1,
-            grid=(end - begin + 1,),
+            grid=(end - begin,),
             in_specs=[
                 pl.BlockSpec(lhs.shape, lambda i, f: (0, 0)),
                 pl.BlockSpec((n_bases, depth, cols), bases_at),
@@ -211,11 +201,11 @@
             + [pl.BlockSpec(memory_space=pl.ANY)] * len(more),
             out_specs=pl.BlockSpec(
                 (blocks // 2, 2, depth, cols),
-                lambda i, f: (0, 0, jnp.maximum(i - 1, 0) + begin, 0),
+                lambda i, f: (0, 0, i + begin, 0),
             ),
             scratch_shapes=[
                 pltpu.VMEM((n_bases, depth + 8, cols), F32),
-                pltpu.VMEM((2, depth // 8, 4 * n_bases, 2 * cols), BF),
+                pltpu.VMEM((depth // 8, 4 * n_bases, 2 * cols), BF),
             ],
         ),
         input_output_aliases={3: 0} if more else {},
@@ -252,7 +242,7 @@
 def blocks_kernel(*refs, group, owners, split, hubs):
     word_ref, src_hbm, dst_hbm = refs[:3]
     pieces, halves = refs[3:6], refs[6:8]
-    w_ref, out_ref, acc, deg, held, joined, src_ref, dst_ref, sems = refs[8:]
+    w_ref, out_hbm, acc, deg, held, joined, src_ref, dst_ref, out_ref, sems = refs[8:]
     spans = word_ref.shape[1] - TILE
     first_group = word_ref[0, spans] if hubs else 0
     end_group = word_ref[0, spans + int(hubs)]
@@ -286,7 +276,13 @@
         def _():
             fetch(here + 1)
 
-        pltpu.make_async_copy(w_ref.at[pl.ds(0, group)], held.at[side], sems.at[side]).wait()
+        def arrive():
+            pltpu.make_async_copy(
+                w_ref.at[pl.ds(0, group)], held.at[side], sems.at[side]
+            ).wait()
+
+        if not hubs:
+            arrive()
         slot = lax.broadcasted_iota(jnp.int32, (TILE, TILE), 0).astype(F32).astype(BF)
         lane = lax.broadcasted_iota(jnp.int32, (TILE, TILE), 1)
         one = jnp.ones((TILE, TILE), BF)
@@ -335,6 +331,8 @@
         for first in range(0, group, split):
             pairs = range(first, first + split)
             found = [adjacency(pair) for pair in pairs]
+            if hubs and first == 0:
+                arrive()
             messages = [message(pair) for pair in pairs]
             sums = [
                 jnp.dot(f[0], m, preferred_element_type=F32) for f, m in zip(found, messages)
@@ -358,6 +356,9 @@
         out_ref[at, :TILE, :] = acc[at].astype(BF)
         rows = jnp.where(line == 0, high, jnp.where(line == 1, low, 0.0))
         out_ref[at, TILE:, :] = rows.astype(BF)
+    leave = pltpu.make_async_copy(out_ref, out_hbm, sems.at[2])
+    leave.start()
+    leave.wait()
 
 
 def blocks_call(words, weights, edge_src, edge_dst, pieces, owners, hubs, group=16, split=16):
@@ -367,9 +368,9 @@
     anywhere = pl.BlockSpec(memory_space=pl.ANY)
     return pl.pallas_call(
         functools.partial(blocks_kernel, group=group, owners=owners, split=split, hubs=hubs),
-        out_shape=jax.ShapeDtypeStruct((owners, TILE + DEG_ROWS, cols), BF),
+        out_shape=pltpu.HBM((owners, TILE + DEG_ROWS, cols), BF),
         in_specs=[smem, anywhere, anywhere] + [vmem] * 3 + [anywhere] * 3,
-        out_specs=vmem,
+        out_specs=anywhere,
         scratch_shapes=[
             pltpu.VMEM((owners, TILE, cols), F32),
             pltpu.VMEM((TILE, TILE), F32),
@@ -377,6 +378,7 @@
             pltpu.VMEM(pieces[0].shape, BF),
             pltpu.VMEM(edge_src.shape, jnp.int32),
             pltpu.VMEM(edge_dst.shape, jnp.int32),
+            pltpu.VMEM((owners, TILE + DEG_ROWS, cols), BF),
             pltpu.SemaphoreType.DMA((6,)),
         ],
         cost_estimate=pl.CostEstimate(

time: 136 us -> 131 us (0.963)
  Pallas kernels: 81.7 us -> 71.8 us
  starting transfers between devices: 34.7 us -> 37.5 us
  waiting for transfers between devices: 16.6 us -> 19.4 us
    pallas_call x2, Pallas kernels: 30.7 us -> 21.6 us  [blocks_call(): pl.pallas_call(functools.partial(blocks_kernel, group=group, owners=owner...]
    all_to_all x1, starting transfers between devices: 19.6 us -> 22.5 us  [on_device(): lax.all_to_all(mirror_part, 'dom', split_axis=0, concat_axis=0, tiled=True)]
    all_to_all x1, waiting for transfers between devices: 7.32 us -> 9.73 us  [on_device(): lax.all_to_all(mirror_part, 'dom', split_axis=0, concat_axis=0, tiled=True)]
  transfers between devices with their start and end apart: 9 -> 9, of which waited for: 6 -> 6; matrix products, arithmetic and copies ran while one was open for 0% -> 0% of each run, Pallas kernels for 43% -> 44%
where the time goes in v7:
time: 131 us
  Pallas kernels  71.8 us (55%)
  starting transfers between devices  37.5 us (29%)
  waiting for transfers between devices  19.4 us (15%)
    pallas_call x2, Pallas kernels, mix(): pl.pallas_call(functools.partial(mix_kernel, chunk=512), out_shape=jax.Sh...  32.6 us
    all_to_all x1, starting transfers between devices, on_device(): lax.all_to_all(mirror_part, 'dom', split_axis=0, concat_axis=0, tiled=True)  22.5 us
    pallas_call x2, Pallas kernels, blocks_call(): pl.pallas_call(functools.partial(blocks_kernel, group=group, owners=owner...  21.6 us
    pallas_call x1, Pallas kernels, mirror_final(): pl.pallas_call(functools.partial(mirror_kernel, chunk=chunk, reach=n_loca...  12.8 us
    all_to_all x1, waiting for transfers between devices, on_device(): lax.all_to_all(mirror_part, 'dom', split_axis=0, concat_axis=0, tiled=True)  9.73 us
    all_to_all x1, waiting for transfers between devices, on_device(): lax.all_to_all(hub_part, 'dom', split_axis=0, concat_axis=0, tiled=True)  5.3 us
    ppermute x3, starting transfers between devices, from_others(): lax.ppermute(x, 'feat', [((i + shift) % size, i) for i in range(size)])  4.34 us
    all_to_all x1, starting transfers between devices, on_device(): lax.all_to_all(hub_part, 'dom', split_axis=0, concat_axis=0, tiled=True)  4.12 us
  transfers between devices with their start and end apart: 9, of which 6 were waited for; matrix products, arithmetic and copies ran while one was open for 0% of the time, Pallas kernels for 44%

profile of v7, /device:TPU:0, one launch (start us, length us, event | category | flops | bytes accessed | tf_op | source)
XLA Modules:
  0.0 130.5 jit_solution(2063069665447508460)
XLA Ops:
  0.0 1.7 %collective-permute-start.1 = (bf16[4096,128]{1,0:T(8,128)(2,1)}, bf16[4096,128]{1,0:T(8,128)(2,1)S(1)}, u32[]{:S(2)}, u32[]{:S(2)}) collective-permute-start(bf16[4096,128]{1,0:T(8,128)(2,1)} %x0_hbm.1), channel_id=1, source_target_pairs={{0,1},{1,2},{2,3},{3,0},{4,5},{5,6},{6,7},{7,4},{8,9},{9,10},{10,1... | collective-permute-start | bytes 3145736 | tf_op jit(solution)/shard_map/ppermute | solution.py:610
  1.7 1.6 %collective-permute-start = (bf16[4096,128]{1,0:T(8,128)(2,1)}, bf16[4096,128]{1,0:T(8,128)(2,1)S(1)}, u32[]{:S(2)}, u32[]{:S(2)}) collective-permute-start(bf16[4096,128]{1,0:T(8,128)(2,1)} %x0_hbm.1), channel_id=1, source_target_pairs={{1,0},{2,1},{3,2},{0,3},{5,4},{6,5},{7,6},{4,7},{9,8},{10,9},{11,1... | collective-permute-start | bytes 3145736 | tf_op jit(solution)/shard_map/ppermute | solution.py:609
  3.9 2.8 %prepare.1 = (s32[1,768]{1,0:T(1,128)S(1)}, bf16[2048,256]{1,0:T(8,128)(2,1)S(1)}) custom-call(s32[1]{0:T(128)S(6)} %copy.13.live_ref, s32[512,128]{1,0:T(8,128)} %refs_1_.3, s32[512,128]{1,0:T(8,128)} %refs_2_.3, s32[1,512]{1,0:T(1,128)} %bitcast.8, bf16[64,822]{1,0:T(8,128)(2,1)} %bitcast.7), custom_call_target="tpu_custom_call" | custom-call | tf_op jit(solution)/shard_map/prepare/pallas_call | solution.py:123
  6.7 18.0 %mix.1.rest_0_ = bf16[256,2,512,128]{3,2,1,0:T(8,128)(2,1)} custom-call(s32[1]{0:T(128)} %bitcast.feat_ref, bf16[2048,256]{1,0:T(8,128)(2,1)S(1)} %get-tuple-element.18.lhs_ref, bf16[64,512,128]{2,1,0:T(8,128)(2,1)} %bases_ref.3), custom_call_target="tpu_custom_call" | custom-call | flops 9663676416 | bytes 37748736 | tf_op jit(solution)/shard_map/mix/pallas_call | solution.py:191
  24.7 1.8 %collective-permute-done.1.refs_5_.x3_hbm = bf16[4096,128]{1,0:T(8,128)(2,1)S(1)} collective-permute-done((bf16[4096,128]{1,0:T(8,128)(2,1)}, bf16[4096,128]{1,0:T(8,128)(2,1)S(1)}, u32[]{:S(2)}, u32[]{:S(2)}) %collective-permute-start.1) | collective-permute-done | bytes 1048608 | tf_op jit(solution)/shard_map/ppermute | solution.py:610
  26.5 0.0 copy-start
  26.5 0.0 collective-permute-done.refs_4_.x1_hbm
  26.5 0.0 copy-start.1
  26.6 0.0 copy-start.2
  26.6 1.6 %collective-permute-start.3 = (bf16[2048,128]{1,0:T(8,128)(2,1)S(1)}, bf16[2048,128]{1,0:T(8,128)(2,1)S(1)}, u32[]{:S(2)}, u32[]{:S(2)}) collective-permute-start(bf16[2048,128]{1,0:T(8,128)(2,1)S(1)} %slice.7), channel_id=1, source_target_pairs={{0,1},{1,2},{2,3},{3,0},{4,5},{5,6},{6,7},{7,4},{8,9},{9,10},{10,1... | collective-permute-start | bytes 1572872 | tf_op jit(solution)/shard_map/ppermute | solution.py:621
  28.2 1.7 %collective-permute-start.2 = (bf16[2048,128]{1,0:T(8,128)(2,1)S(1)}, bf16[2048,128]{1,0:T(8,128)(2,1)S(1)}, u32[]{:S(2)}, u32[]{:S(2)}) collective-permute-start(bf16[2048,128]{1,0:T(8,128)(2,1)S(1)} %slice.6), channel_id=1, source_target_pairs={{1,0},{2,1},{3,2},{0,3},{5,4},{6,5},{7,6},{4,7},{9,8},{10,9},{11,1... | collective-permute-start | bytes 1572872 | tf_op jit(solution)/shard_map/ppermute | solution.py:620
  29.9 14.6 %mix_rest.1.refs_8_ = bf16[256,2,512,128]{3,2,1,0:T(8,128)(2,1)} custom-call(s32[1]{0:T(128)} %bitcast.feat_ref, bf16[2048,256]{1,0:T(8,128)(2,1)S(1)} %get-tuple-element.18.lhs_ref, bf16[64,512,128]{2,1,0:T(8,128)(2,1)} %bases_ref.3, bf16[256,2,512,128]{3,2,1,0:T(8,128)(2,1)} %mix.1.rest_0_), custom_call_target="tpu_custom_call", output_to_operand_aliasing={{}: (3, {})} | custom-call | flops 7516192768 | bytes 29360128 | tf_op jit(solution)/shard_map/mix_rest/pallas_call | solution.py:191
  44.5 0.0 collective-permute-done.3.refs_7_.second_hbm
  44.5 0.0 copy-start.6
  44.5 0.0 collective-permute-done.2.refs_6_.first_hbm
  44.5 0.0 copy-start.7
  44.5 0.8 copy-done.6
  45.3 0.1 copy-done.7
  45.5 0.0 copy-done.2
  45.5 13.0 %mirror_blocks.1 = bf16[32,144,128]{2,1,0:T(8,128)(2,1)} custom-call(s32[1,768]{1,0:T(1,128)S(1)} %get-tuple-element.17.refs_0_, s32[512,128]{1,0:T(8,128)} %refs_1_.3, s32[512,128]{1,0:T(8,128)} %refs_2_.3, bf16[4096,128]{1,0:T(8,128)(2,1)S(1)} %copy-done.2, bf16[4096,128]{1,0:T(8,128)(2,1)S(1)} %collective-permute-done.refs_4_.x1_hbm, ...), custom_call_target="tpu_custom_call" | custom-call | flops 8589934592 | bytes 33554432 | tf_op jit(solution)/shard_map/mirror_blocks/pallas_call | solution.py:369
  58.5 22.5 %all-to-all-start = ((bf16[32,144,128]{2,1,0:T(8,128)(2,1)}), bf16[32,144,128]{2,1,0:T(8,128)(2,1)}, u32[]{:S(2)}, u32[]{:S(2)}) async-start(bf16[32,144,128]{2,1,0:T(8,128)(2,1)} %mirror_blocks.1), calls=%async_computation | async-start | bytes 2359296 | tf_op jit(solution)/shard_map/all_to_all | solution.py:627
  81.0 0.0 copy-done
  81.0 0.0 copy-done.1
  81.0 8.6 %hub_blocks.1 = bf16[32,144,128]{2,1,0:T(8,128)(2,1)} custom-call(s32[1,768]{1,0:T(1,128)S(1)} %get-tuple-element.17.refs_0_, s32[512,128]{1,0:T(8,128)} %refs_1_.3, s32[512,128]{1,0:T(8,128)} %refs_2_.3, bf16[4096,128]{1,0:T(8,128)(2,1)S(1)} %copy-done.2, bf16[4096,128]{1,0:T(8,128)(2,1)S(1)} %collective-permute-done.refs_4_.x1_hbm, ...), custom_call_target="tpu_custom_call" | custom-call | flops 8589934592 | bytes 33554432 | tf_op jit(solution)/shard_map/hub_blocks/pallas_call | solution.py:369
  89.6 0.0 copy-start.4
  89.6 0.0 copy-start.5
  89.6 9.7 %all-to-all-done.mirror_hbm = bf16[32,144,128]{2,1,0:T(8,128)(2,1)} async-done(((bf16[32,144,128]{2,1,0:T(8,128)(2,1)}), bf16[32,144,128]{2,1,0:T(8,128)(2,1)}, u32[]{:S(2)}, u32[]{:S(2)}) %all-to-all-start) | async-done | bytes 1179680 | tf_op jit(solution)/shard_map/all_to_all | solution.py:627
  99.3 4.1 %all-to-all-start.1 = ((bf16[32,144,128]{2,1,0:T(8,128)(2,1)}), bf16[32,144,128]{2,1,0:T(8,128)(2,1)S(1)}, u32[]{:S(2)}, u32[]{:S(2)}) async-start(bf16[32,144,128]{2,1,0:T(8,128)(2,1)} %hub_blocks.1), calls=%async_computation.1 | async-start | bytes 2359296 | tf_op jit(solution)/shard_map/all_to_all | solution.py:631
  103.5 0.0 copy-done.4
  103.5 0.0 copy-done.5
  103.5 12.8 %mirror_final.1 = (f32[4096,128]{1,0:T(8,128)S(1)}, f32[32,128]{1,0:T(8,128)S(1)}) custom-call(s32[1]{0:T(128)} %bitcast.feat_ref, bf16[32,144,128]{2,1,0:T(8,128)(2,1)} %all-to-all-done.mirror_hbm, s32[32,128]{1,0:T(8,128)S(1)} %bitcast.6, bf16[512,128]{1,0:T(8,128)(2,1)S(1)} %copy-done.4, bf16[4096,128]{1,0:T(8,128)(2,1)} %x0_hbm.1, ...), custom_call_target="tpu_custom_call" | custom-call | flops 8589934592 | bytes 8388608 | tf_op jit(solution)/shard_map/mirror_final/pallas_call | solution.py:500
  116.3 0.0 copy-start.3
  116.3 5.3 %all-to-all-done.1.hub_ref = bf16[32,144,128]{2,1,0:T(8,128)(2,1)S(1)} async-done(((bf16[32,144,128]{2,1,0:T(8,128)(2,1)}), bf16[32,144,128]{2,1,0:T(8,128)(2,1)S(1)}, u32[]{:S(2)}, u32[]{:S(2)}) %all-to-all-start.1) | async-done | bytes 1179680 | tf_op jit(solution)/shard_map/all_to_all | solution.py:631
  121.6 0.3 hub_final.1
  122.0 0.4 collective-permute-start.6
  122.4 2.8 %collective-permute-start.5 = (f32[32,128]{1,0:T(8,128)S(1)}, f32[32,128]{1,0:T(8,128)S(1)}, u32[]{:S(2)}, u32[]{:S(2)}) collective-permute-start(f32[32,128]{1,0:T(8,128)S(1)} %get-tuple-element.28.a_ref), channel_id=1, source_target_pairs={{2,0},{3,1},{0,2},{1,3},{6,4},{7,5},{4,6},{5,7},{10,8},{11,9},{8,1... | collective-permute-start | bytes 49160 | tf_op jit(solution)/shard_map/ppermute | solution.py:583
  125.2 1.1 collective-permute-start.4
  126.3 0.6 collective-permute-done.6.d_ref
  127.0 0.7 collective-permute-done.5.c_ref
  127.6 1.3 %collective-permute-done.4.b_ref = f32[32,128]{1,0:T(8,128)S(1)} collective-permute-done((f32[32,128]{1,0:T(8,128)S(1)}, f32[32,128]{1,0:T(8,128)S(1)}, u32[]{:S(2)}, u32[]{:S(2)}) %collective-permute-start.4) | collective-permute-done | bytes 16416 | tf_op jit(solution)/shard_map/ppermute | solution.py:583
  128.9 0.0 copy-done.3
  128.9 1.6 %scale.1 = bf16[4096,128]{1,0:T(8,128)(2,1)} custom-call(f32[4096,128]{1,0:T(8,128)S(1)} %get-tuple-element.24.mixed_ref, f32[128,128]{1,0:T(8,128)S(1)} %get-tuple-element.27.hub_ref, f32[32,128]{1,0:T(8,128)S(1)} %get-tuple-element.28.a_ref, f32[32,128]{1,0:T(8,128)S(1)} %collective-permute-done.4.b_ref, f32[32,128]{1,0:T(8,128)S(1)} %collective-permute-done.5.c_ref, ...), custom_call_target="tpu_custom_call" | custom-call | tf_op jit(solution)/shard_map/scale/pallas_call | solution.py:571
  (2 shorter events, 0.1 us)
Async XLA Ops:
  0.0 26.5 %collective-permute-start.1 = (bf16[4096,128]{1,0:T(8,128)(2,1)}, bf16[4096,128]{1,0:T(8,128)(2,1)S(1)}, u32[]{:S(2)}, u32[]{:S(2)}) collective-permute-start(bf16[4096,128]{1,0:T(8,128)(2,1)} %x0_hbm.1), channel_id=1, source_target_pairs={{0,1},{1,2},{2,3},{3,0},{4,5},{5,6},{6,7},{7,4},{8,9},{9,10},{10,1... | collective-permute-start | bytes 3145736 | tf_op jit(solution)/shard_map/ppermute | solution.py:610
  1.7 24.8 %collective-permute-start = (bf16[4096,128]{1,0:T(8,128)(2,1)}, bf16[4096,128]{1,0:T(8,128)(2,1)S(1)}, u32[]{:S(2)}, u32[]{:S(2)}) collective-permute-start(bf16[4096,128]{1,0:T(8,128)(2,1)} %x0_hbm.1), channel_id=1, source_target_pairs={{1,0},{2,1},{3,2},{0,3},{5,4},{6,5},{7,6},{4,7},{9,8},{10,9},{11,1... | collective-permute-start | bytes 3145736 | tf_op jit(solution)/shard_map/ppermute | solution.py:609
  26.5 54.5 %copy-start = (bf16[4096,128]{1,0:T(8,128)(2,1)}, bf16[4096,128]{1,0:T(8,128)(2,1)S(1)}, u32[]{:S(2)}) copy-start(bf16[4096,128]{1,0:T(8,128)(2,1)S(1)} %collective-permute-done.1.refs_5_.x3_hbm) | copy-start | bytes 3145732
  26.5 54.5 %copy-start.1 = (bf16[4096,128]{1,0:T(8,128)(2,1)}, bf16[4096,128]{1,0:T(8,128)(2,1)S(1)}, u32[]{:S(2)}) copy-start(bf16[4096,128]{1,0:T(8,128)(2,1)S(1)} %collective-permute-done.refs_4_.x1_hbm) | copy-start | bytes 3145732
  26.6 18.9 %copy-start.2 = (bf16[4096,128]{1,0:T(8,128)(2,1)S(1)}, bf16[4096,128]{1,0:T(8,128)(2,1)}, u32[]{:S(2)}) copy-start(bf16[4096,128]{1,0:T(8,128)(2,1)} %x0_hbm.1) | copy-start | bytes 3145732
  26.6 17.9 %collective-permute-start.3 = (bf16[2048,128]{1,0:T(8,128)(2,1)S(1)}, bf16[2048,128]{1,0:T(8,128)(2,1)S(1)}, u32[]{:S(2)}, u32[]{:S(2)}) collective-permute-start(bf16[2048,128]{1,0:T(8,128)(2,1)S(1)} %slice.7), channel_id=1, source_target_pairs={{0,1},{1,2},{2,3},{3,0},{4,5},{5,6},{6,7},{7,4},{8,9},{9,10},{10,1... | collective-permute-start | bytes 1572872 | tf_op jit(solution)/shard_map/ppermute | solution.py:621
  28.2 16.3 %collective-permute-start.2 = (bf16[2048,128]{1,0:T(8,128)(2,1)S(1)}, bf16[2048,128]{1,0:T(8,128)(2,1)S(1)}, u32[]{:S(2)}, u32[]{:S(2)}) collective-permute-start(bf16[2048,128]{1,0:T(8,128)(2,1)S(1)} %slice.6), channel_id=1, source_target_pairs={{1,0},{2,1},{3,2},{0,3},{5,4},{6,5},{7,6},{4,7},{9,8},{10,9},{11,1... | collective-permute-start | bytes 1572872 | tf_op jit(solution)/shard_map/ppermute | solution.py:620
  44.5 0.8 copy-start.6
  44.5 1.0 copy-start.7
  58.5 40.8 %all-to-all-start = ((bf16[32,144,128]{2,1,0:T(8,128)(2,1)}), bf16[32,144,128]{2,1,0:T(8,128)(2,1)}, u32[]{:S(2)}, u32[]{:S(2)}) async-start(bf16[32,144,128]{2,1,0:T(8,128)(2,1)} %mirror_blocks.1), calls=%async_computation | async-start | bytes 2359296 | tf_op jit(solution)/shard_map/all_to_all | solution.py:627
  89.6 13.9 %copy-start.4 = (bf16[512,128]{1,0:T(8,128)(2,1)S(1)}, bf16[512,128]{1,0:T(8,128)(2,1)}, u32[]{:S(2)}) copy-start(bf16[512,128]{1,0:T(8,128)(2,1)} %self_ref.1) | copy-start | bytes 393220
  89.6 13.9 %copy-start.5 = (s32[4096]{0:T(1024)S(1)}, s32[4096]{0:T(1024)}, u32[]{:S(2)}) copy-start(s32[4096]{0:T(1024)} %param.18) | copy-start | bytes 49156
  99.3 22.3 %all-to-all-start.1 = ((bf16[32,144,128]{2,1,0:T(8,128)(2,1)}), bf16[32,144,128]{2,1,0:T(8,128)(2,1)S(1)}, u32[]{:S(2)}, u32[]{:S(2)}) async-start(bf16[32,144,128]{2,1,0:T(8,128)(2,1)} %hub_blocks.1), calls=%async_computation.1 | async-start | bytes 2359296 | tf_op jit(solution)/shard_map/all_to_all | solution.py:631
  116.3 12.6 %copy-start.3 = (f32[128]{0:T(128)S(1)}, f32[128]{0:T(128)}, u32[]{:S(2)}) copy-start(f32[128]{0:T(128)} %param.14) | copy-start | bytes 1540
  122.0 5.0 %collective-permute-start.6 = (f32[32,128]{1,0:T(8,128)S(1)}, f32[32,128]{1,0:T(8,128)S(1)}, u32[]{:S(2)}, u32[]{:S(2)}) collective-permute-start(f32[32,128]{1,0:T(8,128)S(1)} %get-tuple-element.28.a_ref), channel_id=1, source_target_pairs={{3,0},{0,1},{1,2},{2,3},{7,4},{4,5},{5,6},{6,7},{11,8},{8,9},{9,10... | collective-permute-start | bytes 49160 | tf_op jit(solution)/shard_map/ppermute | solution.py:583
  122.4 5.2 %collective-permute-start.5 = (f32[32,128]{1,0:T(8,128)S(1)}, f32[32,128]{1,0:T(8,128)S(1)}, u32[]{:S(2)}, u32[]{:S(2)}) collective-permute-start(f32[32,128]{1,0:T(8,128)S(1)} %get-tuple-element.28.a_ref), channel_id=1, source_target_pairs={{2,0},{3,1},{0,2},{1,3},{6,4},{7,5},{4,6},{5,7},{10,8},{11,9},{8,1... | collective-permute-start | bytes 49160 | tf_op jit(solution)/shard_map/ppermute | solution.py:583
  125.2 3.7 %collective-permute-start.4 = (f32[32,128]{1,0:T(8,128)S(1)}, f32[32,128]{1,0:T(8,128)S(1)}, u32[]{:S(2)}, u32[]{:S(2)}) collective-permute-start(f32[32,128]{1,0:T(8,128)S(1)} %get-tuple-element.28.a_ref), channel_id=1, source_target_pairs={{1,0},{2,1},{3,2},{0,3},{5,4},{6,5},{7,6},{4,7},{9,8},{10,9},{11,1... | collective-permute-start | bytes 49160 | tf_op jit(solution)/shard_map/ppermute | solution.py:583

commit v8 on v7

--- a/solution.py
+++ b/solution.py
@@ -241,8 +241,10 @@
 
 def blocks_kernel(*refs, group, owners, split, hubs):
     word_ref, src_hbm, dst_hbm = refs[:3]
-    pieces, halves = refs[3:6], refs[6:8]
-    w_ref, out_hbm, acc, deg, held, joined, src_ref, dst_ref, out_ref, sems = refs[8:]
+    pieces, halves, w_ref = refs[3:6], refs[6:8], refs[8]
+    n_out = 2 if hubs else 1
+    out_hbms = refs[9 : 9 + n_out]
+    acc, deg, held, joined, src_ref, dst_ref, out_ref, sems = refs[9 + n_out :]
     spans = word_ref.shape[1] - TILE
     first_group = word_ref[0, spans] if hubs else 0
     end_group = word_ref[0, spans + int(hubs)]
@@ -349,16 +351,24 @@
 
     deg[...] = deg[...].T
     line = lax.broadcasted_iota(jnp.int32, (DEG_ROWS, TILE), 0)
-    for at in range(owners):
-        degree = deg[at : at + 1, :]
+    core = lax.axis_index("dom") & 1 if hubs else 0
+    each = owners // n_out
+    for i in range(owners):
+        at = n_out * (i % each) + ((core ^ (i // each)) if hubs else 0)
+        degree = deg[pl.ds(at, 1), :]
         high = jnp.floor(degree * (1.0 / 256.0)) * 256.0
         low = degree - high
-        out_ref[at, :TILE, :] = acc[at].astype(BF)
+        out_ref[i, :TILE, :] = acc[at].astype(BF)
         rows = jnp.where(line == 0, high, jnp.where(line == 1, low, 0.0))
-        out_ref[at, TILE:, :] = rows.astype(BF)
-    leave = pltpu.make_async_copy(out_ref, out_hbm, sems.at[2])
-    leave.start()
-    leave.wait()
+        out_ref[i, TILE:, :] = rows.astype(BF)
+    leaves = [
+        pltpu.make_async_copy(out_ref.at[pl.ds(i * each, each)], out, sems.at[2 + i])
+        for i, out in enumerate(out_hbms)
+    ]
+    for leave in leaves:
+        leave.start()
+    for leave in leaves:
+        leave.wait()
 
 
 def blocks_call(words, weights, edge_src, edge_dst, pieces, owners, hubs, group=16, split=16):
@@ -368,9 +378,11 @@
     anywhere = pl.BlockSpec(memory_space=pl.ANY)
     return pl.pallas_call(
         functools.partial(blocks_kernel, group=group, owners=owners, split=split, hubs=hubs),
-        out_shape=pltpu.HBM((owners, TILE + DEG_ROWS, cols), BF),
+        out_shape=(jax.ShapeDtypeStruct((owners // 2, TILE + DEG_ROWS, cols), BF),) * 2
+        if hubs
+        else (pltpu.HBM((owners, TILE + DEG_ROWS, cols), BF),),
         in_specs=[smem, anywhere, anywhere] + [vmem] * 3 + [anywhere] * 3,
-        out_specs=anywhere,
+        out_specs=(anywhere,) * (2 if hubs else 1),
         scratch_shapes=[
             pltpu.VMEM((owners, TILE, cols), F32),
             pltpu.VMEM((TILE, TILE), F32),
@@ -612,7 +624,7 @@
     words, lhs = prepare(
         block_count, edge_src, edge_dst, block_rel, basis_coef, owners, n_local // TILE, 16
     )
-    steps = 9
+    steps = 10
     weights = mix(feat_at, lhs, bases, blocks, 0, steps)
     weights, after, before = lax.optimization_barrier((weights, after, before))
     half = n_local // 2
@@ -623,12 +635,21 @@
     weights = mix(feat_at, lhs, bases, blocks, steps, None, weights)
     pieces = [embeddings, after, before] + halves
     edges = (edge_src, edge_dst)
-    mirror_part = blocks_call(words, weights, *edges, pieces, owners, False)
+    (mirror_part,) = blocks_call(words, weights, *edges, pieces, owners, False)
     mirror = lax.all_to_all(mirror_part, "dom", split_axis=0, concat_axis=0, tiled=True)
     weights, _ = lax.optimization_barrier((weights, mirror_part))
-    hub_part = blocks_call(words, weights, *edges, pieces, owners, True)
+    kept, sent = blocks_call(words, weights, *edges, pieces, owners, True)
+    came = lax.ppermute(sent, "dom", [(i, i ^ 1) for i in range(owners)])
+    hub_part = (kept.astype(F32) + came.astype(F32)).astype(BF)
     hub_part, mirror = lax.optimization_barrier((hub_part, mirror))
-    hub = lax.all_to_all(hub_part, "dom", split_axis=0, concat_axis=0, tiled=True)
+    hub = lax.all_to_all(
+        hub_part,
+        "dom",
+        split_axis=0,
+        concat_axis=0,
+        tiled=True,
+        axis_index_groups=[list(range(c, owners, 2)) for c in range(2)],
+    )
 
     mixed, squares = mirror_final(
         feat.reshape(1), mirror, mirror_master_rows.reshape(owners, TILE), self_weight, pieces

time: 131 us -> 126 us (0.962)
  waiting for transfers between devices: 19.4 us -> 5.86 us
  starting transfers between devices: 37.5 us -> 46.2 us
  Pallas kernels: 71.8 us -> 69.7 us
    all_to_all x1, waiting for transfers between devices: 9.73 us -> 1.36 us  [on_device(): lax.all_to_all(mirror_part, 'dom', split_axis=0, concat_axis=0, tiled=True)]
    ppermute x0 -> x1, starting transfers between devices: none -> 6.55 us  [on_device(): came = lax.ppermute(sent, 'dom', [(i, i ^ 1) for i in range(owners)])]
    all_to_all x1, waiting for transfers between devices: 5.3 us -> 0.01 us  [on_device(): lax.all_to_all(hub_part, 'dom', split_axis=0, concat_axis=0, tiled=True,...]
    pallas_call x2, Pallas kernels: 21.6 us -> 20 us  [blocks_call(): pl.pallas_call(functools.partial(blocks_kernel, group=group, owners=owner...]
    ppermute x0 -> x1, waiting for transfers between devices: none -> 1.63 us  [on_device(): came = lax.ppermute(sent, 'dom', [(i, i ^ 1) for i in range(owners)])]
    ppermute x1, waiting for transfers between devices: 1.76 us -> 0.23 us  [on_device(): before = lax.ppermute(embeddings, 'feat', behind)]
    all_to_all x1, starting transfers between devices: 4.12 us -> 5.64 us  [on_device(): lax.all_to_all(hub_part, 'dom', split_axis=0, concat_axis=0, tiled=True,...]
  transfers between devices with their start and end apart: 9 -> 10, of which waited for: 6 -> 6; matrix products, arithmetic and copies ran while one was open for 0% -> 1% of each run, Pallas kernels for 44% -> 45%
where the time goes in v8:
time: 126 us; the launch traced here: 125 us
  Pallas kernels  69.7 us (55%)
  starting transfers between devices  46.2 us (37%)
  waiting for transfers between devices  5.86 us (5%)
    pallas_call x2, Pallas kernels, mix(): pl.pallas_call(functools.partial(mix_kernel, chunk=512), out_shape=jax.Sh...  32.3 us
    all_to_all x1, starting transfers between devices, on_device(): lax.all_to_all(mirror_part, 'dom', split_axis=0, concat_axis=0, tiled=True)  23.4 us
    pallas_call x2, Pallas kernels, blocks_call(): pl.pallas_call(functools.partial(blocks_kernel, group=group, owners=owner...  20 us
    pallas_call x1, Pallas kernels, mirror_final(): pl.pallas_call(functools.partial(mirror_kernel, chunk=chunk, reach=n_loca...  12.8 us
    ppermute x1, starting transfers between devices, on_device(): came = lax.ppermute(sent, 'dom', [(i, i ^ 1) for i in range(owners)])  6.55 us
    all_to_all x1, starting transfers between devices, on_device(): lax.all_to_all(hub_part, 'dom', split_axis=0, concat_axis=0, tiled=True,...  5.64 us
    ppermute x3, starting transfers between devices, from_others(): lax.ppermute(x, 'feat', [((i + shift) % size, i) for i in range(size)])  4.1 us
    pallas_call x1, Pallas kernels, prepare(): pl.pallas_call(functools.partial(prepare_kernel, owners=owners, src_tiles...  2.76 us
  transfers between devices with their start and end apart: 10, of which 6 were waited for; matrix products, arithmetic and copies ran while one was open for 1% of the time, Pallas kernels for 45%

profile of v8, /device:TPU:0, one launch (start us, length us, event | category | flops | bytes accessed | tf_op | source)
XLA Modules:
  0.0 124.6 jit_solution(12011865213148189522)
XLA Ops:
  0.0 1.7 %collective-permute-start.1 = (bf16[4096,128]{1,0:T(8,128)(2,1)}, bf16[4096,128]{1,0:T(8,128)(2,1)S(1)}, u32[]{:S(2)}, u32[]{:S(2)}) collective-permute-start(bf16[4096,128]{1,0:T(8,128)(2,1)} %x0_hbm.1), channel_id=1, source_target_pairs={{0,1},{1,2},{2,3},{3,0},{4,5},{5,6},{6,7},{7,4},{8,9},{9,10},{10,1... | collective-permute-start | bytes 3145736 | tf_op jit(solution)/shard_map/ppermute | solution.py:622
  1.7 1.6 %collective-permute-start = (bf16[4096,128]{1,0:T(8,128)(2,1)}, bf16[4096,128]{1,0:T(8,128)(2,1)S(1)}, u32[]{:S(2)}, u32[]{:S(2)}) collective-permute-start(bf16[4096,128]{1,0:T(8,128)(2,1)} %x0_hbm.1), channel_id=1, source_target_pairs={{1,0},{2,1},{3,2},{0,3},{5,4},{6,5},{7,6},{4,7},{9,8},{10,9},{11,1... | collective-permute-start | bytes 3145736 | tf_op jit(solution)/shard_map/ppermute | solution.py:621
  3.9 2.8 %prepare.1 = (s32[1,768]{1,0:T(1,128)S(1)}, bf16[2048,256]{1,0:T(8,128)(2,1)S(1)}) custom-call(s32[1]{0:T(128)S(6)} %copy.13.live_ref, s32[512,128]{1,0:T(8,128)} %refs_1_.3, s32[512,128]{1,0:T(8,128)} %refs_2_.3, s32[1,512]{1,0:T(1,128)} %bitcast.8, bf16[64,822]{1,0:T(8,128)(2,1)} %bitcast.7), custom_call_target="tpu_custom_call" | custom-call | tf_op jit(solution)/shard_map/prepare/pallas_call | solution.py:123
  6.7 19.6 %mix.1.rest_0_ = bf16[256,2,512,128]{3,2,1,0:T(8,128)(2,1)} custom-call(s32[1]{0:T(128)} %bitcast.feat_ref, bf16[2048,256]{1,0:T(8,128)(2,1)S(1)} %get-tuple-element.20.lhs_ref, bf16[64,512,128]{2,1,0:T(8,128)(2,1)} %bases_ref.3), custom_call_target="tpu_custom_call" | custom-call | flops 10737418240 | bytes 41943040 | tf_op jit(solution)/shard_map/mix/pallas_call | solution.py:191
  26.2 0.2 collective-permute-done.1.refs_5_.x3_hbm
  26.5 0.0 copy-start
  26.5 0.0 collective-permute-done.refs_4_.x1_hbm
  26.5 0.0 copy-start.1
  26.6 0.0 copy-start.2
  26.6 1.6 %collective-permute-start.3 = (bf16[2048,128]{1,0:T(8,128)(2,1)S(1)}, bf16[2048,128]{1,0:T(8,128)(2,1)S(1)}, u32[]{:S(2)}, u32[]{:S(2)}) collective-permute-start(bf16[2048,128]{1,0:T(8,128)(2,1)S(1)} %slice.7), channel_id=1, source_target_pairs={{0,1},{1,2},{2,3},{3,0},{4,5},{5,6},{6,7},{7,4},{8,9},{9,10},{10,1... | collective-permute-start | bytes 1572872 | tf_op jit(solution)/shard_map/ppermute | solution.py:633
  28.2 1.7 %collective-permute-start.2 = (bf16[2048,128]{1,0:T(8,128)(2,1)S(1)}, bf16[2048,128]{1,0:T(8,128)(2,1)S(1)}, u32[]{:S(2)}, u32[]{:S(2)}) collective-permute-start(bf16[2048,128]{1,0:T(8,128)(2,1)S(1)} %slice.6), channel_id=1, source_target_pairs={{1,0},{2,1},{3,2},{0,3},{5,4},{6,5},{7,6},{4,7},{9,8},{10,9},{11,1... | collective-permute-start | bytes 1572872 | tf_op jit(solution)/shard_map/ppermute | solution.py:632
  29.9 12.7 %mix_rest.1.refs_8_ = bf16[256,2,512,128]{3,2,1,0:T(8,128)(2,1)} custom-call(s32[1]{0:T(128)} %bitcast.feat_ref, bf16[2048,256]{1,0:T(8,128)(2,1)S(1)} %get-tuple-element.20.lhs_ref, bf16[64,512,128]{2,1,0:T(8,128)(2,1)} %bases_ref.3, bf16[256,2,512,128]{3,2,1,0:T(8,128)(2,1)} %mix.1.rest_0_), custom_call_target="tpu_custom_call", output_to_operand_aliasing={{}: (3, {})} | custom-call | flops 6442450944 | bytes 25165824 | tf_op jit(solution)/shard_map/mix_rest/pallas_call | solution.py:191
  42.6 0.0 collective-permute-done.3.refs_7_.second_hbm
  42.6 0.0 copy-start.6
  42.6 0.0 collective-permute-done.2.refs_6_.first_hbm
  42.6 0.0 copy-start.7
  42.6 0.8 copy-done.6
  43.4 0.2 copy-done.7
  43.6 0.0 copy-done.2
  43.6 12.2 %mirror_blocks.1 = bf16[32,144,128]{2,1,0:T(8,128)(2,1)} custom-call(s32[1,768]{1,0:T(1,128)S(1)} %get-tuple-element.19.refs_0_, s32[512,128]{1,0:T(8,128)} %refs_1_.3, s32[512,128]{1,0:T(8,128)} %refs_2_.3, bf16[4096,128]{1,0:T(8,128)(2,1)S(1)} %copy-done.2, bf16[4096,128]{1,0:T(8,128)(2,1)S(1)} %collective-permute-done.refs_4_.x1_hbm, ...), custom_call_target="tpu_custom_call" | custom-call | flops 8589934592 | bytes 33554432 | tf_op jit(solution)/shard_map/mirror_blocks/pallas_call | solution.py:379
  55.8 23.4 %all-to-all-start = ((bf16[32,144,128]{2,1,0:T(8,128)(2,1)}), bf16[32,144,128]{2,1,0:T(8,128)(2,1)}, u32[]{:S(2)}, u32[]{:S(2)}) async-start(bf16[32,144,128]{2,1,0:T(8,128)(2,1)} %mirror_blocks.1), calls=%async_computation | async-start | bytes 2359296 | tf_op jit(solution)/shard_map/all_to_all | solution.py:639
  79.2 0.0 copy-done
  79.2 0.0 copy-done.1
  79.2 7.8 %hub_blocks.1 = (bf16[16,144,128]{2,1,0:T(8,128)(2,1)S(1)}, bf16[16,144,128]{2,1,0:T(8,128)(2,1)S(1)}) custom-call(s32[1,768]{1,0:T(1,128)S(1)} %get-tuple-element.19.refs_0_, s32[512,128]{1,0:T(8,128)} %refs_1_.3, s32[512,128]{1,0:T(8,128)} %refs_2_.3, bf16[4096,128]{1,0:T(8,128)(2,1)S(1)} %copy-done.2, ...), custom_call_target="tpu_custom_call" | custom-call | flops 8589934592 | bytes 33554432 | tf_op jit(solution)/shard_map/hub_blocks/pallas_call | solution.py:379
  87.0 6.6 %collective-permute-start.4 = (bf16[16,144,128]{2,1,0:T(8,128)(2,1)S(1)}, bf16[16,144,128]{2,1,0:T(8,128)(2,1)S(1)}, u32[]{:S(2)}, u32[]{:S(2)}) collective-permute-start(bf16[16,144,128]{2,1,0:T(8,128)(2,1)S(1)} %get-tuple-element.26), channel_id=1, source_target_pairs={{0,4},{4,0},{8,12},{12,8},{16,20},{20,16},{24,28},{28,24},{32,36},... | collective-permute-start | bytes 1769480 | tf_op jit(solution)/shard_map/ppermute | solution.py:642
  93.5 1.6 %collective-permute-done.4 = bf16[16,144,128]{2,1,0:T(8,128)(2,1)S(1)} collective-permute-done((bf16[16,144,128]{2,1,0:T(8,128)(2,1)S(1)}, bf16[16,144,128]{2,1,0:T(8,128)(2,1)S(1)}, u32[]{:S(2)}, u32[]{:S(2)}) %collective-permute-start.4) | collective-permute-done | bytes 589856 | tf_op jit(solution)/shard_map/ppermute | solution.py:642
  95.2 0.0 copy-start.4
  95.2 0.0 copy-start.5
  95.2 1.0 add_convert_fusion
  96.2 1.4 %all-to-all-done.mirror_hbm = bf16[32,144,128]{2,1,0:T(8,128)(2,1)} async-done(((bf16[32,144,128]{2,1,0:T(8,128)(2,1)}), bf16[32,144,128]{2,1,0:T(8,128)(2,1)}, u32[]{:S(2)}, u32[]{:S(2)}) %all-to-all-start) | async-done | bytes 1179680 | tf_op jit(solution)/shard_map/all_to_all | solution.py:639
  97.5 5.6 %all-to-all-start.1 = ((bf16[16,144,128]{2,1,0:T(8,128)(2,1)}), bf16[16,144,128]{2,1,0:T(8,128)(2,1)S(1)}, u32[]{:S(2)}, u32[]{:S(2)}) async-start(bf16[16,144,128]{2,1,0:T(8,128)(2,1)} %add_convert_fusion), calls=%async_computation.1 | async-start | bytes 1179648 | tf_op jit(solution)/shard_map/all_to_all | solution.py:645
  103.2 0.0 copy-done.4
  103.2 0.0 copy-done.5
  103.2 12.8 %mirror_final.1 = (f32[4096,128]{1,0:T(8,128)S(1)}, f32[32,128]{1,0:T(8,128)S(1)}) custom-call(s32[1]{0:T(128)} %bitcast.feat_ref, bf16[32,144,128]{2,1,0:T(8,128)(2,1)} %all-to-all-done.mirror_hbm, s32[32,128]{1,0:T(8,128)S(1)} %bitcast.6, bf16[512,128]{1,0:T(8,128)(2,1)S(1)} %copy-done.4, bf16[4096,128]{1,0:T(8,128)(2,1)} %x0_hbm.1, ...), custom_call_target="tpu_custom_call" | custom-call | flops 8589934592 | bytes 8388608 | tf_op jit(solution)/shard_map/mirror_final/pallas_call | solution.py:512
  116.0 0.0 all-to-all-done.1.hub_ref
  116.0 0.0 copy-start.3
  116.0 0.3 hub_final.1
  116.3 0.1 collective-permute-start.7
  116.5 2.8 %collective-permute-start.6 = (f32[32,128]{1,0:T(8,128)S(1)}, f32[32,128]{1,0:T(8,128)S(1)}, u32[]{:S(2)}, u32[]{:S(2)}) collective-permute-start(f32[32,128]{1,0:T(8,128)S(1)} %get-tuple-element.32.a_ref), channel_id=1, source_target_pairs={{2,0},{3,1},{0,2},{1,3},{6,4},{7,5},{4,6},{5,7},{10,8},{11,9},{8,1... | collective-permute-start | bytes 49160 | tf_op jit(solution)/shard_map/ppermute | solution.py:595
  119.3 1.1 collective-permute-start.5
  120.5 0.9 collective-permute-done.7.d_ref
  121.3 0.4 collective-permute-done.6.c_ref
  121.7 1.3 %collective-permute-done.5.b_ref = f32[32,128]{1,0:T(8,128)S(1)} collective-permute-done((f32[32,128]{1,0:T(8,128)S(1)}, f32[32,128]{1,0:T(8,128)S(1)}, u32[]{:S(2)}, u32[]{:S(2)}) %collective-permute-start.5) | collective-permute-done | bytes 16416 | tf_op jit(solution)/shard_map/ppermute | solution.py:595
  123.1 0.0 copy-done.3
  123.1 1.6 %scale.1 = bf16[4096,128]{1,0:T(8,128)(2,1)} custom-call(f32[4096,128]{1,0:T(8,128)S(1)} %get-tuple-element.28.mixed_ref, f32[128,128]{1,0:T(8,128)S(1)} %get-tuple-element.31.hub_ref, f32[32,128]{1,0:T(8,128)S(1)} %get-tuple-element.32.a_ref, f32[32,128]{1,0:T(8,128)S(1)} %collective-permute-done.5.b_ref, f32[32,128]{1,0:T(8,128)S(1)} %collective-permute-done.6.c_ref, ...), custom_call_target="tpu_custom_call" | custom-call | tf_op jit(solution)/shard_map/scale/pallas_call | solution.py:583
  (2 shorter events, 0.1 us)
Async XLA Ops:
  0.0 26.5 %collective-permute-start.1 = (bf16[4096,128]{1,0:T(8,128)(2,1)}, bf16[4096,128]{1,0:T(8,128)(2,1)S(1)}, u32[]{:S(2)}, u32[]{:S(2)}) collective-permute-start(bf16[4096,128]{1,0:T(8,128)(2,1)} %x0_hbm.1), channel_id=1, source_target_pairs={{0,1},{1,2},{2,3},{3,0},{4,5},{5,6},{6,7},{7,4},{8,9},{9,10},{10,1... | collective-permute-start | bytes 3145736 | tf_op jit(solution)/shard_map/ppermute | solution.py:622
  1.7 24.8 %collective-permute-start = (bf16[4096,128]{1,0:T(8,128)(2,1)}, bf16[4096,128]{1,0:T(8,128)(2,1)S(1)}, u32[]{:S(2)}, u32[]{:S(2)}) collective-permute-start(bf16[4096,128]{1,0:T(8,128)(2,1)} %x0_hbm.1), channel_id=1, source_target_pairs={{1,0},{2,1},{3,2},{0,3},{5,4},{6,5},{7,6},{4,7},{9,8},{10,9},{11,1... | collective-permute-start | bytes 3145736 | tf_op jit(solution)/shard_map/ppermute | solution.py:621
  26.5 52.7 %copy-start = (bf16[4096,128]{1,0:T(8,128)(2,1)}, bf16[4096,128]{1,0:T(8,128)(2,1)S(1)}, u32[]{:S(2)}) copy-start(bf16[4096,128]{1,0:T(8,128)(2,1)S(1)} %collective-permute-done.1.refs_5_.x3_hbm) | copy-start | bytes 3145732
  26.5 52.7 %copy-start.1 = (bf16[4096,128]{1,0:T(8,128)(2,1)}, bf16[4096,128]{1,0:T(8,128)(2,1)S(1)}, u32[]{:S(2)}) copy-start(bf16[4096,128]{1,0:T(8,128)(2,1)S(1)} %collective-permute-done.refs_4_.x1_hbm) | copy-start | bytes 3145732
  26.6 17.0 %copy-start.2 = (bf16[4096,128]{1,0:T(8,128)(2,1)S(1)}, bf16[4096,128]{1,0:T(8,128)(2,1)}, u32[]{:S(2)}) copy-start(bf16[4096,128]{1,0:T(8,128)(2,1)} %x0_hbm.1) | copy-start | bytes 3145732
  26.6 16.0 %collective-permute-start.3 = (bf16[2048,128]{1,0:T(8,128)(2,1)S(1)}, bf16[2048,128]{1,0:T(8,128)(2,1)S(1)}, u32[]{:S(2)}, u32[]{:S(2)}) collective-permute-start(bf16[2048,128]{1,0:T(8,128)(2,1)S(1)} %slice.7), channel_id=1, source_target_pairs={{0,1},{1,2},{2,3},{3,0},{4,5},{5,6},{6,7},{7,4},{8,9},{9,10},{10,1... | collective-permute-start | bytes 1572872 | tf_op jit(solution)/shard_map/ppermute | solution.py:633
  28.2 14.4 %collective-permute-start.2 = (bf16[2048,128]{1,0:T(8,128)(2,1)S(1)}, bf16[2048,128]{1,0:T(8,128)(2,1)S(1)}, u32[]{:S(2)}, u32[]{:S(2)}) collective-permute-start(bf16[2048,128]{1,0:T(8,128)(2,1)S(1)} %slice.6), channel_id=1, source_target_pairs={{1,0},{2,1},{3,2},{0,3},{5,4},{6,5},{7,6},{4,7},{9,8},{10,9},{11,1... | collective-permute-start | bytes 1572872 | tf_op jit(solution)/shard_map/ppermute | solution.py:632
  42.6 0.8 copy-start.6
  42.6 1.0 copy-start.7
  55.8 41.8 %all-to-all-start = ((bf16[32,144,128]{2,1,0:T(8,128)(2,1)}), bf16[32,144,128]{2,1,0:T(8,128)(2,1)}, u32[]{:S(2)}, u32[]{:S(2)}) async-start(bf16[32,144,128]{2,1,0:T(8,128)(2,1)} %mirror_blocks.1), calls=%async_computation | async-start | bytes 2359296 | tf_op jit(solution)/shard_map/all_to_all | solution.py:639
  87.0 8.2 %collective-permute-start.4 = (bf16[16,144,128]{2,1,0:T(8,128)(2,1)S(1)}, bf16[16,144,128]{2,1,0:T(8,128)(2,1)S(1)}, u32[]{:S(2)}, u32[]{:S(2)}) collective-permute-start(bf16[16,144,128]{2,1,0:T(8,128)(2,1)S(1)} %get-tuple-element.26), channel_id=1, source_target_pairs={{0,4},{4,0},{8,12},{12,8},{16,20},{20,16},{24,28},{28,24},{32,36},... | collective-permute-start | bytes 1769480 | tf_op jit(solution)/shard_map/ppermute | solution.py:642
  95.2 8.0 %copy-start.4 = (bf16[512,128]{1,0:T(8,128)(2,1)S(1)}, bf16[512,128]{1,0:T(8,128)(2,1)}, u32[]{:S(2)}) copy-start(bf16[512,128]{1,0:T(8,128)(2,1)} %self_ref.1) | copy-start | bytes 393220
  95.2 8.0 %copy-start.5 = (s32[4096]{0:T(1024)S(1)}, s32[4096]{0:T(1024)}, u32[]{:S(2)}) copy-start(s32[4096]{0:T(1024)} %param.18) | copy-start | bytes 49156
  97.5 18.5 %all-to-all-start.1 = ((bf16[16,144,128]{2,1,0:T(8,128)(2,1)}), bf16[16,144,128]{2,1,0:T(8,128)(2,1)S(1)}, u32[]{:S(2)}, u32[]{:S(2)}) async-start(bf16[16,144,128]{2,1,0:T(8,128)(2,1)} %add_convert_fusion), calls=%async_computation.1 | async-start | bytes 1179648 | tf_op jit(solution)/shard_map/all_to_all | solution.py:645
  116.0 7.0 %copy-start.3 = (f32[128]{0:T(128)S(1)}, f32[128]{0:T(128)}, u32[]{:S(2)}) copy-start(f32[128]{0:T(128)} %param.14) | copy-start | bytes 1540
  116.3 5.0 %collective-permute-start.7 = (f32[32,128]{1,0:T(8,128)S(1)}, f32[32,128]{1,0:T(8,128)S(1)}, u32[]{:S(2)}, u32[]{:S(2)}) collective-permute-start(f32[32,128]{1,0:T(8,128)S(1)} %get-tuple-element.32.a_ref), channel_id=1, source_target_pairs={{3,0},{0,1},{1,2},{2,3},{7,4},{4,5},{5,6},{6,7},{11,8},{8,9},{9,10... | collective-permute-start | bytes 49160 | tf_op jit(solution)/shard_map/ppermute | solution.py:595
  116.5 5.2 %collective-permute-start.6 = (f32[32,128]{1,0:T(8,128)S(1)}, f32[32,128]{1,0:T(8,128)S(1)}, u32[]{:S(2)}, u32[]{:S(2)}) collective-permute-start(f32[32,128]{1,0:T(8,128)S(1)} %get-tuple-element.32.a_ref), channel_id=1, source_target_pairs={{2,0},{3,1},{0,2},{1,3},{6,4},{7,5},{4,6},{5,7},{10,8},{11,9},{8,1... | collective-permute-start | bytes 49160 | tf_op jit(solution)/shard_map/ppermute | solution.py:595
  119.3 3.7 %collective-permute-start.5 = (f32[32,128]{1,0:T(8,128)S(1)}, f32[32,128]{1,0:T(8,128)S(1)}, u32[]{:S(2)}, u32[]{:S(2)}) collective-permute-start(f32[32,128]{1,0:T(8,128)S(1)} %get-tuple-element.32.a_ref), channel_id=1, source_target_pairs={{1,0},{2,1},{3,2},{0,3},{5,4},{6,5},{7,6},{4,7},{9,8},{10,9},{11,1... | collective-permute-start | bytes 49160 | tf_op jit(solution)/shard_map/ppermute | solution.py:595

commit v9 on v8

--- a/solution.py
+++ b/solution.py
@@ -566,8 +566,8 @@
     )(hub, in_vmem(mixed), in_vmem(squares))
 
 
-def scale_kernel(mixed_ref, hub_ref, a_ref, b_ref, c_ref, d_ref, gain_ref, out_ref, *, model_dim):
-    lines = a_ref[...] + b_ref[...] + c_ref[...] + d_ref[...]
+def scale_kernel(mixed_ref, hub_ref, a_ref, b_ref, gain_ref, out_ref, *, model_dim):
+    lines = a_ref[...] + b_ref[...]
     norm = lax.rsqrt(lines / model_dim + 1e-05)
     gain = gain_ref[...]
     tiles, width = norm.shape
@@ -583,18 +583,11 @@
     return pl.pallas_call(
         functools.partial(scale_kernel, model_dim=model_dim),
         out_shape=jax.ShapeDtypeStruct(mixed.shape, BF),
-        in_specs=[vmem] * 7,
+        in_specs=[vmem] * 5,
         out_specs=vmem,
         compiler_params=pltpu.CompilerParams(vmem_limit_bytes=VMEM_LIMIT),
         name="scale",
     )(in_vmem(mixed), in_vmem(hub_mixed), *[in_vmem(x) for x in lines], gain)
-
-
-def from_others(x, size):
-    return [
-        lax.ppermute(x, "feat", [((i + shift) % size, i) for i in range(size)])
-        for shift in range(1, size)
-    ]
 
 
 def on_device(
@@ -655,7 +648,8 @@
         feat.reshape(1), mirror, mirror_master_rows.reshape(owners, TILE), self_weight, pieces
     )
     hub_mixed, line = hub_final(hub, mixed, squares)
-    lines = [line] + from_others(line, feat_size)
+    pair = line + lax.ppermute(line, "feat", [(i, i ^ 1) for i in range(feat_size)])
+    lines = [pair, lax.ppermute(pair, "feat", [(i, feat_size - 1 - i) for i in range(feat_size)])]
     return scale(mixed, hub_mixed, lines, out_gain.reshape(1, cols), model_dim)
 
 

time: 126 us -> 128 us (1.016); the launches traced: 125 us -> 128 us
  starting transfers between devices: 46.2 us -> 24.5 us
  Pallas kernels: 69.7 us -> 88.7 us
  waiting for transfers between devices: 5.86 us -> 12.1 us
    pallas_call x2, Pallas kernels: 20 us -> 38.9 us  [blocks_call(): pl.pallas_call(functools.partial(blocks_kernel, group=group, owners=owner...]
    all_to_all x1, starting transfers between devices: 23.4 us -> 9.9 us  [on_device(): lax.all_to_all(mirror_part, 'dom', split_axis=0, concat_axis=0, tiled=True)]
    ppermute x1, starting transfers between devices: 6.55 us -> 0.09 us  [on_device(): came = lax.ppermute(sent, 'dom', [(i, i ^ 1) for i in range(owners)])]
    ppermute x3 -> x2, waiting for transfers between devices: 2.6 us -> 6.59 us  [the longest x1 3.37 us: on_device(): lax.ppermute(line, 'feat', [(i, i ^ 1) for i in range(feat_size)])]
    ppermute x3 -> x2, starting transfers between devices: 4.1 us -> 2.14 us  [the longest x1 1.72 us: on_device(): lax.ppermute(pair, 'feat', [(i, feat_size - 1 - i) for i in range(feat_si...]
    all_to_all x1, waiting for transfers between devices: 1.36 us -> 3.31 us  [on_device(): lax.all_to_all(mirror_part, 'dom', split_axis=0, concat_axis=0, tiled=True)]
  transfers between devices with their start and end apart: 10 -> 9, of which waited for: 6 -> 5; matrix products, arithmetic and copies ran while one was open for 1% -> 1% of each run, Pallas kernels for 45% -> 47%
where the time goes in v9:
time: 128 us
  Pallas kernels  88.7 us (69%)
  starting transfers between devices  24.5 us (19%)
  waiting for transfers between devices  12.1 us (9%)
    pallas_call x2, Pallas kernels, blocks_call(): pl.pallas_call(functools.partial(blocks_kernel, group=group, owners=owner...  38.9 us
    pallas_call x2, Pallas kernels, mix(): pl.pallas_call(functools.partial(mix_kernel, chunk=512), out_shape=jax.Sh...  32.3 us
    pallas_call x1, Pallas kernels, mirror_final(): pl.pallas_call(functools.partial(mirror_kernel, chunk=chunk, reach=n_loca...  12.8 us
    all_to_all x1, starting transfers between devices, on_device(): lax.all_to_all(mirror_part, 'dom', split_axis=0, concat_axis=0, tiled=True)  9.9 us
    all_to_all x1, starting transfers between devices, on_device(): lax.all_to_all(hub_part, 'dom', split_axis=0, concat_axis=0, tiled=True,...  5.83 us
    ppermute x1, waiting for transfers between devices, on_device(): lax.ppermute(line, 'feat', [(i, i ^ 1) for i in range(feat_size)])  3.37 us
    all_to_all x1, waiting for transfers between devices, on_device(): lax.all_to_all(mirror_part, 'dom', split_axis=0, concat_axis=0, tiled=True)  3.31 us
    ppermute x1, waiting for transfers between devices, on_device(): lax.ppermute(pair, 'feat', [(i, feat_size - 1 - i) for i in range(feat_si...  3.23 us
  transfers between devices with their start and end apart: 9, of which 5 were waited for; matrix products, arithmetic and copies ran while one was open for 1% of the time, Pallas kernels for 47%

profile of v9, /device:TPU:0, one launch (start us, length us, event | category | flops | bytes accessed | tf_op | source)
XLA Modules:
  0.0 128.2 jit_solution(7417090559072225470)
XLA Ops:
  0.0 1.7 %collective-permute-start.1 = (bf16[4096,128]{1,0:T(8,128)(2,1)}, bf16[4096,128]{1,0:T(8,128)(2,1)S(1)}, u32[]{:S(2)}, u32[]{:S(2)}) collective-permute-start(bf16[4096,128]{1,0:T(8,128)(2,1)} %x0_hbm.1), channel_id=1, source_target_pairs={{0,1},{1,2},{2,3},{3,0},{4,5},{5,6},{6,7},{7,4},{8,9},{9,10},{10,1... | collective-permute-start | bytes 3145736 | tf_op jit(solution)/shard_map/ppermute | solution.py:615
  1.7 1.6 %collective-permute-start = (bf16[4096,128]{1,0:T(8,128)(2,1)}, bf16[4096,128]{1,0:T(8,128)(2,1)S(1)}, u32[]{:S(2)}, u32[]{:S(2)}) collective-permute-start(bf16[4096,128]{1,0:T(8,128)(2,1)} %x0_hbm.1), channel_id=1, source_target_pairs={{1,0},{2,1},{3,2},{0,3},{5,4},{6,5},{7,6},{4,7},{9,8},{10,9},{11,1... | collective-permute-start | bytes 3145736 | tf_op jit(solution)/shard_map/ppermute | solution.py:614
  3.9 2.8 %prepare.1 = (s32[1,768]{1,0:T(1,128)S(1)}, bf16[2048,256]{1,0:T(8,128)(2,1)S(1)}) custom-call(s32[1]{0:T(128)S(6)} %copy.13.live_ref, s32[512,128]{1,0:T(8,128)} %refs_1_.3, s32[512,128]{1,0:T(8,128)} %refs_2_.3, s32[1,512]{1,0:T(1,128)} %bitcast.8, bf16[64,822]{1,0:T(8,128)(2,1)} %bitcast.7), custom_call_target="tpu_custom_call" | custom-call | tf_op jit(solution)/shard_map/prepare/pallas_call | solution.py:123
  6.7 19.6 %mix.1.rest_0_ = bf16[256,2,512,128]{3,2,1,0:T(8,128)(2,1)} custom-call(s32[1]{0:T(128)} %bitcast.feat_ref, bf16[2048,256]{1,0:T(8,128)(2,1)S(1)} %get-tuple-element.20.lhs_ref, bf16[64,512,128]{2,1,0:T(8,128)(2,1)} %bases_ref.3), custom_call_target="tpu_custom_call" | custom-call | flops 10737418240 | bytes 41943040 | tf_op jit(solution)/shard_map/mix/pallas_call | solution.py:191
  26.2 0.2 collective-permute-done.1.refs_5_.x3_hbm
  26.5 0.0 copy-start
  26.5 0.0 collective-permute-done.refs_4_.x1_hbm
  26.5 0.0 copy-start.1
  26.6 0.0 copy-start.2
  26.6 1.6 %collective-permute-start.3 = (bf16[2048,128]{1,0:T(8,128)(2,1)S(1)}, bf16[2048,128]{1,0:T(8,128)(2,1)S(1)}, u32[]{:S(2)}, u32[]{:S(2)}) collective-permute-start(bf16[2048,128]{1,0:T(8,128)(2,1)S(1)} %slice.7), channel_id=1, source_target_pairs={{0,1},{1,2},{2,3},{3,0},{4,5},{5,6},{6,7},{7,4},{8,9},{9,10},{10,1... | collective-permute-start | bytes 1572872 | tf_op jit(solution)/shard_map/ppermute | solution.py:626
  28.2 1.7 %collective-permute-start.2 = (bf16[2048,128]{1,0:T(8,128)(2,1)S(1)}, bf16[2048,128]{1,0:T(8,128)(2,1)S(1)}, u32[]{:S(2)}, u32[]{:S(2)}) collective-permute-start(bf16[2048,128]{1,0:T(8,128)(2,1)S(1)} %slice.6), channel_id=1, source_target_pairs={{1,0},{2,1},{3,2},{0,3},{5,4},{6,5},{7,6},{4,7},{9,8},{10,9},{11,1... | collective-permute-start | bytes 1572872 | tf_op jit(solution)/shard_map/ppermute | solution.py:625
  29.9 12.7 %mix_rest.1.refs_8_ = bf16[256,2,512,128]{3,2,1,0:T(8,128)(2,1)} custom-call(s32[1]{0:T(128)} %bitcast.feat_ref, bf16[2048,256]{1,0:T(8,128)(2,1)S(1)} %get-tuple-element.20.lhs_ref, bf16[64,512,128]{2,1,0:T(8,128)(2,1)} %bases_ref.3, bf16[256,2,512,128]{3,2,1,0:T(8,128)(2,1)} %mix.1.rest_0_), custom_call_target="tpu_custom_call", output_to_operand_aliasing={{}: (3, {})} | custom-call | flops 6442450944 | bytes 25165824 | tf_op jit(solution)/shard_map/mix_rest/pallas_call | solution.py:191
  42.6 0.0 collective-permute-done.3.refs_7_.second_hbm
  42.6 0.0 copy-start.6
  42.6 0.0 collective-permute-done.2.refs_6_.first_hbm
  42.6 0.0 copy-start.7
  42.6 0.8 copy-done.6
  43.4 0.2 copy-done.7
  43.6 0.0 copy-done.2
  43.6 27.0 %mirror_blocks.1 = bf16[32,144,128]{2,1,0:T(8,128)(2,1)} custom-call(s32[1,768]{1,0:T(1,128)S(1)} %get-tuple-element.19.refs_0_, s32[512,128]{1,0:T(8,128)} %refs_1_.3, s32[512,128]{1,0:T(8,128)} %refs_2_.3, bf16[4096,128]{1,0:T(8,128)(2,1)S(1)} %copy-done.2, bf16[4096,128]{1,0:T(8,128)(2,1)S(1)} %collective-permute-done.refs_4_.x1_hbm, ...), custom_call_target="tpu_custom_call" | custom-call | flops 8589934592 | bytes 33554432 | tf_op jit(solution)/shard_map/mirror_blocks/pallas_call | solution.py:379
  70.5 9.9 %all-to-all-start = ((bf16[32,144,128]{2,1,0:T(8,128)(2,1)}), bf16[32,144,128]{2,1,0:T(8,128)(2,1)}, u32[]{:S(2)}, u32[]{:S(2)}) async-start(bf16[32,144,128]{2,1,0:T(8,128)(2,1)} %mirror_blocks.1), calls=%async_computation | async-start | bytes 2359296 | tf_op jit(solution)/shard_map/all_to_all | solution.py:632
  80.4 0.0 copy-done
  80.5 0.0 copy-done.1
  80.5 12.0 %hub_blocks.1 = (bf16[16,144,128]{2,1,0:T(8,128)(2,1)S(1)}, bf16[16,144,128]{2,1,0:T(8,128)(2,1)S(1)}) custom-call(s32[1,768]{1,0:T(1,128)S(1)} %get-tuple-element.19.refs_0_, s32[512,128]{1,0:T(8,128)} %refs_1_.3, s32[512,128]{1,0:T(8,128)} %refs_2_.3, bf16[4096,128]{1,0:T(8,128)(2,1)S(1)} %copy-done.2, ...), custom_call_target="tpu_custom_call" | custom-call | flops 8589934592 | bytes 33554432 | tf_op jit(solution)/shard_map/hub_blocks/pallas_call | solution.py:379
  92.4 0.1 collective-permute-start.4
  92.5 2.0 %collective-permute-done.4 = bf16[16,144,128]{2,1,0:T(8,128)(2,1)S(1)} collective-permute-done((bf16[16,144,128]{2,1,0:T(8,128)(2,1)S(1)}, bf16[16,144,128]{2,1,0:T(8,128)(2,1)S(1)}, u32[]{:S(2)}, u32[]{:S(2)}) %collective-permute-start.4) | collective-permute-done | bytes 589856 | tf_op jit(solution)/shard_map/ppermute | solution.py:635
  94.5 0.0 copy-start.4
  94.5 0.0 copy-start.5
  94.5 1.0 add_convert_fusion
  95.5 3.3 %all-to-all-done.mirror_hbm = bf16[32,144,128]{2,1,0:T(8,128)(2,1)} async-done(((bf16[32,144,128]{2,1,0:T(8,128)(2,1)}), bf16[32,144,128]{2,1,0:T(8,128)(2,1)}, u32[]{:S(2)}, u32[]{:S(2)}) %all-to-all-start) | async-done | bytes 1179680 | tf_op jit(solution)/shard_map/all_to_all | solution.py:632
  98.8 5.8 %all-to-all-start.1 = ((bf16[16,144,128]{2,1,0:T(8,128)(2,1)}), bf16[16,144,128]{2,1,0:T(8,128)(2,1)S(1)}, u32[]{:S(2)}, u32[]{:S(2)}) async-start(bf16[16,144,128]{2,1,0:T(8,128)(2,1)} %add_convert_fusion), calls=%async_computation.1 | async-start | bytes 1179648 | tf_op jit(solution)/shard_map/all_to_all | solution.py:638
  104.6 0.0 copy-done.4
  104.7 0.0 copy-done.5
  104.7 12.8 %mirror_final.1 = (f32[4096,128]{1,0:T(8,128)S(1)}, f32[32,128]{1,0:T(8,128)S(1)}) custom-call(s32[1]{0:T(128)} %bitcast.feat_ref, bf16[32,144,128]{2,1,0:T(8,128)(2,1)} %all-to-all-done.mirror_hbm, s32[32,128]{1,0:T(8,128)S(1)} %bitcast.6, bf16[512,128]{1,0:T(8,128)(2,1)S(1)} %copy-done.4, bf16[4096,128]{1,0:T(8,128)(2,1)} %x0_hbm.1, ...), custom_call_target="tpu_custom_call" | custom-call | flops 8589934592 | bytes 8388608 | tf_op jit(solution)/shard_map/mirror_final/pallas_call | solution.py:512
  117.5 0.0 all-to-all-done.1.hub_ref
  117.5 0.0 copy-start.3
  117.5 0.3 hub_final.1
  117.8 0.4 collective-permute-start.5
  118.2 3.4 %collective-permute-done.5 = f32[32,128]{1,0:T(8,128)S(1)} collective-permute-done((f32[32,128]{1,0:T(8,128)S(1)}, f32[32,128]{1,0:T(8,128)S(1)}, u32[]{:S(2)}, u32[]{:S(2)}) %collective-permute-start.5) | collective-permute-done | bytes 16416 | tf_op jit(solution)/shard_map/ppermute | solution.py:651
  121.6 1.7 %collective-permute-start.6 = (f32[32,128]{1,0:T(8,128)S(1)}, f32[32,128]{1,0:T(8,128)S(1)}, u32[]{:S(2)}, u32[]{:S(2)}) collective-permute-start(f32[32,128]{1,0:T(8,128)S(1)} %add.7.a_ref), channel_id=1, source_target_pairs={{0,3},{1,2},{2,1},{3,0},{4,7},{5,6},{6,5},{7,4},{8,11},{9,10},{10,... | collective-permute-start | bytes 49160 | tf_op jit(solution)/shard_map/ppermute | solution.py:652
  123.3 3.2 %collective-permute-done.6.b_ref = f32[32,128]{1,0:T(8,128)S(1)} collective-permute-done((f32[32,128]{1,0:T(8,128)S(1)}, f32[32,128]{1,0:T(8,128)S(1)}, u32[]{:S(2)}, u32[]{:S(2)}) %collective-permute-start.6) | collective-permute-done | bytes 16416 | tf_op jit(solution)/shard_map/ppermute | solution.py:652
  126.6 0.0 copy-done.3
  126.6 1.6 %scale.1 = bf16[4096,128]{1,0:T(8,128)(2,1)} custom-call(f32[4096,128]{1,0:T(8,128)S(1)} %get-tuple-element.28.mixed_ref, f32[128,128]{1,0:T(8,128)S(1)} %get-tuple-element.31.hub_ref, f32[32,128]{1,0:T(8,128)S(1)} %add.7.a_ref, f32[32,128]{1,0:T(8,128)S(1)} %collective-permute-done.6.b_ref, f32[1,128]{1,0:T(1,128)S(1)} %bitcast.5), custom_call_target="tpu_custom_call" | custom-call | tf_op jit(solution)/shard_map/scale/pallas_call | solution.py:583
  (3 shorter events, 0.1 us)
Async XLA Ops:
  0.0 26.5 %collective-permute-start.1 = (bf16[4096,128]{1,0:T(8,128)(2,1)}, bf16[4096,128]{1,0:T(8,128)(2,1)S(1)}, u32[]{:S(2)}, u32[]{:S(2)}) collective-permute-start(bf16[4096,128]{1,0:T(8,128)(2,1)} %x0_hbm.1), channel_id=1, source_target_pairs={{0,1},{1,2},{2,3},{3,0},{4,5},{5,6},{6,7},{7,4},{8,9},{9,10},{10,1... | collective-permute-start | bytes 3145736 | tf_op jit(solution)/shard_map/ppermute | solution.py:615
  1.7 24.8 %collective-permute-start = (bf16[4096,128]{1,0:T(8,128)(2,1)}, bf16[4096,128]{1,0:T(8,128)(2,1)S(1)}, u32[]{:S(2)}, u32[]{:S(2)}) collective-permute-start(bf16[4096,128]{1,0:T(8,128)(2,1)} %x0_hbm.1), channel_id=1, source_target_pairs={{1,0},{2,1},{3,2},{0,3},{5,4},{6,5},{7,6},{4,7},{9,8},{10,9},{11,1... | collective-permute-start | bytes 3145736 | tf_op jit(solution)/shard_map/ppermute | solution.py:614
  26.5 54.0 %copy-start = (bf16[4096,128]{1,0:T(8,128)(2,1)}, bf16[4096,128]{1,0:T(8,128)(2,1)S(1)}, u32[]{:S(2)}) copy-start(bf16[4096,128]{1,0:T(8,128)(2,1)S(1)} %collective-permute-done.1.refs_5_.x3_hbm) | copy-start | bytes 3145732
  26.5 54.0 %copy-start.1 = (bf16[4096,128]{1,0:T(8,128)(2,1)}, bf16[4096,128]{1,0:T(8,128)(2,1)S(1)}, u32[]{:S(2)}) copy-start(bf16[4096,128]{1,0:T(8,128)(2,1)S(1)} %collective-permute-done.refs_4_.x1_hbm) | copy-start | bytes 3145732
  26.6 17.0 %copy-start.2 = (bf16[4096,128]{1,0:T(8,128)(2,1)S(1)}, bf16[4096,128]{1,0:T(8,128)(2,1)}, u32[]{:S(2)}) copy-start(bf16[4096,128]{1,0:T(8,128)(2,1)} %x0_hbm.1) | copy-start | bytes 3145732
  26.6 16.0 %collective-permute-start.3 = (bf16[2048,128]{1,0:T(8,128)(2,1)S(1)}, bf16[2048,128]{1,0:T(8,128)(2,1)S(1)}, u32[]{:S(2)}, u32[]{:S(2)}) collective-permute-start(bf16[2048,128]{1,0:T(8,128)(2,1)S(1)} %slice.7), channel_id=1, source_target_pairs={{0,1},{1,2},{2,3},{3,0},{4,5},{5,6},{6,7},{7,4},{8,9},{9,10},{10,1... | collective-permute-start | bytes 1572872 | tf_op jit(solution)/shard_map/ppermute | solution.py:626
  28.2 14.3 %collective-permute-start.2 = (bf16[2048,128]{1,0:T(8,128)(2,1)S(1)}, bf16[2048,128]{1,0:T(8,128)(2,1)S(1)}, u32[]{:S(2)}, u32[]{:S(2)}) collective-permute-start(bf16[2048,128]{1,0:T(8,128)(2,1)S(1)} %slice.6), channel_id=1, source_target_pairs={{1,0},{2,1},{3,2},{0,3},{5,4},{6,5},{7,6},{4,7},{9,8},{10,9},{11,1... | collective-permute-start | bytes 1572872 | tf_op jit(solution)/shard_map/ppermute | solution.py:625
  42.6 0.8 copy-start.6
  42.6 1.0 copy-start.7
  70.5 28.3 %all-to-all-start = ((bf16[32,144,128]{2,1,0:T(8,128)(2,1)}), bf16[32,144,128]{2,1,0:T(8,128)(2,1)}, u32[]{:S(2)}, u32[]{:S(2)}) async-start(bf16[32,144,128]{2,1,0:T(8,128)(2,1)} %mirror_blocks.1), calls=%async_computation | async-start | bytes 2359296 | tf_op jit(solution)/shard_map/all_to_all | solution.py:632
  92.4 2.1 %collective-permute-start.4 = (bf16[16,144,128]{2,1,0:T(8,128)(2,1)S(1)}, bf16[16,144,128]{2,1,0:T(8,128)(2,1)S(1)}, u32[]{:S(2)}, u32[]{:S(2)}) collective-permute-start(bf16[16,144,128]{2,1,0:T(8,128)(2,1)S(1)} %get-tuple-element.26), channel_id=1, source_target_pairs={{0,4},{4,0},{8,12},{12,8},{16,20},{20,16},{24,28},{28,24},{32,36},... | collective-permute-start | bytes 1769480 | tf_op jit(solution)/shard_map/ppermute | solution.py:635
  94.5 10.1 %copy-start.4 = (bf16[512,128]{1,0:T(8,128)(2,1)S(1)}, bf16[512,128]{1,0:T(8,128)(2,1)}, u32[]{:S(2)}) copy-start(bf16[512,128]{1,0:T(8,128)(2,1)} %self_ref.1) | copy-start | bytes 393220
  94.5 10.1 %copy-start.5 = (s32[4096]{0:T(1024)S(1)}, s32[4096]{0:T(1024)}, u32[]{:S(2)}) copy-start(s32[4096]{0:T(1024)} %param.18) | copy-start | bytes 49156
  98.8 18.7 %all-to-all-start.1 = ((bf16[16,144,128]{2,1,0:T(8,128)(2,1)}), bf16[16,144,128]{2,1,0:T(8,128)(2,1)S(1)}, u32[]{:S(2)}, u32[]{:S(2)}) async-start(bf16[16,144,128]{2,1,0:T(8,128)(2,1)} %add_convert_fusion), calls=%async_computation.1 | async-start | bytes 1179648 | tf_op jit(solution)/shard_map/all_to_all | solution.py:638
  117.5 9.1 %copy-start.3 = (f32[128]{0:T(128)S(1)}, f32[128]{0:T(128)}, u32[]{:S(2)}) copy-start(f32[128]{0:T(128)} %param.14) | copy-start | bytes 1540
  117.8 3.8 %collective-permute-start.5 = (f32[32,128]{1,0:T(8,128)S(1)}, f32[32,128]{1,0:T(8,128)S(1)}, u32[]{:S(2)}, u32[]{:S(2)}) collective-permute-start(f32[32,128]{1,0:T(8,128)S(1)} %get-tuple-element.32), channel_id=1, source_target_pairs={{0,1},{1,0},{2,3},{3,2},{4,5},{5,4},{6,7},{7,6},{8,9},{9,8},{10,11... | collective-permute-start | bytes 49160 | tf_op jit(solution)/shard_map/ppermute | solution.py:651
  121.6 4.9 %collective-permute-start.6 = (f32[32,128]{1,0:T(8,128)S(1)}, f32[32,128]{1,0:T(8,128)S(1)}, u32[]{:S(2)}, u32[]{:S(2)}) collective-permute-start(f32[32,128]{1,0:T(8,128)S(1)} %add.7.a_ref), channel_id=1, source_target_pairs={{0,3},{1,2},{2,1},{3,0},{4,7},{5,6},{6,5},{7,4},{8,11},{9,10},{10,... | collective-permute-start | bytes 49160 | tf_op jit(solution)/shard_map/ppermute | solution.py:652
